TPU v7x, 32 devices: a whole 2x2x4 slice. The times are simulated.
32 devices in a mesh: group: 2 (over y), rep: 8 (over z, x), tp: 2 (over core).
Axes of the slice: x: 2, y: 2, z: 4, core: 2. Of those that a mesh axis runs over, the one named last changes fastest.
Arguments:
- queries: bfloat16 [2048, 4096], P(('group', 'rep'), 'tp'), parts along dimension 0, may hold values from -6 to 6
- current_key_value: bfloat16 [2048, 1024], P(('group', 'rep'), 'tp'), parts along dimension 0, may hold values from -6 to 6
- key_value_pool: bfloat16 [1536, 16, 1024], P(('group', 'rep'), None, 'tp'), parts along dimension 0, may hold values from -6 to 6
- request_page_entries: int32 [2048, 4], P(('group', 'rep')), parts along dimension 0, may hold values from 0 to 111, as said below
- context_length: int32 [2048], P(('group', 'rep')), parts along dimension 0, may hold values from 1 to 64, as said below
- migration_page: int32 [96], P(('group', 'rep')), parts along dimension 0, may hold values from 0 to 95, as said below
- migration_target: int32 [96], P(('group', 'rep')), parts along dimension 0, may hold values from 0 to 7, as said below
- adapter_replica: int32 [2048, 1], P(('group', 'rep')), parts along dimension 0, may hold values from 0 to 7; in each aligned block of 128 rows (0 to 127, 128 to 255, ...) at most 32 rows name the same one
- adapter_position: int32 [2048], P(('group', 'rep')), parts along dimension 0, may hold values from 0 to 1
- adapter_down_weight: bfloat16 [16, 4096, 64], P('rep', 'tp'), may hold values from -0.09375 to 0.09375
- adapter_up_weight: bfloat16 [16, 64, 8192], P('rep', None, 'tp'), may hold values from -0.75 to 0.75
Outputs:
- adapter_delta: bfloat16 [2048, 8192], P(('group', 'rep'), 'tp'), parts along dimension 0
There are 2 independent parts, one for each index of `group`. A program takes and returns all parts, laid end to end along the dimension named above; an argument that names none is the same for every part. Nothing has to cross between parts.
Inputs may be any that keep to these rules, and one draw needn't show every extreme that they name: `adapter_replica`: within the 128 rows of one replica no value appears more than 32 times. `migration_target`: A replica's list never names the replica itself and names one destination at most 2 times; every list names some destination exactly 2 times. `migration_page`: the 6 entries of one replica's list are distinct pages of its own pool. `request_page_entries`: an entry of 96 or more names an incoming page that exists for the request's replica. Entries past a request's first ceil(context_length / 16) are 0. `context_length`: every replica holds a request of 64 tokens.
All inputs are finite; a program needn't handle non-finite values.
Results may differ from a plain program's by a relative error of at most 0.009.
Values may be sent and summed in bfloat16 or wider, within the bound.
No kernel may reach another device: no remote copies, remote signals or barrier semaphores. Data moves between devices by JAX's collectives and lax.ppermute only.
A program may use at most 64 MiB of HBM per device.

v0:
```python
import math

import jax
import jax.numpy as jnp
from jax import lax
from jax.sharding import PartitionSpec as P

HEAD_SIZE = 128
QUERY_GROUP = 8
MCAP = 2


def slot_order(targets, groups, slot_depth):
    item_count = targets.shape[0]
    position = jnp.arange(item_count, dtype=jnp.int32)
    same_target = (targets[:, None] == targets[None, :]) & (position[None, :] < position[:, None])
    before_count = jnp.sum(same_target.astype(jnp.int32), axis=1)
    slot_index = targets * slot_depth + before_count
    return jnp.arange(groups * slot_depth, dtype=jnp.int32)[:, None] == slot_index[None, :]


def local(
    queries,
    current_key_value,
    key_value_pool,
    request_page_entries,
    context_length,
    migration_page,
    migration_target,
    adapter_replica,
    adapter_position,
    adapter_down_weight,
    adapter_up_weight,
):
    replicas = lax.axis_size("rep")
    kv_local = current_key_value.shape[1] // (2 * HEAD_SIZE)
    row_count = queries.shape[0]
    page_len = key_value_pool.shape[1]
    token_count = request_page_entries.shape[1] * page_len
    slot_select = slot_order(migration_target, replicas, MCAP)
    chosen = jnp.sum(jnp.where(slot_select, migration_page[None, :], 0), axis=1)
    filled = jnp.any(slot_select, axis=1)
    outgoing = jnp.where(
        filled[:, None, None], key_value_pool[chosen], jnp.zeros((), key_value_pool.dtype)
    )
    query_heads = queries.reshape(row_count, kv_local, QUERY_GROUP, HEAD_SIZE)
    score_scale = 1.0 / math.sqrt(HEAD_SIZE)
    arrived = lax.all_to_all(outgoing, "rep", split_axis=0, concat_axis=0, tiled=True)
    page_cache = jnp.concatenate([key_value_pool, arrived], axis=0)
    cache_rows = page_cache[request_page_entries].reshape(
        row_count, token_count, kv_local, 2, HEAD_SIZE
    )
    scores = (
        jnp.einsum(
            "rgjk,rtgk->rgjt",
            query_heads,
            cache_rows[:, :, :, 0, :],
            preferred_element_type=jnp.float32,
        )
        * score_scale
    )
    fresh = current_key_value.reshape(row_count, kv_local, 2, HEAD_SIZE)
    visible = jnp.arange(token_count, dtype=jnp.int32)[None, :] < context_length[:, None]
    scores = jnp.where(visible[:, None, None, :], scores, -1e30)
    own_score = (
        jnp.einsum(
            "rgjk,rgk->rgj", query_heads, fresh[:, :, 0, :], preferred_element_type=jnp.float32
        )
        * score_scale
    )
    row_max = jnp.maximum(jnp.max(scores, axis=3), own_score)
    weights = jnp.exp(scores - row_max[:, :, :, None])
    own_weight = jnp.exp(own_score - row_max)
    normaliser = jnp.sum(weights, axis=3) + own_weight
    probabilities = (weights / normaliser[:, :, :, None]).astype(jnp.bfloat16)
    own_prob = (own_weight / normaliser).astype(jnp.bfloat16)
    attended = jnp.einsum(
        "rgjt,rtgk->rgjk",
        probabilities,
        cache_rows[:, :, :, 1, :],
        preferred_element_type=jnp.float32,
    )
    attended = attended + own_prob.astype(jnp.float32)[:, :, :, None] * fresh[
        :, :, None, 1, :
    ].astype(jnp.float32)
    heads_out = attended.reshape(row_count, kv_local * QUERY_GROUP * HEAD_SIZE).astype(jnp.bfloat16)
    adapter_number = adapter_down_weight.shape[0]
    slot_cap = max(2, (2 * row_count + replicas - 1) // replicas)
    routing = slot_order(adapter_replica[:, 0], replicas, slot_cap)
    route_mask = routing.astype(jnp.bfloat16)
    outbound = jnp.dot(route_mask, heads_out, preferred_element_type=jnp.float32).astype(
        jnp.bfloat16
    )
    outbound = outbound.reshape(replicas, slot_cap, -1)
    adapter_labels = (
        jnp.sum(jnp.where(routing, adapter_position[None, :], 0), axis=1)
        .astype(jnp.bfloat16)
        .reshape(replicas, slot_cap)
    )
    activations = lax.all_to_all(outbound, "rep", split_axis=0, concat_axis=0, tiled=True)
    adapter_index = lax.all_to_all(adapter_labels, "rep", split_axis=0, concat_axis=0, tiled=True)
    shape_in = activations.shape
    flat_output = activations.reshape(-1, shape_in[2])
    selector = (
        adapter_index.reshape(-1, 1).astype(jnp.int32)
        == jnp.arange(adapter_number, dtype=jnp.int32)[None, :]
    )
    reduced_rank_total = jnp.einsum(
        "oh,pht->opt", flat_output, adapter_down_weight, preferred_element_type=jnp.float32
    )
    partial_low = jnp.sum(jnp.where(selector[:, :, None], reduced_rank_total, 0.0), axis=1)
    low_rank = lax.psum(partial_low, "tp").astype(jnp.bfloat16)
    broadcast_result = jnp.where(
        selector[:, :, None], low_rank[:, None, :], jnp.zeros((), jnp.bfloat16)
    )
    broadcast_result = broadcast_result.reshape(flat_output.shape[0], -1)
    lifted = jnp.dot(
        broadcast_result,
        adapter_up_weight.reshape(-1, adapter_up_weight.shape[2]),
        preferred_element_type=jnp.float32,
    )
    lifted = lifted.astype(jnp.bfloat16).reshape(shape_in[0], shape_in[1], -1)
    returned = lax.all_to_all(lifted, "rep", split_axis=0, concat_axis=0, tiled=True)
    delta = jnp.einsum(
        "sr,sd->rd",
        route_mask,
        returned.reshape(replicas * slot_cap, -1),
        preferred_element_type=jnp.float32,
    )
    return delta.astype(jnp.bfloat16)


def solution(mesh):
    return jax.shard_map(
        local,
        mesh=mesh,
        in_specs=(
            P(("group", "rep"), "tp"),
            P(("group", "rep"), "tp"),
            P(("group", "rep"), None, "tp"),
            P(("group", "rep"), None),
            P(("group", "rep")),
            P(("group", "rep")),
            P(("group", "rep")),
            P(("group", "rep"), None),
            P(("group", "rep")),
            P("rep", "tp", None),
            P("rep", None, "tp"),
        ),
        out_specs=P(("group", "rep"), "tp"),
        check_vma=False,
    )
```

profile of v0, /device:TPU:0, one launch (start us, length us, event | category | flops | bytes accessed | tf_op | source)
XLA Modules:
  0.0 169.5 jit_solution(7984110057268517361)
XLA Ops:
  0.0 0.0 copy-start
  0.0 0.0 copy-start.6
  0.0 0.0 copy-start.5
  0.0 0.0 copy-start.4
  0.0 0.9 convert_reduce_fusion.2
  1.0 0.7 multiply_add_fusion
  1.6 0.1 fusion.25
  1.7 0.7 select_reduce_fusion.2
  2.5 2.0 %gather_fusion = bf16[16,16,512]{2,1,0:T(8,128)(2,1)S(1)} fusion(bf16[96,16,512]{2,1,0:T(8,128)(2,1)} %param.13, s32[1024]{0:T(1024)S(1)} %pad_clamp_fusion.1), kind=kCustom, calls=%fused_computation | custom fusion | bytes 524352 | tf_op jit(solution)/shard_map/gather | solution.py:44
  4.4 0.8 broadcast_select_fusion
  5.2 7.3 %all-to-all-start.1 = ((bf16[16,16,512]{2,1,0:T(8,128)(2,1)}), bf16[16,16,512]{2,1,0:T(8,128)(2,1)S(1)}, u32[]{:S(2)}, u32[]{:S(2)}) async-start(bf16[16,16,512]{2,1,0:T(8,128)(2,1)} %broadcast_select_fusion), calls=%async_computation.1 | async-start | bytes 524288 | tf_op jit(solution)/shard_map/all_to_all | solution.py:48
  12.5 0.7 compare_select_fusion
  13.2 1.1 copy.63
  14.3 0.0 copy-start.2
  14.3 1.2 copy.50
  15.5 0.1 copy.51
  15.6 0.9 convert_reduce_fusion
  16.6 0.4 fusion.13
  17.0 0.0 copy-done.6
  17.0 0.1 copy.48
  17.1 0.1 reshape.139
  17.2 0.1 copy.60
  17.3 0.1 copy.58
  17.4 0.0 copy-done.5
  17.4 0.1 select_reduce_fusion.1
  17.6 0.7 convert_element_type.76
  18.2 0.0 copy-done.4
  18.2 0.1 iota_compare_fusion.3
  18.3 3.1 %all-to-all-done.1 = bf16[16,16,512]{2,1,0:T(8,128)(2,1)S(1)} async-done(((bf16[16,16,512]{2,1,0:T(8,128)(2,1)}), bf16[16,16,512]{2,1,0:T(8,128)(2,1)S(1)}, u32[]{:S(2)}, u32[]{:S(2)}) %all-to-all-start.1) | async-done | bytes 262176 | tf_op jit(solution)/shard_map/all_to_all | solution.py:48
  21.4 0.0 copy-done.2
  21.4 3.6 %all-to-all-start = ((bf16[8,1,32]{2,1,0:T(2,128)(2,1)}), bf16[8,1,32]{2,1,0:T(2,128)(2,1)S(1)}, u32[]{:S(2)}, u32[]{:S(2)}) async-start(bf16[8,1,32]{2,1,0:T(2,128)(2,1)} %convert_element_type.76), calls=%async_computation | async-start | bytes 8192 | tf_op jit(solution)/shard_map/all_to_all | solution.py:101
  25.0 1.6 pad_maximum_fusion
  26.6 13.3 %gather_fusion.1 = bf16[512,16,512]{2,1,0:T(8,128)(2,1)} fusion(bf16[112,16,512]{2,1,0:T(8,128)(2,1)S(1)} %pad_maximum_fusion, s32[1024]{0:T(1024)S(1)} %pad_clamp_fusion), kind=kCustom, calls=%fused_computation.1 | custom fusion | bytes 16779264 | tf_op jit(solution)/shard_map/gather | solution.py:50
  39.9 12.5 %reshape.120 = bf16[128,64,2,2,128]{4,3,2,1,0:T(2,128)(2,1)} reshape(bf16[512,16,512]{2,1,0:T(8,128)(2,1)} %gather_fusion.1) | data formatting | bytes 16777216 | tf_op jit(solution)/shard_map/reshape | solution.py:50
  52.4 0.0 copy-start.3
  52.4 17.7 %fusion.30 = (bf16[128,64,2,1,128]{4,3,2,1,0:T(2,128)(2,1)S(1)}, bf16[128,64,2,1,128]{4,3,2,1,0:T(2,128)(2,1)}) fusion(bf16[128,64,2,2,128]{4,3,2,1,0:T(2,128)(2,1)} %reshape.120), kind=kLoop, calls=%fused_computation.63 | loop fusion | bytes 16777216 | tf_op jit(solution)/shard_map/slice | solution.py:57
  70.1 0.0 copy-done.3
  70.1 2.5 %fusion.32 = (f32[128,2,8]{2,1,0:T(2,128)S(1)}, f32[128,2,8,64]{3,2,1,0:T(8,128)S(1)}) fusion(bf16[128,2,8,128]{3,2,1,0:T(8,128)(2,1)S(1)} %bitcast.82, bf16[128,64,2,1,128]{4,3,2,1,0:T(2,128)(2,1)S(1)} %get-tuple-element.5, pred[128,64]{1,0:T(8,128)(4,1)S(1)} %iota_compare_fusion.3), kind=kOutput, calls=%fused_computation.65 | convolution fusion | flops 33945600 | bytes 5259264 | tf_op jit(solution)/shard_map/rgjk,rtgk->rgjt/dot_general | solution.py:54
  72.6 0.1 copy.52
  72.7 0.2 copy.53
  72.9 0.8 fusion.8
  73.6 0.1 copy.54
  73.7 0.1 copy.55
  73.9 0.1 copy.57
  74.0 0.0 copy-start.1
  74.0 4.7 %fusion.5 = bf16[128,2,8,128]{3,2,1,0:T(8,128)(2,1)S(1)} fusion(bf16[128,64,2,1,128]{4,3,2,1,0:T(2,128)(2,1)} %get-tuple-element.6, f32[128,2,8,64]{3,2,1,0:T(8,128)S(1)} %get-tuple-element.12, f32[128,2,128]{2,1,0:T(2,128)S(1)} %copy.58, f32[128,2,8]{2,1,0:T(2,128)S(1)} %copy.57, f32[128,2,8]{2,1,0:T(2,128)S(1)} %copy.55, f32[128,2,8]{2,1,0:T(2,128)S(1)} %copy.53), kind=kOutput, calls=%fused_computation.13 | convolution fusion | flops 34734080 | bytes 5398528 | tf_op jit(solution)/shard_map/rgjt,rtgk->rgjk/dot_general | solution.py:77
  78.8 1.4 convolution_convert_fusion.1
  80.2 0.0 all-to-all-done
  80.2 6.0 %all-to-all-start.2 = ((bf16[8,32,2048]{2,1,0:T(8,128)(2,1)}), bf16[8,32,2048]{2,1,0:T(8,128)(2,1)S(1)}, u32[]{:S(2)}, u32[]{:S(2)}) async-start(bf16[8,32,2048]{2,1,0:T(8,128)(2,1)} %bitcast.11), calls=%async_computation.2 | async-start | bytes 2097152 | tf_op jit(solution)/shard_map/all_to_all | solution.py:100
  86.3 0.1 reshape.127
  86.3 25.0 %all-to-all-done.2 = bf16[8,32,2048]{2,1,0:T(8,128)(2,1)S(1)} async-done(((bf16[8,32,2048]{2,1,0:T(8,128)(2,1)}), bf16[8,32,2048]{2,1,0:T(8,128)(2,1)S(1)}, u32[]{:S(2)}, u32[]{:S(2)}) %all-to-all-start.2) | async-done | bytes 1048608 | tf_op jit(solution)/shard_map/all_to_all | solution.py:100
  111.3 0.0 copy-done.1
  111.3 0.5 fusion.33
  111.8 3.6 %psum.7 = bf16[256,64]{0,1:T(8,128)(2,1)S(1)} all-reduce(f32[256,64]{0,1:T(8,128)S(1)} %select_reduce_fusion), channel_id=1, replica_groups=mesh['group'=2,'rep'=8,'tp'=2] {'tp'}, use_global_device_ids=true, to_apply=%region_8.9 | all-reduce | flops 16384 | bytes 98304 | tf_op jit(solution)/shard_map/psum | solution.py:112
  115.4 0.0 copy-done
  115.5 0.7 fusion
  116.2 51.9 %all_to_all.21 = bf16[8,32,4096]{2,1,0:T(8,128)(2,1)S(1)} all-to-all(bf16[8,32,4096]{2,1,0:T(8,128)(2,1)S(1)} %bitcast.76), channel_id=1, replica_groups=mesh['group'=2,'rep'=8,'tp'=2] {'rep'}, dimensions={0} | all-to-all | bytes 4194304 | tf_op jit(solution)/shard_map/all_to_all | solution.py:123
  168.1 1.5 convolution_convert_fusion
  (11 shorter events, 0.1 us)
Async XLA Ops:
  0.0 115.4 %copy-start = (bf16[2,64,4096]{2,1,0:T(8,128)(2,1)S(1)}, bf16[2,64,4096]{2,1,0:T(8,128)(2,1)}, u32[]{:S(2)}) copy-start(bf16[2,64,4096]{2,1,0:T(8,128)(2,1)} %param.21) | copy-start | bytes 3145732
  0.0 17.0 %copy-start.6 = (s32[128,1]{0,1:T(1,128)S(1)}, s32[128,1]{0,1:T(1,128)}, u32[]{:S(2)}) copy-start(s32[128,1]{0,1:T(1,128)} %param.18) | copy-start | bytes 1540
  0.0 17.4 %copy-start.5 = (s32[128]{0:T(128)S(1)}, s32[128]{0:T(128)}, u32[]{:S(2)}) copy-start(s32[128]{0:T(128)} %param.19) | copy-start | bytes 1540
  0.0 18.2 %copy-start.4 = (s32[128]{0:T(128)S(1)}, s32[128]{0:T(128)}, u32[]{:S(2)}) copy-start(s32[128]{0:T(128)} %param.15) | copy-start | bytes 1540
  5.2 16.2 %all-to-all-start.1 = ((bf16[16,16,512]{2,1,0:T(8,128)(2,1)}), bf16[16,16,512]{2,1,0:T(8,128)(2,1)S(1)}, u32[]{:S(2)}, u32[]{:S(2)}) async-start(bf16[16,16,512]{2,1,0:T(8,128)(2,1)} %broadcast_select_fusion), calls=%async_computation.1 | async-start | bytes 524288 | tf_op jit(solution)/shard_map/all_to_all | solution.py:48
  14.3 7.1 %copy-start.2 = (bf16[16,8,16,128]{3,2,1,0:T(8,128)(2,1)}, bf16[16,8,16,128]{3,2,1,0:T(8,128)(2,1)S(1)}, u32[]{:S(2)}) copy-start(bf16[16,8,16,128]{3,2,1,0:T(8,128)(2,1)S(1)} %copy.63) | copy-start | bytes 1572868
  21.4 58.8 %all-to-all-start = ((bf16[8,1,32]{2,1,0:T(2,128)(2,1)}), bf16[8,1,32]{2,1,0:T(2,128)(2,1)S(1)}, u32[]{:S(2)}, u32[]{:S(2)}) async-start(bf16[8,1,32]{2,1,0:T(2,128)(2,1)} %convert_element_type.76), calls=%async_computation | async-start | bytes 8192 | tf_op jit(solution)/shard_map/all_to_all | solution.py:101
  52.4 17.7 %copy-start.3 = (bf16[16,8,16,128]{3,2,1,0:T(8,128)(2,1)S(1)}, bf16[16,8,16,128]{3,2,1,0:T(8,128)(2,1)}, u32[]{:S(2)}) copy-start(bf16[16,8,16,128]{3,2,1,0:T(8,128)(2,1)} %copy-done.2) | copy-start | bytes 1572868
  74.0 37.3 %copy-start.1 = (bf16[2,2048,64]{1,2,0:T(8,128)(2,1)S(1)}, bf16[2,2048,64]{1,2,0:T(8,128)(2,1)}, u32[]{:S(2)}) copy-start(bf16[2,2048,64]{1,2,0:T(8,128)(2,1)} %param.20) | copy-start | bytes 1572868
  80.2 31.1 %all-to-all-start.2 = ((bf16[8,32,2048]{2,1,0:T(8,128)(2,1)}), bf16[8,32,2048]{2,1,0:T(8,128)(2,1)S(1)}, u32[]{:S(2)}, u32[]{:S(2)}) async-start(bf16[8,32,2048]{2,1,0:T(8,128)(2,1)} %bitcast.11), calls=%async_computation.2 | async-start | bytes 2097152 | tf_op jit(solution)/shard_map/all_to_all | solution.py:100
where the time goes:
time: 170 us
  blocking collectives  55.5 us (33%)
  local copies, waits for them, and re-layouts  49.7 us (29%)
  waiting for transfers between devices  28 us (16%)
  starting transfers between devices  16.9 us (10%)
  matrix products  11.8 us (7%)
  other arithmetic  7.45 us (4%)
    all_to_all x1, blocking collectives, local(): lax.all_to_all(lifted, 'rep', split_axis=0, concat_axis=0, tiled=True)  51.9 us
    all_to_all x1, waiting for transfers between devices, local(): lax.all_to_all(outbound, 'rep', split_axis=0, concat_axis=0, tiled=True)  25 us
    slice x1, local copies, waits for them, and re-layouts, local(): cache_rows[:, :, :, 0, :]  17.7 us
    gather x1, local copies, waits for them, and re-layouts, local(): page_cache[request_page_entries]  13.3 us
    reshape x1, local copies, waits for them, and re-layouts, local(): page_cache[request_page_entries]  12.5 us
    all_to_all x1, starting transfers between devices, local(): lax.all_to_all(outgoing, 'rep', split_axis=0, concat_axis=0, tiled=True)  7.26 us
    all_to_all x1, starting transfers between devices, local(): lax.all_to_all(outbound, 'rep', split_axis=0, concat_axis=0, tiled=True)  6.03 us
    dot_general x1, matrix products, local(): jnp.einsum('rgjt,rtgk->rgjk', probabilities, cache_rows[:, :, :, 1, :], p...  4.74 us
  transfers between devices with their start and end apart: 3, of which 2 were waited for; matrix products, arithmetic and copies ran while one was open for 36% of the time, Pallas kernels for 0%

commit v1 on v0

v1 whole, which is shorter than its diff:
```python
import functools
import math

import jax
import jax.numpy as jnp
from jax import lax
from jax.experimental import pallas as pl
from jax.experimental.pallas import tpu as pltpu
from jax.sharding import PartitionSpec as P

HEAD_SIZE = 128
QUERY_GROUP = 8
MCAP = 2
LANES = 128
TOKEN_STEP = 256
HIDDEN = -1e30
SCORE_SCALE = math.log2(math.e) / math.sqrt(HEAD_SIZE)
VMEM_LIMIT = 48 * 1024 * 1024


def vmem_spec():
    return pl.BlockSpec(memory_space=pltpu.VMEM)


def smem_spec():
    return pl.BlockSpec(memory_space=pltpu.SMEM)


def params():
    return pltpu.CompilerParams(vmem_limit_bytes=VMEM_LIMIT)


def row_to_column(row):
    count = row.shape[1]
    across = lax.broadcasted_iota(jnp.int32, (count, count), 1)
    down = lax.broadcasted_iota(jnp.int32, (count, count), 0)
    return jnp.sum(jnp.where(across == down, row, 0), axis=1, keepdims=True)


def column_to_row(column):
    count = column.shape[0]
    across = lax.broadcasted_iota(jnp.int32, (count, count), 1)
    down = lax.broadcasted_iota(jnp.int32, (count, count), 0)
    return jnp.sum(jnp.where(across == down, column, 0), axis=0, keepdims=True)


def outgoing_kernel(page_ref, target_ref, pool_ref, out_ref, count_ref, chosen_ref):
    entry_number = page_ref.shape[0]
    slot_number = out_ref.shape[0]

    def clear(slot, carry):
        chosen_ref[slot] = 0
        count_ref[slot // MCAP] = 0
        return carry

    def place(entry, carry):
        target = target_ref[entry]
        rank = count_ref[target]
        chosen_ref[target * MCAP + rank] = page_ref[entry]
        count_ref[target] = rank + 1
        return carry

    def copy(slot, carry):
        out_ref[slot] = pool_ref[chosen_ref[slot]]
        return carry

    lax.fori_loop(0, slot_number, clear, 0)
    lax.fori_loop(0, entry_number, place, 0)
    lax.fori_loop(0, slot_number, copy, 0)


def outgoing_pages(migration_page, migration_target, pool, replicas):
    slots = replicas * MCAP
    return pl.pallas_call(
        outgoing_kernel,
        out_shape=jax.ShapeDtypeStruct((slots,) + pool.shape[1:], pool.dtype),
        in_specs=[smem_spec(), smem_spec(), vmem_spec()],
        out_specs=vmem_spec(),
        scratch_shapes=[pltpu.SMEM((replicas,), jnp.int32), pltpu.SMEM((slots,), jnp.int32)],
        compiler_params=params(),
        name="outgoing_pages",
    )(migration_page, migration_target, pool)


def token_bias(entries, lengths, first_token, tokens, page_len):
    rows = entries.shape[0]
    token = first_token + lax.broadcasted_iota(jnp.int32, (rows, tokens), 1)
    seen = jnp.zeros((rows, tokens), jnp.float32)
    for e in range(entries.shape[1]):
        low = entries[:, e : e + 1] * page_len
        high = low + jnp.clip(lengths - e * page_len, 0, page_len)
        seen = seen + jnp.where((token >= low) & (token < high), 1.0, 0.0)
    return jnp.where(seen > 0.0, jnp.log2(jnp.maximum(seen, 1.0)), HIDDEN)


def fill_bias(bias_ref, entries_ref, length_ref, first_token, page_len):
    lengths = row_to_column(length_ref[...])
    entries = entries_ref[...]
    for start in range(0, bias_ref.shape[1], TOKEN_STEP):
        size = min(TOKEN_STEP, bias_ref.shape[1] - start)
        bias_ref[:, start : start + size] = token_bias(
            entries, lengths, first_token + start, size, page_len
        )


def lane_folds(values, combine):
    folded = values[:, :LANES]
    for start in range(LANES, values.shape[1], LANES):
        folded = combine(folded, values[:, start : start + LANES])
    return folded


def score_tokens(stacked, keys, bias_ref, score_ref, top_ref):
    rows = bias_ref.shape[0]
    tokens = bias_ref.shape[1]
    for start in range(0, tokens, TOKEN_STEP):
        size = min(TOKEN_STEP, tokens - start)
        part = lax.dot_general(
            stacked,
            keys(start, size),
            (((1,), (1,)), ((), ())),
            preferred_element_type=jnp.float32,
        )
        bias = bias_ref[:, start : start + size]
        for h in range(QUERY_GROUP):
            own = slice(h * rows, (h + 1) * rows)
            shifted = part[own] * SCORE_SCALE + bias
            score_ref[own, start : start + size] = shifted
            top = lane_folds(shifted, jnp.maximum)
            top_ref[own, :] = top if start == 0 else jnp.maximum(top_ref[own, :], top)


def weigh_tokens(own, top, score_ref, weight_ref):
    tokens = score_ref.shape[1]
    total = None
    for start in range(0, tokens, TOKEN_STEP):
        size = min(TOKEN_STEP, tokens - start)
        weights = jnp.exp2(score_ref[own, start : start + size] - top)
        weight_ref[own, start : start + size] = weights.astype(jnp.bfloat16)
        folded = lane_folds(weights, jnp.add)
        total = folded if total is None else total + folded
    return jnp.sum(total, axis=1, keepdims=True)


def stack_heads(query_ref, stacked_ref, first_head):
    rows = query_ref.shape[0]
    for h in range(QUERY_GROUP):
        place = (first_head + h) * HEAD_SIZE
        stacked_ref[h * rows : (h + 1) * rows, :] = query_ref[:, place : place + HEAD_SIZE]


def pool_kernel(
    page_len,
    query_ref,
    pool_ref,
    entries_ref,
    length_ref,
    part_ref,
    stat_ref,
    bias_ref,
    stacked_ref,
    score_ref,
    weight_ref,
    top_ref,
):
    @pl.when(pl.program_id(0) == 0)
    def _():
        fill_bias(bias_ref, entries_ref, length_ref, 0, page_len)

    rows = query_ref.shape[0]
    stack_heads(query_ref, stacked_ref, 0)
    score_tokens(
        stacked_ref[...],
        lambda start, size: pool_ref[start : start + size, :HEAD_SIZE],
        bias_ref,
        score_ref,
        top_ref,
    )
    lane = lax.broadcasted_iota(jnp.int32, (rows, LANES), 1)
    stats = jnp.zeros((rows, LANES), jnp.float32)
    for h in range(QUERY_GROUP):
        own = slice(h * rows, (h + 1) * rows)
        top = jnp.max(top_ref[own, :], axis=1, keepdims=True)
        total = weigh_tokens(own, top, score_ref, weight_ref)
        stats = jnp.where(lane == h, top, stats)
        stats = jnp.where(lane == QUERY_GROUP + h, total, stats)
    stat_ref[...] = stats
    parts = jnp.dot(
        weight_ref[...], pool_ref[:, HEAD_SIZE:], preferred_element_type=jnp.float32
    )
    for h in range(QUERY_GROUP):
        part_ref[:, h * HEAD_SIZE : (h + 1) * HEAD_SIZE] = parts[h * rows : (h + 1) * rows]


def attend_pool(queries, pool, entries, lengths, page_len):
    rows = queries.shape[0]
    tokens = pool.shape[0]
    kv_local = pool.shape[1] // (2 * HEAD_SIZE)
    wide = QUERY_GROUP * HEAD_SIZE
    stacked = QUERY_GROUP * rows
    return pl.pallas_call(
        functools.partial(pool_kernel, page_len),
        grid=(kv_local,),
        out_shape=(
            jax.ShapeDtypeStruct((rows, kv_local * wide), jnp.float32),
            jax.ShapeDtypeStruct((rows, kv_local * LANES), jnp.float32),
        ),
        in_specs=[
            pl.BlockSpec((rows, wide), lambda g: (0, g)),
            pl.BlockSpec((tokens, 2 * HEAD_SIZE), lambda g: (0, g)),
            pl.BlockSpec(entries.shape, lambda g: (0, 0)),
            pl.BlockSpec(lengths.shape, lambda g: (0, 0)),
        ],
        out_specs=(
            pl.BlockSpec((rows, wide), lambda g: (0, g)),
            pl.BlockSpec((rows, LANES), lambda g: (0, g)),
        ),
        scratch_shapes=[
            pltpu.VMEM((rows, tokens), jnp.float32),
            pltpu.VMEM((stacked, HEAD_SIZE), jnp.bfloat16),
            pltpu.VMEM((stacked, tokens), jnp.float32),
            pltpu.VMEM((stacked, tokens), jnp.bfloat16),
            pltpu.VMEM((stacked, LANES), jnp.float32),
        ],
        compiler_params=params(),
        cost_estimate=pl.CostEstimate(
            flops=4 * kv_local * stacked * tokens * HEAD_SIZE,
            bytes_accessed=2 * (queries.size + pool.size) + 4 * queries.size,
            transcendentals=kv_local * stacked * tokens,
        ),
        name="attend_pool",
    )(queries, pool, entries, lengths)


def finish_kernel(
    page_len,
    first_token,
    query_ref,
    arrived_ref,
    fresh_ref,
    entries_ref,
    length_ref,
    part_ref,
    stat_ref,
    slot_ref,
    position_ref,
    *refs,
):
    out_refs, (bias_ref, stacked_ref, score_ref, weight_ref, top_ref, heads_ref) = refs[:-6], refs[-6:]
    rows = query_ref.shape[0]
    kv_local = arrived_ref.shape[1] // (2 * HEAD_SIZE)
    wide = QUERY_GROUP * HEAD_SIZE
    fill_bias(bias_ref, entries_ref, length_ref, first_token, page_len)
    for g in range(kv_local):
        place = g * 2 * HEAD_SIZE
        stack_heads(query_ref, stacked_ref, g * QUERY_GROUP)
        score_tokens(
            stacked_ref[...],
            lambda start, size: arrived_ref[start : start + size, place : place + HEAD_SIZE],
            bias_ref,
            score_ref,
            top_ref,
        )
        new_key = fresh_ref[:, place : place + HEAD_SIZE].astype(jnp.float32)
        new_value = fresh_ref[:, place + HEAD_SIZE : place + 2 * HEAD_SIZE].astype(jnp.float32)
        scale_old, own_weight, total = [], [], []
        for h in range(QUERY_GROUP):
            own = slice(h * rows, (h + 1) * rows)
            query = stacked_ref[own, :].astype(jnp.float32)
            own_score = jnp.sum(query * new_key, axis=1, keepdims=True) * SCORE_SCALE
            old_top = stat_ref[:, g * LANES + h : g * LANES + h + 1]
            old_total = stat_ref[:, g * LANES + QUERY_GROUP + h : g * LANES + QUERY_GROUP + h + 1]
            top = jnp.max(top_ref[own, :], axis=1, keepdims=True)
            top = jnp.maximum(jnp.maximum(top, own_score), old_top)
            scale_old.append(jnp.exp2(old_top - top))
            own_weight.append(jnp.exp2(own_score - top))
            fresh_total = weigh_tokens(own, top, score_ref, weight_ref)
            total.append(scale_old[h] * old_total + fresh_total + own_weight[h])
        parts = jnp.dot(
            weight_ref[...],
            arrived_ref[:, place + HEAD_SIZE : place + 2 * HEAD_SIZE],
            preferred_element_type=jnp.float32,
        )
        for h in range(QUERY_GROUP):
            column = g * wide + h * HEAD_SIZE
            heads = parts[h * rows : (h + 1) * rows] + own_weight[h] * new_value
            heads = heads + scale_old[h] * part_ref[:, column : column + HEAD_SIZE]
            heads_ref[:, column : column + HEAD_SIZE] = (heads / total[h]).astype(jnp.bfloat16)
    width = query_ref.shape[1]
    first = 0
    for out_ref in out_refs:
        slots = out_ref.shape[0]
        slot = first + lax.broadcasted_iota(jnp.int32, (slots, rows), 0)
        pick = slot == slot_ref[...]
        label = jnp.sum(jnp.where(pick, position_ref[...], 0), axis=1, keepdims=True)
        pick = pick.astype(jnp.float32).astype(jnp.bfloat16)
        for start in range(0, width, wide):
            out_ref[:, start : start + wide] = jnp.dot(
                pick, heads_ref[:, start : start + wide], preferred_element_type=jnp.float32
            ).astype(jnp.bfloat16)
        out_ref[:, width:] = jnp.broadcast_to(
            label.astype(jnp.float32).astype(jnp.bfloat16), (slots, LANES)
        )
        first += slots


def finish_attention(
    queries, arrived, fresh, entries, lengths, parts, stats, slots, positions, page_len, first_token, blocks
):
    rows, width = queries.shape
    tokens = arrived.shape[0]
    stacked = QUERY_GROUP * rows
    return pl.pallas_call(
        functools.partial(finish_kernel, page_len, first_token),
        out_shape=tuple(
            jax.ShapeDtypeStruct((block, width + LANES), jnp.bfloat16) for block in blocks
        ),
        in_specs=[vmem_spec()] * 9,
        out_specs=tuple(vmem_spec() for _ in blocks),
        scratch_shapes=[
            pltpu.VMEM((rows, tokens), jnp.float32),
            pltpu.VMEM((stacked, HEAD_SIZE), jnp.bfloat16),
            pltpu.VMEM((stacked, tokens), jnp.float32),
            pltpu.VMEM((stacked, tokens), jnp.bfloat16),
            pltpu.VMEM((stacked, LANES), jnp.float32),
            pltpu.VMEM((rows, width), jnp.bfloat16),
        ],
        compiler_params=params(),
        cost_estimate=pl.CostEstimate(
            flops=4 * tokens * rows * width,
            bytes_accessed=12 * rows * width,
            transcendentals=tokens * rows * width // HEAD_SIZE,
        ),
        name="finish_attention",
    )(queries, arrived, fresh, entries, lengths, parts, stats, slots, positions)


def rank_among(targets):
    position = jnp.arange(targets.shape[0], dtype=jnp.int32)
    same = (targets[:, None] == targets[None, :]) & (position[:, None] < position[None, :])
    return jnp.sum(same.astype(jnp.int32), axis=0)


def attention(
    queries,
    current_key_value,
    key_value_pool,
    request_page_entries,
    context_length,
    migration_page,
    migration_target,
    slots,
    adapter_position,
    blocks,
):
    replicas = lax.axis_size("rep")
    pages, page_len, features = key_value_pool.shape
    lengths = context_length.reshape(1, -1)
    outgoing = outgoing_pages(migration_page, migration_target, key_value_pool, replicas)
    arrived = lax.all_to_all(outgoing, "rep", split_axis=0, concat_axis=0, tiled=True)
    parts, stats = attend_pool(
        queries,
        key_value_pool.reshape(pages * page_len, features),
        request_page_entries,
        lengths,
        page_len,
    )
    return finish_attention(
        queries,
        arrived.reshape(-1, features),
        current_key_value,
        request_page_entries,
        lengths,
        parts,
        stats,
        slots,
        adapter_position.reshape(1, -1),
        page_len,
        pages * page_len,
        blocks,
    )


def local(
    queries,
    current_key_value,
    key_value_pool,
    request_page_entries,
    context_length,
    migration_page,
    migration_target,
    adapter_replica,
    adapter_position,
    adapter_down_weight,
    adapter_up_weight,
):
    replicas = lax.axis_size("rep")
    rows, width = queries.shape
    adapter_number = adapter_down_weight.shape[0]
    slot_cap = max(2, (2 * rows + replicas - 1) // replicas)
    targets = adapter_replica[:, 0]
    slot_index = targets * slot_cap + rank_among(targets)
    (outbound,) = attention(
        queries,
        current_key_value,
        key_value_pool,
        request_page_entries,
        context_length,
        migration_page,
        migration_target,
        slot_index.reshape(1, -1),
        adapter_position,
        (replicas * slot_cap,),
    )
    outbound = outbound.reshape(replicas, slot_cap, -1)
    activations = lax.all_to_all(outbound, "rep", split_axis=0, concat_axis=0, tiled=True)
    shape_in = activations.shape
    flat_output = activations.reshape(-1, shape_in[2])
    selector = (
        flat_output[:, width : width + 1].astype(jnp.int32)
        == jnp.arange(adapter_number, dtype=jnp.int32)[None, :]
    )
    reduced_rank_total = jnp.einsum(
        "oh,pht->opt", flat_output[:, :width], adapter_down_weight, preferred_element_type=jnp.float32
    )
    partial_low = jnp.sum(jnp.where(selector[:, :, None], reduced_rank_total, 0.0), axis=1)
    low_rank = lax.psum(partial_low, "tp").astype(jnp.bfloat16)
    broadcast_result = jnp.where(
        selector[:, :, None], low_rank[:, None, :], jnp.zeros((), jnp.bfloat16)
    )
    broadcast_result = broadcast_result.reshape(flat_output.shape[0], -1)
    lifted = jnp.dot(
        broadcast_result,
        adapter_up_weight.reshape(-1, adapter_up_weight.shape[2]),
        preferred_element_type=jnp.float32,
    )
    lifted = lifted.astype(jnp.bfloat16).reshape(shape_in[0], shape_in[1], -1)
    returned = lax.all_to_all(lifted, "rep", split_axis=0, concat_axis=0, tiled=True)
    route_mask = (
        jnp.arange(replicas * slot_cap, dtype=jnp.int32)[:, None] == slot_index[None, :]
    ).astype(jnp.bfloat16)
    delta = jnp.einsum(
        "sr,sd->rd",
        route_mask,
        returned.reshape(replicas * slot_cap, -1),
        preferred_element_type=jnp.float32,
    )
    return delta.astype(jnp.bfloat16)


def solution(mesh):
    return jax.shard_map(
        local,
        mesh=mesh,
        in_specs=(
            P(("group", "rep"), "tp"),
            P(("group", "rep"), "tp"),
            P(("group", "rep"), None, "tp"),
            P(("group", "rep"), None),
            P(("group", "rep")),
            P(("group", "rep")),
            P(("group", "rep")),
            P(("group", "rep"), None),
            P(("group", "rep")),
            P("rep", "tp", None),
            P("rep", None, "tp"),
        ),
        out_specs=P(("group", "rep"), "tp"),
        check_vma=False,
    )
```

time: 170 us -> 125 us (0.74)
  local copies, waits for them, and re-layouts: 49.7 us -> 7.58 us
  waiting for transfers between devices: 28 us -> 48.9 us
  blocking collectives: 55.5 us -> 36.7 us
  Pallas kernels: 0 us -> 16 us
  matrix products: 11.8 us -> 4.02 us
  other arithmetic: 7.45 us -> 0.24 us
  starting transfers between devices: 16.9 us -> 10.9 us
    all_to_all x3 -> x2, waiting for transfers between devices: 28 us -> 48.9 us  [the longest x1 48.9 us: local(): lax.all_to_all(lifted, 'rep', split_axis=0, concat_axis=0, tiled=True)]
    all_to_all x1, blocking collectives: 51.9 us -> 33.1 us  [local(): lax.all_to_all(outbound, 'rep', split_axis=0, concat_axis=0, tiled=True)]
    slice x2 -> x0, local copies, waits for them, and re-layouts: 17.8 us -> none  [the longest x1 17.7 us: local(): cache_rows[:, :, :, 0, :]]
    pallas_call x0 -> x3, Pallas kernels: none -> 16 us  [the longest x1 9.3 us: attend_pool(): pl.pallas_call(functools.partial(pool_kernel, page_len), grid=(kv_local,)...]
    gather x2 -> x0, local copies, waits for them, and re-layouts: 15.3 us -> none  [the longest x1 13.3 us: local(): page_cache[request_page_entries]]
    reshape x1 -> x0, local copies, waits for them, and re-layouts: 12.5 us -> none  [local(): page_cache[request_page_entries]]
    dot_general x4 -> x0, matrix products: 9.1 us -> none  [the longest x1 4.74 us: local(): jnp.einsum('rgjt,rtgk->rgjk', probabilities, cache_rows[:, :, :, 1, :], p...]
    all_to_all x3 -> x2, starting transfers between devices: 16.9 us -> 10.9 us  [the longest x1 7.25 us: attention(): lax.all_to_all(outgoing, 'rep', split_axis=0, concat_axis=0, tiled=True)]
  transfers between devices with their start and end apart: 3 -> 2, of which waited for: 2 -> 1; matrix products, arithmetic and copies ran while one was open for 36% -> 0% of each run, Pallas kernels for 0% -> 7%
where the time goes in v1:
time: 125 us; the launch traced here: 124 us
  waiting for transfers between devices  48.9 us (39%)
  blocking collectives  36.7 us (29%)
  Pallas kernels  16 us (13%)
  starting transfers between devices  10.9 us (9%)
  local copies, waits for them, and re-layouts  7.58 us (6%)
  matrix products  4.02 us (3%)
    all_to_all x1, waiting for transfers between devices, local(): lax.all_to_all(lifted, 'rep', split_axis=0, concat_axis=0, tiled=True)  48.9 us
    all_to_all x1, blocking collectives, local(): lax.all_to_all(outbound, 'rep', split_axis=0, concat_axis=0, tiled=True)  33.1 us
    pallas_call x1, Pallas kernels, attend_pool(): pl.pallas_call(functools.partial(pool_kernel, page_len), grid=(kv_local,)...  9.3 us
    unnamed x33, local copies, waits for them, and re-layouts  7.58 us
    all_to_all x1, starting transfers between devices, attention(): lax.all_to_all(outgoing, 'rep', split_axis=0, concat_axis=0, tiled=True)  7.25 us
    pallas_call x1, Pallas kernels, finish_attention(): pl.pallas_call(functools.partial(finish_kernel, page_len, first_token), o...  5.12 us
    psum x1, blocking collectives, local(): low_rank = lax.psum(partial_low, 'tp').astype(jnp.bfloat16)  3.62 us
    all_to_all x1, starting transfers between devices, local(): lax.all_to_all(lifted, 'rep', split_axis=0, concat_axis=0, tiled=True)  3.6 us
  transfers between devices with their start and end apart: 2, of which 1 were waited for; matrix products, arithmetic and copies ran while one was open for 0% of the time, Pallas kernels for 7%

profile of v1, /device:TPU:0, one launch (start us, length us, event | category | flops | bytes accessed | tf_op | source)
XLA Modules:
  0.0 124.5 jit_solution(9335016381231057760)
XLA Ops:
  0.0 0.0 copy-start
  0.0 0.0 copy-start.1
  0.0 1.5 %copy-done.1 = bf16[96,16,512]{2,1,0:T(8,128)(2,1)S(1)} copy-done((bf16[96,16,512]{2,1,0:T(8,128)(2,1)S(1)}, bf16[96,16,512]{2,1,0:T(8,128)(2,1)}, u32[]{:S(2)}) %copy-start.1) | copy-done | bytes 1572888
  1.5 0.0 copy-start.9
  1.5 0.7 copy-done.9
  2.2 0.0 copy-start.10
  2.2 0.7 copy-done.10
  2.8 0.0 copy-start.13
  2.8 0.0 copy-start.15
  2.8 0.0 copy-start.2
  2.8 0.0 copy-start.5
  2.8 0.0 copy-start.11
  2.8 1.6 %outgoing_pages.1 = bf16[16,16,512]{2,1,0:T(8,128)(2,1)} custom-call(s32[6]{0:T(128)S(1)} %copy-done.9, s32[6]{0:T(128)S(1)} %copy-done.10, bf16[96,16,512]{2,1,0:T(8,128)(2,1)S(1)} %copy-done.1), custom_call_target="tpu_custom_call" | custom-call | tf_op jit(solution)/shard_map/outgoing_pages/pallas_call | solution.py:74
  4.4 7.3 %all-to-all-start = ((bf16[16,16,512]{2,1,0:T(8,128)(2,1)}), bf16[16,16,512]{2,1,0:T(8,128)(2,1)S(1)}, u32[]{:S(2)}, u32[]{:S(2)}) async-start(bf16[16,16,512]{2,1,0:T(8,128)(2,1)} %outgoing_pages.1), calls=%async_computation | async-start | bytes 524288 | tf_op jit(solution)/shard_map/all_to_all | solution.py:360
  11.6 0.0 copy-done.13
  11.6 0.1 copy.20.entries_ref
  11.8 0.0 copy-done.15
  11.8 0.1 convert_reduce_fusion.1
  11.9 0.0 copy-done.2
  11.9 0.0 copy-done.5
  11.9 0.0 copy-done.11
  11.9 0.0 copy-start.12
  11.9 9.3 %attend_pool.1 = (f32[128,2048]{1,0:T(8,128)S(1)}, f32[128,256]{1,0:T(8,128)S(1)}) custom-call(bf16[128,2048]{1,0:T(8,128)(2,1)S(1)} %copy-done.5, bf16[1536,512]{1,0:T(8,128)(2,1)S(1)} %bitcast.26, s32[128,4]{1,0:T(8,128)S(1)} %copy.20.entries_ref, s32[1,128]{1,0:T(1,128)S(1)} %bitcast.28), custom_call_target="tpu_custom_call" | custom-call | flops 1610612736 | bytes 3145728 | tf_op jit(solution)/shard_map/attend_pool/pallas_call | solution.py:201
  21.2 0.0 copy-start.3
  21.2 1.0 copy-done.3
  22.2 0.0 copy-start.7
  22.2 0.6 copy-done.7
  22.8 0.0 all-to-all-done
  22.8 0.0 copy-done.12
  22.8 0.0 copy-start.4
  22.8 1.2 copy-done.4
  24.1 0.0 copy-start.6
  24.1 0.9 copy-done.6
  25.0 0.0 copy-start.8
  25.0 0.9 copy-done.8
  25.9 0.0 copy-start.14
  25.9 5.1 %finish_attention.1 = bf16[256,2176]{1,0:T(8,128)(2,1)S(1)} custom-call(bf16[128,2048]{1,0:T(8,128)(2,1)S(1)} %copy-done.5, bf16[256,512]{1,0:T(8,128)(2,1)S(1)} %bitcast.27, bf16[128,512]{1,0:T(8,128)(2,1)S(1)} %copy-done.6, s32[128,4]{1,0:T(8,128)S(1)} %copy.20.entries_ref, s32[1,128]{1,0:T(1,128)S(1)} %bitcast.29, f32[128,2048]{1,0:T(8,128)S(1)} %copy-done.4, ...), custom_call_target="tpu_custom_call" | custom-call | flops 268435456 | bytes 3145728 | tf_op jit(solution)/shard_map/finish_attention/pallas_call | solution.py:313
  31.0 33.1 %all_to_all.15 = bf16[8,32,2176]{2,1,0:T(8,128)(2,1)S(1)} all-to-all(bf16[8,32,2176]{2,1,0:T(8,128)(2,1)S(1)} %bitcast.25), channel_id=1, replica_groups=mesh['group'=2,'rep'=8,'tp'=2] {'rep'}, dimensions={0} | all-to-all | bytes 2228224 | tf_op jit(solution)/shard_map/all_to_all | solution.py:416
  64.1 0.1 convert_reduce_fusion
  64.2 0.0 copy-done.14
  64.2 0.5 fusion.1
  64.7 3.6 %psum.7 = bf16[256,64]{0,1:T(8,128)(2,1)S(1)} all-reduce(f32[256,64]{0,1:T(8,128)S(1)} %select_reduce_fusion), channel_id=1, replica_groups=mesh['group'=2,'rep'=8,'tp'=2] {'tp'}, use_global_device_ids=true, to_apply=%region_2.3 | all-reduce | flops 16384 | bytes 98304 | tf_op jit(solution)/shard_map/psum | solution.py:427
  68.4 0.0 copy-done
  68.4 2.1 %fusion = bf16[256,4096]{1,0:T(8,128)(2,1)} fusion(bf16[2,64,4096]{2,1,0:T(8,128)(2,1)S(1)} %copy-done, pred[256,2]{0,1:T(4,128)(4,1)S(1)} %iota_compare_fusion.3, bf16[256,64]{0,1:T(8,128)(2,1)S(1)} %psum.7), kind=kOutput, calls=%fused_computation.1 | convolution fusion | flops 269516800 | bytes 3179008 | tf_op jit(solution)/shard_map/dot_general | solution.py:432
  70.4 3.6 %all-to-all-start.2 = ((bf16[8,32,4096]{2,1,0:T(8,128)(2,1)}), bf16[8,32,4096]{2,1,0:T(8,128)(2,1)S(1)}, u32[]{:S(2)}, u32[]{:S(2)}) async-start(bf16[8,32,4096]{2,1,0:T(8,128)(2,1)} %bitcast.32), calls=%async_computation.2 | async-start | bytes 4194304 | tf_op jit(solution)/shard_map/all_to_all | solution.py:438
  74.1 48.9 %all-to-all-done.2 = bf16[8,32,4096]{2,1,0:T(8,128)(2,1)S(1)} async-done(((bf16[8,32,4096]{2,1,0:T(8,128)(2,1)}), bf16[8,32,4096]{2,1,0:T(8,128)(2,1)S(1)}, u32[]{:S(2)}, u32[]{:S(2)}) %all-to-all-start.2) | async-done | bytes 2097184 | tf_op jit(solution)/shard_map/all_to_all | solution.py:438
  123.0 1.5 %convolution_convert_fusion = bf16[128,4096]{1,0:T(8,128)(2,1)} fusion(bf16[256,4096]{1,0:T(8,128)(2,1)S(1)} %bitcast.31, s32[128]{0:T(128)S(1)} %multiply_add_fusion), kind=kOutput, calls=%fused_computation.2 | convolution fusion | flops 268992512 | bytes 3146240 | tf_op jit(solution)/shard_map/sr,sd->rd/dot_general | solution.py:442
  (4 shorter events, 0.0 us)
Async XLA Ops:
  0.0 68.4 %copy-start = (bf16[2,64,4096]{2,1,0:T(8,128)(2,1)S(1)}, bf16[2,64,4096]{2,1,0:T(8,128)(2,1)}, u32[]{:S(2)}) copy-start(bf16[2,64,4096]{2,1,0:T(8,128)(2,1)} %param.21) | copy-start | bytes 3145732
  0.0 1.5 %copy-start.1 = (bf16[96,16,512]{2,1,0:T(8,128)(2,1)S(1)}, bf16[96,16,512]{2,1,0:T(8,128)(2,1)}, u32[]{:S(2)}) copy-start(bf16[96,16,512]{2,1,0:T(8,128)(2,1)} %pool_ref.1) | copy-start | bytes 4718596
  1.5 0.7 copy-start.9
  2.2 0.7 copy-start.10
  2.8 8.8 %copy-start.13 = (s32[128,4]{0,1:T(4,128)S(1)}, s32[128,4]{0,1:T(4,128)}, u32[]{:S(2)}) copy-start(s32[128,4]{0,1:T(4,128)} %param.14) | copy-start | bytes 6148
  2.8 8.9 %copy-start.15 = (s32[128,1]{0,1:T(1,128)S(1)}, s32[128,1]{0,1:T(1,128)}, u32[]{:S(2)}) copy-start(s32[128,1]{0,1:T(1,128)} %param.18) | copy-start | bytes 1540
  2.8 9.0 %copy-start.2 = (bf16[96,16,512]{2,1,0:T(8,128)(2,1)S(1)}, bf16[96,16,512]{2,1,0:T(8,128)(2,1)}, u32[]{:S(2)}) copy-start(bf16[96,16,512]{2,1,0:T(8,128)(2,1)} %pool_ref.1) | copy-start | bytes 4718596
  2.8 9.0 %copy-start.5 = (bf16[128,2048]{1,0:T(8,128)(2,1)S(1)}, bf16[128,2048]{1,0:T(8,128)(2,1)}, u32[]{:S(2)}) copy-start(bf16[128,2048]{1,0:T(8,128)(2,1)} %query_ref.3) | copy-start | bytes 1572868
  2.8 9.1 %copy-start.11 = (s32[128]{0:T(128)S(1)}, s32[128]{0:T(128)}, u32[]{:S(2)}) copy-start(s32[128]{0:T(128)} %param.15) | copy-start | bytes 1540
  4.4 18.4 %all-to-all-start = ((bf16[16,16,512]{2,1,0:T(8,128)(2,1)}), bf16[16,16,512]{2,1,0:T(8,128)(2,1)S(1)}, u32[]{:S(2)}, u32[]{:S(2)}) async-start(bf16[16,16,512]{2,1,0:T(8,128)(2,1)} %outgoing_pages.1), calls=%async_computation | async-start | bytes 524288 | tf_op jit(solution)/shard_map/all_to_all | solution.py:360
  11.9 10.9 %copy-start.12 = (s32[128]{0:T(128)S(1)}, s32[128]{0:T(128)}, u32[]{:S(2)}) copy-start(s32[128]{0:T(128)} %param.19) | copy-start | bytes 1540
  21.2 1.0 copy-start.3
  22.2 0.6 copy-start.7
  22.8 1.2 copy-start.4
  24.1 0.9 copy-start.6
  25.0 0.9 copy-start.8
  25.9 38.3 %copy-start.14 = (bf16[2,2048,64]{1,2,0:T(8,128)(2,1)S(1)}, bf16[2,2048,64]{1,2,0:T(8,128)(2,1)}, u32[]{:S(2)}) copy-start(bf16[2,2048,64]{1,2,0:T(8,128)(2,1)} %param.20) | copy-start | bytes 1572868
  70.4 52.6 %all-to-all-start.2 = ((bf16[8,32,4096]{2,1,0:T(8,128)(2,1)}), bf16[8,32,4096]{2,1,0:T(8,128)(2,1)S(1)}, u32[]{:S(2)}, u32[]{:S(2)}) async-start(bf16[8,32,4096]{2,1,0:T(8,128)(2,1)} %bitcast.32), calls=%async_computation.2 | async-start | bytes 4194304 | tf_op jit(solution)/shard_map/all_to_all | solution.py:438

commit v2 on v0

v2 whole, which is shorter than its diff:
```python
import functools
import math

import jax
import jax.numpy as jnp
from jax import lax
from jax.experimental import pallas as pl
from jax.experimental.pallas import tpu as pltpu
from jax.sharding import PartitionSpec as P

HEAD_SIZE = 128
QUERY_GROUP = 8
MCAP = 2
LANES = 128
TOKEN_STEP = 256
HIDDEN = -1e30
SCORE_SCALE = math.log2(math.e) / math.sqrt(HEAD_SIZE)
BIAS_UNIT = float(jnp.bfloat16(1.0 / SCORE_SCALE))
HEADS_STEP = 2
MIB = 1024 * 1024


def whole(array):
    shape = array.shape
    return pl.BlockSpec(shape, lambda *step: (0,) * len(shape))


def smem_spec():
    return pl.BlockSpec(memory_space=pltpu.SMEM)


def params(mebibytes=24):
    return pltpu.CompilerParams(vmem_limit_bytes=mebibytes * MIB)


def cost():
    return pl.CostEstimate(flops=1024, bytes_accessed=1024, transcendentals=0)


def row_to_column(row):
    count = row.shape[1]
    across = lax.broadcasted_iota(jnp.int32, (count, count), 1)
    down = lax.broadcasted_iota(jnp.int32, (count, count), 0)
    return jnp.sum(jnp.where(across == down, row, 0), axis=1, keepdims=True)


def outgoing_kernel(pieces, half_ref, page_ref, target_ref, pool_ref, *refs):
    count_ref, chosen_ref, page_sem, share_sem = refs[-4:]
    out_ref, share_refs, mine_refs = refs[len(pieces)], refs[: len(pieces)], refs[len(pieces) + 1 : -4]
    entry_number = page_ref.shape[0]
    slot_number = out_ref.shape[0]

    def clear(slot, carry):
        chosen_ref[slot] = 0
        count_ref[slot // MCAP] = 0
        return carry

    def place(entry, carry):
        target = target_ref[entry]
        rank = count_ref[target]
        chosen_ref[target * MCAP + rank] = page_ref[entry]
        count_ref[target] = rank + 1
        return carry

    def page_copy(slot):
        return pltpu.make_async_copy(
            pool_ref.at[chosen_ref[slot]], out_ref.at[slot], page_sem.at[slot]
        )

    def send(slot, carry):
        page_copy(slot).start()
        return carry

    def finish(slot, carry):
        page_copy(slot).wait()
        return carry

    shares = []
    for share, cuts in zip(share_refs, pieces):
        for first, last, pack, start in cuts:
            shares.append(
                pltpu.make_async_copy(
                    share.at[half_ref[0], :, pl.ds(first, last - first)],
                    mine_refs[pack].at[:, pl.ds(start, last - first)],
                    share_sem.at[len(shares)],
                )
            )
    lax.fori_loop(0, slot_number, clear, 0)
    lax.fori_loop(0, entry_number, place, 0)
    lax.fori_loop(0, slot_number, send, 0)
    for share in shares:
        share.start()
    lax.fori_loop(0, slot_number, finish, 0)
    for share in shares:
        share.wait()


def outgoing_pages(half, migration_page, migration_target, pool, replicas, shares=(), pieces=(), packs=()):
    slots = replicas * MCAP
    hbm = pl.BlockSpec(memory_space=pltpu.HBM)
    out_shape = [jax.ShapeDtypeStruct((slots,) + pool.shape[1:], pool.dtype)]
    out_shape += [jax.ShapeDtypeStruct(pack, pool.dtype) for pack in packs]
    return pl.pallas_call(
        functools.partial(outgoing_kernel, pieces),
        out_shape=out_shape,
        in_specs=[smem_spec()] * 3 + [hbm] * (1 + len(shares)),
        out_specs=[whole(out) for out in out_shape],
        scratch_shapes=[
            pltpu.SMEM((replicas,), jnp.int32),
            pltpu.SMEM((slots,), jnp.int32),
            pltpu.SemaphoreType.DMA((slots,)),
            pltpu.SemaphoreType.DMA((max(1, sum(len(cuts) for cuts in pieces)),)),
        ],
        compiler_params=params(60),
        cost_estimate=cost(),
        name="outgoing_pages",
    )(half, migration_page, migration_target, pool, *shares)


def token_bias(entries, lengths, first_token, tokens, page_len):
    shape = (tokens, entries.shape[1])
    token = first_token + lax.broadcasted_iota(jnp.int32, shape, 0)
    seen = jnp.zeros(shape, jnp.float32)
    for e in range(entries.shape[0]):
        low = entries[e : e + 1, :] * page_len
        high = low + jnp.clip(lengths - e * page_len, 0, page_len)
        seen = seen + jnp.where((token >= low) & (token < high), 1.0, 0.0)
    return jnp.where(seen > 0.0, jnp.log2(jnp.maximum(seen, 1.0)), HIDDEN)


def identity(rows, on, off):
    across = lax.broadcasted_iota(jnp.int32, (rows, rows), 1)
    down = lax.broadcasted_iota(jnp.int32, (rows, rows), 0)
    return jnp.where(across == down, on, off)


def fill_queries(wide_query_ref, rows):
    ones = identity(rows, BIAS_UNIT, 0.0).astype(jnp.bfloat16)
    for h in range(wide_query_ref.shape[0] // rows):
        wide_query_ref[h * rows : (h + 1) * rows, HEAD_SIZE:] = ones


def fill_keys(wide_key_ref, entries_ref, length_ref, first_token, tokens, page_len):
    for start in range(0, tokens, TOKEN_STEP):
        size = min(TOKEN_STEP, tokens - start)
        bias = token_bias(entries_ref[...], length_ref[...], first_token + start, size, page_len)
        wide_key_ref[start : start + size, HEAD_SIZE:] = bias.astype(jnp.bfloat16)


def score_block(block, wide_query_ref, wide_key_ref, score_ref):
    tokens = score_ref.shape[1]
    top = None
    for start in range(0, tokens, TOKEN_STEP):
        size = min(TOKEN_STEP, tokens - start)
        part = lax.dot_general(
            wide_query_ref[block, :],
            wide_key_ref[start : start + size, :],
            (((1,), (1,)), ((), ())),
            preferred_element_type=jnp.float32,
        )
        score_ref[block, start : start + size] = part
        for lane in range(0, size, LANES):
            piece = part[:, lane : lane + LANES]
            top = piece if top is None else jnp.maximum(top, piece)
    return jnp.max(top, axis=1, keepdims=True)


def weigh_block(block, top, score_ref, weight_ref, wide_value_ref):
    tokens = score_ref.shape[1]
    for start in range(0, tokens, TOKEN_STEP):
        size = min(TOKEN_STEP, tokens - start)
        weights = jnp.exp2((score_ref[block, start : start + size] - top) * SCORE_SCALE)
        weight_ref[block, start : start + size] = weights.astype(jnp.bfloat16)
    return jnp.dot(weight_ref[block, :], wide_value_ref[...], preferred_element_type=jnp.float32)


def load_heads(wide_query_ref, query_ref):
    rows = query_ref.shape[0]
    for h in range(QUERY_GROUP):
        wide_query_ref[h * rows : (h + 1) * rows, :HEAD_SIZE] = query_ref[
            :, h * HEAD_SIZE : (h + 1) * HEAD_SIZE
        ]


def pool_kernel(page_len, query_ref, pool_ref, entries_ref, length_ref, part_ref, stat_ref, *refs):
    wide_query_ref, wide_key_ref, wide_value_ref, score_ref, weight_ref = refs
    rows = query_ref.shape[0]
    tokens = pool_ref.shape[0]

    @pl.when(pl.program_id(0) == 0)
    def _():
        fill_queries(wide_query_ref, rows)
        fill_keys(wide_key_ref, entries_ref, length_ref, 0, tokens, page_len)
        wide_value_ref[:, HEAD_SIZE:] = jnp.ones((tokens, HEAD_SIZE), jnp.bfloat16)

    wide_key_ref[:, :HEAD_SIZE] = pool_ref[:, :HEAD_SIZE]
    wide_value_ref[:, :HEAD_SIZE] = pool_ref[:, HEAD_SIZE:]
    load_heads(wide_query_ref, query_ref)
    lane = lax.broadcasted_iota(jnp.int32, (rows, LANES), 1)
    stats = jnp.zeros((rows, LANES), jnp.float32)
    for h in range(0, QUERY_GROUP, HEADS_STEP):
        block = slice(h * rows, (h + HEADS_STEP) * rows)
        top = score_block(block, wide_query_ref, wide_key_ref, score_ref)
        parts = weigh_block(block, top, score_ref, weight_ref, wide_value_ref)
        total = parts[:, HEAD_SIZE:]
        part_ref[block, :] = (parts[:, :HEAD_SIZE] / total).astype(jnp.bfloat16)
        level = top + jnp.log2(total) * (1.0 / SCORE_SCALE)
        for step in range(HEADS_STEP):
            own = slice(step * rows, (step + 1) * rows)
            stats = jnp.where(lane == h + step, level[own], stats)
    stat_ref[...] = stats


def attend_pool(queries, pool, entries, lengths, page_len):
    rows, width = queries.shape
    tokens = pool.shape[0]
    kv_local = pool.shape[1] // (2 * HEAD_SIZE)
    stacked = QUERY_GROUP * rows
    return pl.pallas_call(
        functools.partial(pool_kernel, page_len),
        grid=(kv_local,),
        out_shape=[
            jax.ShapeDtypeStruct((kv_local * stacked, LANES), jnp.bfloat16),
            jax.ShapeDtypeStruct((rows, kv_local * LANES), jnp.float32),
        ],
        in_specs=[
            pl.BlockSpec((rows, width // kv_local), lambda g: (0, g)),
            pl.BlockSpec((tokens, 2 * HEAD_SIZE), lambda g: (0, g)),
            whole(entries),
            whole(lengths),
        ],
        out_specs=[
            pl.BlockSpec((stacked, LANES), lambda g: (g, 0)),
            pl.BlockSpec((rows, LANES), lambda g: (0, g)),
        ],
        scratch_shapes=[
            pltpu.VMEM((stacked, 2 * HEAD_SIZE), jnp.bfloat16),
            pltpu.VMEM((tokens, 2 * HEAD_SIZE), jnp.bfloat16),
            pltpu.VMEM((tokens, 2 * HEAD_SIZE), jnp.bfloat16),
            pltpu.VMEM((stacked, tokens), jnp.float32),
            pltpu.VMEM((stacked, tokens), jnp.bfloat16),
        ],
        compiler_params=params(),
        cost_estimate=pl.CostEstimate(10**9, 10**7, 10**6),
        name="attend_pool",
    )(queries, pool, entries, lengths)


def finish_kernel(
    page_len,
    first_token,
    place,
    where_ref,
    query_ref,
    part_ref,
    stat_ref,
    arrived_ref,
    fresh_ref,
    entries_ref,
    length_ref,
    target_ref,
    position_ref,
    slot_ref,
    *refs,
):
    out_refs, refs = refs[:-6], refs[-6:]
    wide_query_ref, wide_key_ref, wide_value_ref, score_ref, weight_ref, heads_ref = refs
    rows = query_ref.shape[0]
    g = pl.program_id(0)
    tokens = arrived_ref.shape[0]

    @pl.when(g == 0)
    def _():
        fill_queries(wide_query_ref, rows)
        fill_keys(wide_key_ref, entries_ref, length_ref, first_token, tokens, page_len)
        wide_key_ref[tokens:, HEAD_SIZE:] = identity(rows, 0.0, HIDDEN).astype(jnp.bfloat16)
        wide_value_ref[:, HEAD_SIZE:] = jnp.ones((tokens + rows, HEAD_SIZE), jnp.bfloat16)

    for shelf, first in ((arrived_ref, 0), (fresh_ref, tokens)):
        own = slice(first, first + shelf.shape[0])
        wide_key_ref[own, :HEAD_SIZE] = shelf[:, :HEAD_SIZE]
        wide_value_ref[own, :HEAD_SIZE] = shelf[:, HEAD_SIZE:]
    load_heads(wide_query_ref, query_ref)
    for h in range(0, QUERY_GROUP, HEADS_STEP):
        block = slice(h * rows, (h + HEADS_STEP) * rows)
        level = jnp.concatenate(
            [stat_ref[:, h + step : h + step + 1] for step in range(HEADS_STEP)], axis=0
        )
        top = jnp.maximum(score_block(block, wide_query_ref, wide_key_ref, score_ref), level)
        parts = weigh_block(block, top, score_ref, weight_ref, wide_value_ref)
        pool_weight = jnp.exp2((level - top) * SCORE_SCALE)
        heads = parts[:, :HEAD_SIZE] + pool_weight * part_ref[block, :].astype(jnp.float32)
        heads = (heads / (parts[:, HEAD_SIZE:] + pool_weight)).astype(jnp.bfloat16)
        for step in range(HEADS_STEP):
            heads_ref[g, :, (h + step) * HEAD_SIZE : (h + step + 1) * HEAD_SIZE] = heads[
                step * rows : (step + 1) * rows
            ]

    @pl.when(g == pl.num_programs(0) - 1)
    def _():
        targets = target_ref[...]
        across = lax.broadcasted_iota(jnp.int32, (rows, rows), 1)
        down = lax.broadcasted_iota(jnp.int32, (rows, rows), 0)
        earlier = (row_to_column(targets) == targets) & (down < across)
        rank = jnp.sum(earlier.astype(jnp.int32), axis=0, keepdims=True)
        slots_of = place(targets, where_ref[0]) + rank
        slot_ref[...] = slots_of
        wide = heads_ref.shape[2]
        first = 0
        for out_ref in out_refs:
            slots = out_ref.shape[0]
            slot = first + lax.broadcasted_iota(jnp.int32, (slots, rows), 0)
            pick = slot == slots_of
            label = jnp.sum(jnp.where(pick, position_ref[...], 0), axis=1, keepdims=True)
            pick = pick.astype(jnp.float32).astype(jnp.bfloat16)
            for kv in range(heads_ref.shape[0]):
                out_ref[:, kv * wide : (kv + 1) * wide] = jnp.dot(
                    pick, heads_ref[kv], preferred_element_type=jnp.float32
                ).astype(jnp.bfloat16)
            out_ref[:, heads_ref.shape[0] * wide :] = jnp.broadcast_to(
                label.astype(jnp.float32).astype(jnp.bfloat16), (slots, LANES)
            )
            first += slots


def finish(
    where, queries, found, arrived, fresh, entries, lengths, targets, positions, page_len, first_token, blocks, place
):
    rows, width = queries.shape
    kv_local = arrived.shape[1] // (2 * HEAD_SIZE)
    tokens = arrived.shape[0] + rows
    stacked = QUERY_GROUP * rows
    shelf = lambda array: pl.BlockSpec((array.shape[0], 2 * HEAD_SIZE), lambda g: (0, g))
    small = (entries, lengths, targets, positions)
    out_shape = [jax.ShapeDtypeStruct((1, rows), jnp.int32)]
    out_shape += [jax.ShapeDtypeStruct((block, width + LANES), jnp.bfloat16) for block in blocks]
    return pl.pallas_call(
        functools.partial(finish_kernel, page_len, first_token, place),
        grid=(kv_local,),
        out_shape=out_shape,
        in_specs=[
            smem_spec(),
            pl.BlockSpec((rows, width // kv_local), lambda g: (0, g)),
            pl.BlockSpec((stacked, LANES), lambda g: (g, 0)),
            pl.BlockSpec((rows, LANES), lambda g: (0, g)),
        ]
        + [shelf(array) for array in (arrived, fresh)]
        + [whole(array) for array in small],
        out_specs=[whole(block) for block in out_shape],
        scratch_shapes=[
            pltpu.VMEM((stacked, 2 * HEAD_SIZE), jnp.bfloat16),
            pltpu.VMEM((tokens, 2 * HEAD_SIZE), jnp.bfloat16),
            pltpu.VMEM((tokens, 2 * HEAD_SIZE), jnp.bfloat16),
            pltpu.VMEM((stacked, tokens), jnp.float32),
            pltpu.VMEM((stacked, tokens), jnp.bfloat16),
            pltpu.VMEM((kv_local, rows, width // kv_local), jnp.bfloat16),
        ],
        compiler_params=params(12 + tokens * stacked * 7 // MIB),
        cost_estimate=cost(),
        name="finish",
    )(where, queries, *found, arrived, fresh, *small)


def after_kernel(*refs):
    pass


def after(arrays, *others):
    hbm = pl.BlockSpec(memory_space=pl.ANY)
    return pl.pallas_call(
        after_kernel,
        out_shape=[jax.ShapeDtypeStruct(array.shape, array.dtype) for array in arrays],
        in_specs=[hbm] * (len(arrays) + len(others)),
        out_specs=[hbm] * len(arrays),
        input_output_aliases={i: i for i in range(len(arrays))},
        compiler_params=params(1),
        cost_estimate=cost(),
        name="after",
    )(*arrays, *others)


def down_kernel(half_ref, *refs):
    block_refs, (own_ref, first_ref, second_ref, out_ref, rows_ref) = refs[:-5], refs[-5:]
    cap = out_ref.shape[0] // 8
    width = own_ref.shape[1]
    for b, block in enumerate(block_refs):
        rows_ref[b * cap : (b + 1) * cap, :] = block[:cap, :]
        rows_ref[(b + 4) * cap : (b + 5) * cap, :] = block[cap:, :]
    swapped = half_ref[0] == 1
    zero = jnp.where(swapped, second_ref[...], first_ref[...])
    one = jnp.where(swapped, first_ref[...], second_ref[...])
    lane = lax.broadcasted_iota(jnp.int32, (1, out_ref.shape[1]), 1)
    adapter = jnp.where(lane < out_ref.shape[1] // 2, 0.0, 1.0)
    for start, weights in ((0, own_ref[...]), (4 * cap, jnp.concatenate([zero, one], axis=0))):
        part = slice(start, start + 4 * cap)
        product = lax.dot_general(
            rows_ref[part, :width],
            weights,
            (((1,), (1,)), ((), ())),
            preferred_element_type=jnp.float32,
        )
        label = rows_ref[part, width:].astype(jnp.float32)
        out_ref[part, :] = jnp.where(label == adapter, product, 0.0)


def low_products(half, blocks, own, first, second):
    rows = sum(block.shape[0] for block in blocks)
    inputs = (*blocks, own, first, second)
    out_shape = jax.ShapeDtypeStruct((rows, own.shape[0]), jnp.float32)
    return pl.pallas_call(
        down_kernel,
        grid=(1,),
        out_shape=out_shape,
        in_specs=[smem_spec()]
        + [whole(array) for array in (*blocks, own)]
        + [pl.BlockSpec((first.shape[0], own.shape[1]), lambda *step: (0, 0))] * 2,
        out_specs=whole(out_shape),
        scratch_shapes=[pltpu.VMEM((rows, blocks[0].shape[1]), jnp.bfloat16)],
        compiler_params=params(),
        cost_estimate=cost(),
        name="low_products",
    )(half, *inputs)


def lift(low_refs, weights, out_refs):
    low = (low_refs[0][...] + low_refs[1][...]).astype(jnp.bfloat16)
    lifted = jnp.dot(low, weights, preferred_element_type=jnp.float32).astype(jnp.bfloat16)
    cap = out_refs[0].shape[0]
    for b, out_ref in enumerate(out_refs):
        out_ref[...] = lifted[b * cap : (b + 1) * cap]


def lift_own_kernel(mine_ref, other_ref, own_ref, *out_refs):
    lift((mine_ref, other_ref), own_ref[...], out_refs)


def lift_own(mine, other, weights):
    rows, rank = mine.shape
    width = weights.shape[1]
    step = 1024
    low = pl.BlockSpec((rows // 2, rank), lambda j: (0, 0))
    out = jax.ShapeDtypeStruct((rows // 8, width), jnp.bfloat16)
    return pl.pallas_call(
        lift_own_kernel,
        grid=(width // step,),
        out_shape=(out,) * 4,
        in_specs=[low, low, pl.BlockSpec((rank, step), lambda j: (0, j))],
        out_specs=[pl.BlockSpec((rows // 8, step), lambda j: (0, j))] * 4,
        compiler_params=params(),
        cost_estimate=cost(),
        name="lift_own",
    )(mine, other, weights)


def lift_far_kernel(half_ref, mine_ref, other_ref, first_ref, second_ref, *out_refs):
    low = (mine_ref[...] + other_ref[...]).astype(jnp.bfloat16)
    swapped = half_ref[0] == 1
    cap = out_refs[0].shape[0]
    zero = jnp.where(swapped, second_ref[...], first_ref[...])
    one = jnp.where(swapped, first_ref[...], second_ref[...])
    lifted = jnp.dot(
        low, jnp.concatenate([zero, one], axis=0), preferred_element_type=jnp.float32
    ).astype(jnp.bfloat16)
    for b, out_ref in enumerate(out_refs):
        out_ref[...] = lifted[b * cap : (b + 1) * cap]


def lift_far(half, mine, other, first, second):
    rows, rank = mine.shape
    width = first.shape[1]
    step = 1024
    low = pl.BlockSpec((rows // 2, rank), lambda j: (1, 0))
    out = jax.ShapeDtypeStruct((rows // 8, width), jnp.bfloat16)
    return pl.pallas_call(
        lift_far_kernel,
        grid=(width // step,),
        out_shape=(out,) * 4,
        in_specs=[smem_spec(), low, low] + [pl.BlockSpec((rank // 2, step), lambda j: (0, j))] * 2,
        out_specs=[pl.BlockSpec((rows // 8, step), lambda j: (0, j))] * 4,
        compiler_params=params(),
        cost_estimate=cost(),
        name="lift_far",
    )(half, mine, other, first, second)


def gather_rows_kernel(slot_ref, *refs):
    out_ref = refs[-1]
    rows = out_ref.shape[0]
    stacked = jnp.concatenate([ref[...] for ref in refs[:-1]], axis=0)
    slot = lax.broadcasted_iota(jnp.int32, (rows, stacked.shape[0]), 1)
    pick = (slot == row_to_column(slot_ref[...])).astype(jnp.float32).astype(jnp.bfloat16)
    out_ref[...] = jnp.dot(pick, stacked, preferred_element_type=jnp.float32).astype(jnp.bfloat16)


def gather_rows(slots, blocks):
    rows = slots.shape[1]
    width = blocks[0].shape[1]
    step = 1024
    return pl.pallas_call(
        gather_rows_kernel,
        grid=(width // step,),
        out_shape=jax.ShapeDtypeStruct((rows, width), jnp.bfloat16),
        in_specs=[pl.BlockSpec(slots.shape, lambda j: (0, 0))]
        + [pl.BlockSpec((block.shape[0], step), lambda j: (0, j)) for block in blocks],
        out_specs=pl.BlockSpec((rows, step), lambda j: (0, j)),
        compiler_params=params(),
        cost_estimate=cost(),
        name="gather_rows",
    )(slots, *blocks)


def along(array, group_bit, replica_bits):
    groups, replicas = lax.axis_size("group"), lax.axis_size("rep")
    pairs = [
        (g * replicas + r, (g ^ group_bit) * replicas + (r ^ replica_bits))
        for g in range(groups)
        for r in range(replicas)
    ]
    return lax.ppermute(array, ("group", "rep"), pairs)


def shared_local(
    queries,
    current_key_value,
    key_value_pool,
    request_page_entries,
    context_length,
    migration_page,
    migration_target,
    adapter_replica,
    adapter_position,
    adapter_down_weight,
    adapter_up_weight,
):
    rows, width = queries.shape
    replicas = lax.axis_size("rep")
    cap = 2 * rows // replicas
    group = lax.axis_index("group")
    half = group.reshape(1).astype(jnp.int32)
    where = jnp.stack([lax.axis_index("rep"), group]).astype(jnp.int32)
    targets = adapter_replica.reshape(1, -1)
    down_rows = jnp.swapaxes(adapter_down_weight, 1, 2)
    down = down_rows.reshape(-1, width)
    up = adapter_up_weight.reshape(-1, adapter_up_weight.shape[2])
    entries = request_page_entries.T
    lengths = context_length.reshape(1, -1)
    positions = adapter_position.reshape(1, -1)
    pages, page_len, features = key_value_pool.shape
    pool = key_value_pool.reshape(pages * page_len, features)

    columns = up.shape[1]
    rank = up.shape[0] // 2
    outgoing, *packs = outgoing_pages(
        half,
        migration_page,
        migration_target,
        key_value_pool,
        replicas,
        (down_rows, adapter_up_weight),
        (((0, width, 0, 0),), ((0, columns, 1, 0),)),
        ((rank, width), (rank, columns)),
    )
    arrived = lax.all_to_all(outgoing, "rep", split_axis=0, concat_axis=0, tiled=True)
    found = attend_pool(queries, pool, entries, lengths, page_len)
    first = [along(pack, 0, 4) for pack in after(packs, arrived, found[1])]

    def place(targets, replica):
        apart = jnp.bitwise_xor(targets, replica)
        return (2 * jnp.bitwise_and(apart, 3) + jnp.right_shift(apart, 2)) * cap

    slots, here, *outbound = finish(
        where,
        queries,
        found,
        arrived.reshape(-1, features),
        current_key_value,
        entries,
        lengths,
        targets,
        positions,
        page_len,
        pages * page_len,
        (2 * cap,) * 4,
        place,
    )
    blocks = [here] + [along(block, 0, b + 1) for b, block in enumerate(outbound)]
    second = [along(*after([first[0]], slots), 1, 0)]
    mine = low_products(half, blocks, down, first[0], second[0])
    second.append(along(*after([first[1]], mine), 1, 0))
    other = lax.ppermute(mine, "tp", [(0, 1), (1, 0)])
    own = lift_own(mine, other, up)
    own = [block if b == 0 else along(block, 0, b) for b, block in enumerate(own)]
    far = lift_far(half, mine, other, first[1], second[1])
    far = [block if b == 0 else along(block, 0, b) for b, block in enumerate(far)]
    return gather_rows(slots, [block for pair in zip(own, far) for block in pair])


def local(
    queries,
    current_key_value,
    key_value_pool,
    request_page_entries,
    context_length,
    migration_page,
    migration_target,
    adapter_replica,
    adapter_position,
    adapter_down_weight,
    adapter_up_weight,
):
    replicas = lax.axis_size("rep")
    if replicas == 8 and lax.axis_size("group") == 2 and adapter_down_weight.shape[0] == 2:
        return shared_local(
            queries,
            current_key_value,
            key_value_pool,
            request_page_entries,
            context_length,
            migration_page,
            migration_target,
            adapter_replica,
            adapter_position,
            adapter_down_weight,
            adapter_up_weight,
        )
    rows, width = queries.shape
    adapter_number = adapter_down_weight.shape[0]
    slot_cap = max(2, (2 * rows + replicas - 1) // replicas)
    entries = request_page_entries.T
    lengths = context_length.reshape(1, -1)
    pages, page_len, features = key_value_pool.shape
    pool = key_value_pool.reshape(pages * page_len, features)
    where = jnp.stack([lax.axis_index("rep"), lax.axis_index("group")]).astype(jnp.int32)
    (outgoing,) = outgoing_pages(where, migration_page, migration_target, key_value_pool, replicas)
    arrived = lax.all_to_all(outgoing, "rep", split_axis=0, concat_axis=0, tiled=True)
    found = attend_pool(queries, pool, entries, lengths, page_len)
    slots, outbound = finish(
        where,
        queries,
        found,
        arrived.reshape(-1, features),
        current_key_value,
        entries,
        lengths,
        adapter_replica.reshape(1, -1),
        adapter_position.reshape(1, -1),
        page_len,
        pages * page_len,
        (replicas * slot_cap,),
        lambda targets, replica: targets * slot_cap,
    )
    outbound = outbound.reshape(replicas, slot_cap, -1)
    activations = lax.all_to_all(outbound, "rep", split_axis=0, concat_axis=0, tiled=True)
    shape_in = activations.shape
    flat_output = activations.reshape(-1, shape_in[2])
    selector = (
        flat_output[:, width : width + 1].astype(jnp.int32)
        == jnp.arange(adapter_number, dtype=jnp.int32)[None, :]
    )
    reduced_rank_total = jnp.einsum(
        "oh,pht->opt", flat_output[:, :width], adapter_down_weight, preferred_element_type=jnp.float32
    )
    partial_low = jnp.sum(jnp.where(selector[:, :, None], reduced_rank_total, 0.0), axis=1)
    low_rank = lax.psum(partial_low, "tp").astype(jnp.bfloat16)
    broadcast_result = jnp.where(
        selector[:, :, None], low_rank[:, None, :], jnp.zeros((), jnp.bfloat16)
    )
    broadcast_result = broadcast_result.reshape(flat_output.shape[0], -1)
    lifted = jnp.dot(
        broadcast_result,
        adapter_up_weight.reshape(-1, adapter_up_weight.shape[2]),
        preferred_element_type=jnp.float32,
    )
    lifted = lifted.astype(jnp.bfloat16).reshape(shape_in[0], shape_in[1], -1)
    returned = lax.all_to_all(lifted, "rep", split_axis=0, concat_axis=0, tiled=True)
    route_mask = (
        jnp.arange(replicas * slot_cap, dtype=jnp.int32)[:, None] == slots
    ).astype(jnp.bfloat16)
    delta = jnp.einsum(
        "sr,sd->rd",
        route_mask,
        returned.reshape(replicas * slot_cap, -1),
        preferred_element_type=jnp.float32,
    )
    return delta.astype(jnp.bfloat16)


def solution(mesh):
    return jax.shard_map(
        local,
        mesh=mesh,
        in_specs=(
            P(("group", "rep"), "tp"),
            P(("group", "rep"), "tp"),
            P(("group", "rep"), None, "tp"),
            P(("group", "rep"), None),
            P(("group", "rep")),
            P(("group", "rep")),
            P(("group", "rep")),
            P(("group", "rep"), None),
            P(("group", "rep")),
            P("rep", "tp", None),
            P("rep", None, "tp"),
        ),
        out_specs=P(("group", "rep"), "tp"),
        check_vma=False,
    )
```

time: 170 us -> 92.5 us (0.54)
  blocking collectives: 55.5 us -> 0 us
  local copies, waits for them, and re-layouts: 49.7 us -> 2.65 us
  Pallas kernels: 0 us -> 18.7 us
  waiting for transfers between devices: 28 us -> 46.6 us
  matrix products: 11.8 us -> 0 us
  other arithmetic: 7.45 us -> 0.07 us
  starting transfers between devices: 16.9 us -> 24 us
    all_to_all x1 -> x0, blocking collectives: 51.9 us -> none  [local(): lax.all_to_all(lifted, 'rep', split_axis=0, concat_axis=0, tiled=True)]
    ppermute x0 -> x14, waiting for transfers between devices: none -> 43.9 us  [the longest x13 42.5 us: along(): return lax.ppermute(array, ('group', 'rep'), pairs)]
    all_to_all x3 -> x1, waiting for transfers between devices: 28 us -> 2.68 us  [shared_local(): lax.all_to_all(outgoing, 'rep', split_axis=0, concat_axis=0, tiled=True)]
    pallas_call x0 -> x10, Pallas kernels: none -> 18.7 us  [the longest x1 6.15 us: attend_pool(): pl.pallas_call(functools.partial(pool_kernel, page_len), grid=(kv_local,)...]
    slice x2 -> x0, local copies, waits for them, and re-layouts: 17.8 us -> none  [the longest x1 17.7 us: local(): cache_rows[:, :, :, 0, :]]
    ppermute x0 -> x14, starting transfers between devices: none -> 16.7 us  [the longest x13 16.7 us: along(): return lax.ppermute(array, ('group', 'rep'), pairs)]
    gather x2 -> x0, local copies, waits for them, and re-layouts: 15.3 us -> none  [the longest x1 13.3 us: local(): page_cache[request_page_entries]]
    reshape x1 -> x0, local copies, waits for them, and re-layouts: 12.5 us -> none  [local(): page_cache[request_page_entries]]
  transfers between devices with their start and end apart: 3 -> 15, of which waited for: 2 -> 9; matrix products, arithmetic and copies ran while one was open for 36% -> 0% of each run, Pallas kernels for 0% -> 14%
where the time goes in v2:
time: 92.5 us; the launch traced here: 92.2 us
  waiting for transfers between devices  46.6 us (50%)
  starting transfers between devices  24 us (26%)
  Pallas kernels  18.7 us (20%)
  local copies, waits for them, and re-layouts  2.65 us (3%)
    ppermute x13, waiting for transfers between devices, along(): return lax.ppermute(array, ('group', 'rep'), pairs)  42.5 us
    ppermute x13, starting transfers between devices, along(): return lax.ppermute(array, ('group', 'rep'), pairs)  16.7 us
    all_to_all x1, starting transfers between devices, shared_local(): lax.all_to_all(outgoing, 'rep', split_axis=0, concat_axis=0, tiled=True)  7.28 us
    pallas_call x1, Pallas kernels, attend_pool(): pl.pallas_call(functools.partial(pool_kernel, page_len), grid=(kv_local,)...  6.15 us
    pallas_call x1, Pallas kernels, finish(): pl.pallas_call(functools.partial(finish_kernel, page_len, first_token, pl...  3.97 us
    pallas_call x1, Pallas kernels, outgoing_pages(): pl.pallas_call(functools.partial(outgoing_kernel, pieces), out_shape=out_...  3.49 us
    all_to_all x1, waiting for transfers between devices, shared_local(): lax.all_to_all(outgoing, 'rep', split_axis=0, concat_axis=0, tiled=True)  2.68 us
    unnamed x26, local copies, waits for them, and re-layouts  2.65 us
  transfers between devices with their start and end apart: 15, of which 9 were waited for; matrix products, arithmetic and copies ran while one was open for 0% of the time, Pallas kernels for 14%

profile of v2, /device:TPU:0, one launch (start us, length us, event | category | flops | bytes accessed | tf_op | source)
XLA Modules:
  0.0 92.2 jit_solution(8984282793371212026)
XLA Ops:
  0.0 0.0 copy-start.2
  0.0 0.0 copy-start.3
  0.0 0.0 copy-start.8
  0.0 0.0 copy-start.9
  0.0 3.5 %outgoing_pages.1 = (bf16[16,16,512]{2,1,0:T(8,128)(2,1)}, bf16[64,2048]{1,0:T(8,128)(2,1)}, bf16[64,4096]{1,0:T(8,128)(2,1)}) custom-call(s32[1]{0:T(128)} %bitcast.1.half_ref, s32[6]{0:T(128)} %page_ref.1, s32[6]{0:T(128)} %target_ref.1, bf16[96,16,512]{2,1,0:T(8,128)(2,1)} %pool_ref.1, bf16[2,64,2048]{2,1,0:T(8,128)(2,1)} %bitcast.14, ...), custom_call_target="tpu_custom_call" | custom-call | flops 1024 | bytes 1024 | tf_op jit(solution)/shard_map/outgoing_pages/pallas_call | solution.py:103
  3.5 7.3 %all-to-all-start = ((bf16[16,16,512]{2,1,0:T(8,128)(2,1)}), bf16[16,16,512]{2,1,0:T(8,128)(2,1)S(1)}, u32[]{:S(2)}, u32[]{:S(2)}) async-start(bf16[16,16,512]{2,1,0:T(8,128)(2,1)} %get-tuple-element.27), calls=%async_computation | async-start | bytes 524288 | tf_op jit(solution)/shard_map/all_to_all | solution.py:563
  10.8 0.0 copy-done.2
  10.8 0.0 copy-done.3
  10.8 0.0 copy-done.8
  10.8 0.0 copy-done.9
  10.8 0.0 copy-start.4
  10.8 0.0 copy-start.10
  10.8 0.0 copy-start.11
  10.9 6.2 %attend_pool.1 = (bf16[2048,128]{1,0:T(8,128)(2,1)S(1)}, f32[128,256]{1,0:T(8,128)S(1)}) custom-call(bf16[128,2048]{1,0:T(8,128)(2,1)S(1)} %copy-done.3, bf16[1536,512]{1,0:T(8,128)(2,1)S(1)} %bitcast.16, s32[4,128]{1,0:T(4,128)S(1)} %bitcast.17, s32[1,128]{1,0:T(1,128)S(1)} %bitcast.19), custom_call_target="tpu_custom_call" | custom-call | flops 1000000000 | bytes 1000000 | tf_op jit(solution)/shard_map/attend_pool/pallas_call | solution.py:219
  17.0 2.7 %all-to-all-done.refs_2_ = bf16[16,16,512]{2,1,0:T(8,128)(2,1)S(1)} async-done(((bf16[16,16,512]{2,1,0:T(8,128)(2,1)}), bf16[16,16,512]{2,1,0:T(8,128)(2,1)S(1)}, u32[]{:S(2)}, u32[]{:S(2)}) %all-to-all-start) | async-done | bytes 262176 | tf_op jit(solution)/shard_map/all_to_all | solution.py:563
  19.7 0.0 copy-done.4
  19.7 0.0 copy-start.5
  19.7 0.9 %copy-done.5 = bf16[64,2048]{1,0:T(8,128)(2,1)S(1)} copy-done((bf16[64,2048]{1,0:T(8,128)(2,1)S(1)}, bf16[64,2048]{1,0:T(8,128)(2,1)}, u32[]{:S(2)}) %copy-start.5) | copy-done | bytes 262168
  20.7 0.0 copy-start.6
  20.7 0.7 copy-done.6
  21.4 0.0 copy-start.1
  21.4 1.1 %collective-permute-start.3 = (bf16[64,2048]{1,0:T(8,128)(2,1)}, bf16[64,2048]{1,0:T(8,128)(2,1)S(1)}, u32[]{:S(2)}, u32[]{:S(2)}) collective-permute-start(bf16[64,2048]{1,0:T(8,128)(2,1)} %copy-done.6), channel_id=1, source_target_pairs={{0,8},{2,10},{4,12},{6,14},{8,0},{10,2},{12,4},{14,6},{16,24},{18,... | collective-permute-start | bytes 786440 | tf_op jit(solution)/shard_map/ppermute | solution.py:519
  22.4 1.9 %collective-permute-start.6 = (bf16[64,4096]{1,0:T(8,128)(2,1)S(1)}, bf16[64,4096]{1,0:T(8,128)(2,1)S(1)}, u32[]{:S(2)}, u32[]{:S(2)}) collective-permute-start(bf16[64,4096]{1,0:T(8,128)(2,1)S(1)} %get-tuple-element.37), channel_id=1, source_target_pairs={{0,8},{2,10},{4,12},{6,14},{8,0},{10,2},{12,4},{14,6},{16,24},{18,... | collective-permute-start | bytes 1572872 | tf_op jit(solution)/shard_map/ppermute | solution.py:519
  24.3 0.1 pad_add_fusion.where_ref
  24.4 0.0 copy-done.10
  24.4 0.0 copy-done.11
  24.4 0.0 copy-start.7
  24.4 0.9 copy-done.7
  25.3 4.0 %finish.1 = (s32[1,128]{1,0:T(1,128)S(1)}, bf16[64,2176]{1,0:T(8,128)(2,1)S(1)}, bf16[64,2176]{1,0:T(8,128)(2,1)S(1)}, bf16[64,2176]{1,0:T(8,128)(2,1)S(1)}, bf16[64,2176]{1,0:T(8,128)(2,1)S(1)}) custom-call(s32[2]{0:T(128)S(1)} %pad_add_fusion.where_ref, bf16[128,2048]{1,0:T(8,128)(2,1)S(1)} %copy-done.3, bf16[2048,128]{1,0:T(8,128)(2,1)S(1)} %get-tuple-element.25.part_ref, ...), custom_call_target="tpu_custom_call" | custom-call | flops 1024 | bytes 1024 | tf_op jit(solution)/shard_map/finish/pallas_call | solution.py:337
  29.3 1.5 %collective-permute-start = (bf16[64,2176]{1,0:T(8,128)(2,1)S(1)}, bf16[64,2176]{1,0:T(8,128)(2,1)S(1)}, u32[]{:S(2)}, u32[]{:S(2)}) collective-permute-start(bf16[64,2176]{1,0:T(8,128)(2,1)S(1)} %get-tuple-element.30), channel_id=1, source_target_pairs={{0,2},{2,0},{4,6},{6,4},{8,10},{10,8},{12,14},{14,12},{16,18},{18,... | collective-permute-start | bytes 835592 | tf_op jit(solution)/shard_map/ppermute | solution.py:519
  30.7 0.1 collective-permute-start.1
  30.8 2.0 %collective-permute-start.2 = (bf16[64,2176]{1,0:T(8,128)(2,1)S(1)}, bf16[64,2176]{1,0:T(8,128)(2,1)S(1)}, u32[]{:S(2)}, u32[]{:S(2)}) collective-permute-start(bf16[64,2176]{1,0:T(8,128)(2,1)S(1)} %get-tuple-element.32), channel_id=1, source_target_pairs={{0,6},{2,4},{4,2},{6,0},{8,14},{10,12},{12,10},{14,8},{16,22},{18,... | collective-permute-start | bytes 835592 | tf_op jit(solution)/shard_map/ppermute | solution.py:519
  32.8 13.0 %collective-permute-done.3.refs_5_ = bf16[64,2048]{1,0:T(8,128)(2,1)S(1)} collective-permute-done((bf16[64,2048]{1,0:T(8,128)(2,1)}, bf16[64,2048]{1,0:T(8,128)(2,1)S(1)}, u32[]{:S(2)}, u32[]{:S(2)}) %collective-permute-start.3) | collective-permute-done | bytes 262176 | tf_op jit(solution)/shard_map/ppermute | solution.py:519
  45.9 1.6 %collective-permute-start.4 = (bf16[64,2048]{1,0:T(8,128)(2,1)S(1)}, bf16[64,2048]{1,0:T(8,128)(2,1)S(1)}, u32[]{:S(2)}, u32[]{:S(2)}) collective-permute-start(bf16[64,2048]{1,0:T(8,128)(2,1)S(1)} %after.4), channel_id=1, source_target_pairs={{0,16},{2,18},{4,20},{6,22},{8,24},{10,26},{12,28},{14,30},{16,0},... | collective-permute-start | bytes 786440 | tf_op jit(solution)/shard_map/ppermute | solution.py:519
  47.4 0.0 collective-permute-done.refs_1_
  47.4 0.0 collective-permute-done.1.refs_2_
  47.4 11.2 %collective-permute-done.2.refs_3_ = bf16[64,2176]{1,0:T(8,128)(2,1)S(1)} collective-permute-done((bf16[64,2176]{1,0:T(8,128)(2,1)S(1)}, bf16[64,2176]{1,0:T(8,128)(2,1)S(1)}, u32[]{:S(2)}, u32[]{:S(2)}) %collective-permute-start.2) | collective-permute-done | bytes 278560 | tf_op jit(solution)/shard_map/ppermute | solution.py:519
  58.7 0.0 collective-permute-done.4.refs_6_
  58.7 0.0 copy-done.1
  58.7 0.5 low_products.1.mine_ref.refs_1_
  59.1 0.0 copy-start
  59.1 0.0 collective-permute-done.6.first_ref
  59.2 1.6 %collective-permute-start.7 = (bf16[64,4096]{1,0:T(8,128)(2,1)S(1)}, bf16[64,4096]{1,0:T(8,128)(2,1)S(1)}, u32[]{:S(2)}, u32[]{:S(2)}) collective-permute-start(bf16[64,4096]{1,0:T(8,128)(2,1)S(1)} %after.5), channel_id=1, source_target_pairs={{0,16},{2,18},{4,20},{6,22},{8,24},{10,26},{12,28},{14,30},{16,0},... | collective-permute-start | bytes 1572872 | tf_op jit(solution)/shard_map/ppermute | solution.py:519
  60.8 0.0 collective-permute-start.5
  60.8 1.3 %collective-permute-done.5.other_ref = f32[256,128]{1,0:T(8,128)S(1)} collective-permute-done((f32[256,128]{1,0:T(8,128)S(1)}, f32[256,128]{1,0:T(8,128)S(1)}, u32[]{:S(2)}, u32[]{:S(2)}) %collective-permute-start.5) | collective-permute-done | bytes 131104 | tf_op jit(solution)/shard_map/ppermute | solution.py:590
  62.1 0.0 copy-done
  62.1 1.1 %lift_own.1 = (bf16[32,4096]{1,0:T(8,128)(2,1)S(1)}, bf16[32,4096]{1,0:T(8,128)(2,1)S(1)}, bf16[32,4096]{1,0:T(8,128)(2,1)S(1)}, bf16[32,4096]{1,0:T(8,128)(2,1)S(1)}) custom-call(f32[256,128]{1,0:T(8,128)S(1)} %low_products.1.mine_ref.refs_1_, f32[256,128]{1,0:T(8,128)S(1)} %collective-permute-done.5.other_ref, bf16[128,4096]{1,0:T(8,128)(2,1)S(1)} %bitcast.12), custom_call_target="tpu_custom_call" | custom-call | flops 1024 | bytes 1024 | tf_op jit(solution)/shard_map/lift_own/pallas_call | solution.py:443
  63.2 1.7 %collective-permute-start.8 = (bf16[32,4096]{1,0:T(8,128)(2,1)S(1)}, bf16[32,4096]{1,0:T(8,128)(2,1)S(1)}, u32[]{:S(2)}, u32[]{:S(2)}) collective-permute-start(bf16[32,4096]{1,0:T(8,128)(2,1)S(1)} %get-tuple-element.39), channel_id=1, source_target_pairs={{0,2},{2,0},{4,6},{6,4},{8,10},{10,8},{12,14},{14,12},{16,18},{18,... | collective-permute-start | bytes 786440 | tf_op jit(solution)/shard_map/ppermute | solution.py:519
  65.0 0.0 collective-permute-start.10
  65.0 1.8 %collective-permute-start.12 = (bf16[32,4096]{1,0:T(8,128)(2,1)S(1)}, bf16[32,4096]{1,0:T(8,128)(2,1)S(1)}, u32[]{:S(2)}, u32[]{:S(2)}) collective-permute-start(bf16[32,4096]{1,0:T(8,128)(2,1)S(1)} %get-tuple-element.43), channel_id=1, source_target_pairs={{0,6},{2,4},{4,2},{6,0},{8,14},{10,12},{12,10},{14,8},{16,22},{18,... | collective-permute-start | bytes 786440 | tf_op jit(solution)/shard_map/ppermute | solution.py:519
  66.8 3.9 %collective-permute-done.7.second_ref = bf16[64,4096]{1,0:T(8,128)(2,1)S(1)} collective-permute-done((bf16[64,4096]{1,0:T(8,128)(2,1)S(1)}, bf16[64,4096]{1,0:T(8,128)(2,1)S(1)}, u32[]{:S(2)}, u32[]{:S(2)}) %collective-permute-start.7) | collective-permute-done | bytes 524320 | tf_op jit(solution)/shard_map/ppermute | solution.py:519
  70.7 1.1 %lift_far.1 = (bf16[32,4096]{1,0:T(8,128)(2,1)S(1)}, bf16[32,4096]{1,0:T(8,128)(2,1)S(1)}, bf16[32,4096]{1,0:T(8,128)(2,1)S(1)}, bf16[32,4096]{1,0:T(8,128)(2,1)S(1)}) custom-call(s32[1]{0:T(128)} %bitcast.1.half_ref, f32[256,128]{1,0:T(8,128)S(1)} %low_products.1.mine_ref.refs_1_, f32[256,128]{1,0:T(8,128)S(1)} %collective-permute-done.5.other_ref, ...), custom_call_target="tpu_custom_call" | custom-call | flops 1024 | bytes 1024 | tf_op jit(solution)/shard_map/lift_far/pallas_call | solution.py:474
  71.8 0.7 collective-permute-start.9
  72.5 0.6 collective-permute-start.11
  73.0 0.0 collective-permute-done.8.refs_2_
  73.0 2.3 %collective-permute-start.13 = (bf16[32,4096]{1,0:T(8,128)(2,1)S(1)}, bf16[32,4096]{1,0:T(8,128)(2,1)S(1)}, u32[]{:S(2)}, u32[]{:S(2)}) collective-permute-start(bf16[32,4096]{1,0:T(8,128)(2,1)S(1)} %get-tuple-element.44), channel_id=1, source_target_pairs={{0,6},{2,4},{4,2},{6,0},{8,14},{10,12},{12,10},{14,8},{16,22},{18,... | collective-permute-start | bytes 786440 | tf_op jit(solution)/shard_map/ppermute | solution.py:519
  75.3 0.0 collective-permute-done.10.refs_4_
  75.3 4.3 %collective-permute-done.12.refs_6_ = bf16[32,4096]{1,0:T(8,128)(2,1)S(1)} collective-permute-done((bf16[32,4096]{1,0:T(8,128)(2,1)S(1)}, bf16[32,4096]{1,0:T(8,128)(2,1)S(1)}, u32[]{:S(2)}, u32[]{:S(2)}) %collective-permute-start.12) | collective-permute-done | bytes 262176 | tf_op jit(solution)/shard_map/ppermute | solution.py:519
  79.6 3.3 %collective-permute-done.9.refs_3_ = bf16[32,4096]{1,0:T(8,128)(2,1)S(1)} collective-permute-done((bf16[32,4096]{1,0:T(8,128)(2,1)S(1)}, bf16[32,4096]{1,0:T(8,128)(2,1)S(1)}, u32[]{:S(2)}, u32[]{:S(2)}) %collective-permute-start.9) | collective-permute-done | bytes 262176 | tf_op jit(solution)/shard_map/ppermute | solution.py:519
  82.9 2.5 %collective-permute-done.11.refs_5_ = bf16[32,4096]{1,0:T(8,128)(2,1)S(1)} collective-permute-done((bf16[32,4096]{1,0:T(8,128)(2,1)S(1)}, bf16[32,4096]{1,0:T(8,128)(2,1)S(1)}, u32[]{:S(2)}, u32[]{:S(2)}) %collective-permute-start.11) | collective-permute-done | bytes 262176 | tf_op jit(solution)/shard_map/ppermute | solution.py:519
  85.4 4.3 %collective-permute-done.13.refs_7_ = bf16[32,4096]{1,0:T(8,128)(2,1)S(1)} collective-permute-done((bf16[32,4096]{1,0:T(8,128)(2,1)S(1)}, bf16[32,4096]{1,0:T(8,128)(2,1)S(1)}, u32[]{:S(2)}, u32[]{:S(2)}) %collective-permute-start.13) | collective-permute-done | bytes 262176 | tf_op jit(solution)/shard_map/ppermute | solution.py:519
  89.7 2.4 %gather_rows.1 = bf16[128,4096]{1,0:T(8,128)(2,1)} custom-call(s32[1,128]{1,0:T(1,128)S(1)} %get-tuple-element.28.refs_1_.slot_ref, bf16[32,4096]{1,0:T(8,128)(2,1)S(1)} %get-tuple-element.36.refs_0_, bf16[32,4096]{1,0:T(8,128)(2,1)S(1)} %get-tuple-element.38.refs_1_, bf16[32,4096]{1,0:T(8,128)(2,1)S(1)} %collective-permute-done.8.refs_2_, ...), custom_call_target="tpu_custom_call" | custom-call | flops 1024 | bytes 1024 | tf_op jit(solution)/shard_map/gather_rows/pallas_call | solution.py:499
  (5 shorter events, 0.1 us)
Async XLA Ops:
  0.0 10.8 %copy-start.2 = (bf16[96,16,512]{2,1,0:T(8,128)(2,1)S(1)}, bf16[96,16,512]{2,1,0:T(8,128)(2,1)}, u32[]{:S(2)}) copy-start(bf16[96,16,512]{2,1,0:T(8,128)(2,1)} %pool_ref.1) | copy-start | bytes 4718596
  0.0 10.8 %copy-start.3 = (bf16[128,2048]{1,0:T(8,128)(2,1)S(1)}, bf16[128,2048]{1,0:T(8,128)(2,1)}, u32[]{:S(2)}) copy-start(bf16[128,2048]{1,0:T(8,128)(2,1)} %query_ref.3) | copy-start | bytes 1572868
  0.0 10.8 %copy-start.8 = (s32[128,4]{0,1:T(4,128)S(1)}, s32[128,4]{0,1:T(4,128)}, u32[]{:S(2)}) copy-start(s32[128,4]{0,1:T(4,128)} %param.14) | copy-start | bytes 6148
  0.0 10.8 %copy-start.9 = (s32[128]{0:T(128)S(1)}, s32[128]{0:T(128)}, u32[]{:S(2)}) copy-start(s32[128]{0:T(128)} %param.15) | copy-start | bytes 1540
  3.5 16.2 %all-to-all-start = ((bf16[16,16,512]{2,1,0:T(8,128)(2,1)}), bf16[16,16,512]{2,1,0:T(8,128)(2,1)S(1)}, u32[]{:S(2)}, u32[]{:S(2)}) async-start(bf16[16,16,512]{2,1,0:T(8,128)(2,1)} %get-tuple-element.27), calls=%async_computation | async-start | bytes 524288 | tf_op jit(solution)/shard_map/all_to_all | solution.py:563
  10.8 8.9 %copy-start.4 = (bf16[64,4096]{1,0:T(8,128)(2,1)S(1)}, bf16[64,4096]{1,0:T(8,128)(2,1)}, u32[]{:S(2)}) copy-start(bf16[64,4096]{1,0:T(8,128)(2,1)} %get-tuple-element.34.refs_1_) | copy-start | bytes 1572868
  10.8 13.5 %copy-start.10 = (s32[128,1]{0,1:T(1,128)S(1)}, s32[128,1]{0,1:T(1,128)}, u32[]{:S(2)}) copy-start(s32[128,1]{0,1:T(1,128)} %param.18) | copy-start | bytes 1540
  10.8 13.5 %copy-start.11 = (s32[128]{0:T(128)S(1)}, s32[128]{0:T(128)}, u32[]{:S(2)}) copy-start(s32[128]{0:T(128)} %param.19) | copy-start | bytes 1540
  19.7 1.0 %copy-start.5 = (bf16[64,2048]{1,0:T(8,128)(2,1)S(1)}, bf16[64,2048]{1,0:T(8,128)(2,1)}, u32[]{:S(2)}) copy-start(bf16[64,2048]{1,0:T(8,128)(2,1)} %get-tuple-element.33.refs_0_) | copy-start | bytes 786436
  20.7 0.7 copy-start.6
  21.4 37.3 %copy-start.1 = (bf16[2,2048,64]{1,2,0:T(8,128)(2,1)S(1)}, bf16[2,2048,64]{1,2,0:T(8,128)(2,1)}, u32[]{:S(2)}) copy-start(bf16[2,2048,64]{1,2,0:T(8,128)(2,1)} %param.20) | copy-start | bytes 1572868
  21.4 24.5 %collective-permute-start.3 = (bf16[64,2048]{1,0:T(8,128)(2,1)}, bf16[64,2048]{1,0:T(8,128)(2,1)S(1)}, u32[]{:S(2)}, u32[]{:S(2)}) collective-permute-start(bf16[64,2048]{1,0:T(8,128)(2,1)} %copy-done.6), channel_id=1, source_target_pairs={{0,8},{2,10},{4,12},{6,14},{8,0},{10,2},{12,4},{14,6},{16,24},{18,... | collective-permute-start | bytes 786440 | tf_op jit(solution)/shard_map/ppermute | solution.py:519
  22.4 36.7 %collective-permute-start.6 = (bf16[64,4096]{1,0:T(8,128)(2,1)S(1)}, bf16[64,4096]{1,0:T(8,128)(2,1)S(1)}, u32[]{:S(2)}, u32[]{:S(2)}) collective-permute-start(bf16[64,4096]{1,0:T(8,128)(2,1)S(1)} %get-tuple-element.37), channel_id=1, source_target_pairs={{0,8},{2,10},{4,12},{6,14},{8,0},{10,2},{12,4},{14,6},{16,24},{18,... | collective-permute-start | bytes 1572872 | tf_op jit(solution)/shard_map/ppermute | solution.py:519
  24.4 0.9 copy-start.7
  29.3 18.2 %collective-permute-start = (bf16[64,2176]{1,0:T(8,128)(2,1)S(1)}, bf16[64,2176]{1,0:T(8,128)(2,1)S(1)}, u32[]{:S(2)}, u32[]{:S(2)}) collective-permute-start(bf16[64,2176]{1,0:T(8,128)(2,1)S(1)} %get-tuple-element.30), channel_id=1, source_target_pairs={{0,2},{2,0},{4,6},{6,4},{8,10},{10,8},{12,14},{14,12},{16,18},{18,... | collective-permute-start | bytes 835592 | tf_op jit(solution)/shard_map/ppermute | solution.py:519
  30.7 16.7 %collective-permute-start.1 = (bf16[64,2176]{1,0:T(8,128)(2,1)S(1)}, bf16[64,2176]{1,0:T(8,128)(2,1)S(1)}, u32[]{:S(2)}, u32[]{:S(2)}) collective-permute-start(bf16[64,2176]{1,0:T(8,128)(2,1)S(1)} %get-tuple-element.31), channel_id=1, source_target_pairs={{0,4},{2,6},{4,0},{6,2},{8,12},{10,14},{12,8},{14,10},{16,20},{18,... | collective-permute-start | bytes 835592 | tf_op jit(solution)/shard_map/ppermute | solution.py:519
  30.8 27.9 %collective-permute-start.2 = (bf16[64,2176]{1,0:T(8,128)(2,1)S(1)}, bf16[64,2176]{1,0:T(8,128)(2,1)S(1)}, u32[]{:S(2)}, u32[]{:S(2)}) collective-permute-start(bf16[64,2176]{1,0:T(8,128)(2,1)S(1)} %get-tuple-element.32), channel_id=1, source_target_pairs={{0,6},{2,4},{4,2},{6,0},{8,14},{10,12},{12,10},{14,8},{16,22},{18,... | collective-permute-start | bytes 835592 | tf_op jit(solution)/shard_map/ppermute | solution.py:519
  45.9 12.8 %collective-permute-start.4 = (bf16[64,2048]{1,0:T(8,128)(2,1)S(1)}, bf16[64,2048]{1,0:T(8,128)(2,1)S(1)}, u32[]{:S(2)}, u32[]{:S(2)}) collective-permute-start(bf16[64,2048]{1,0:T(8,128)(2,1)S(1)} %after.4), channel_id=1, source_target_pairs={{0,16},{2,18},{4,20},{6,22},{8,24},{10,26},{12,28},{14,30},{16,0},... | collective-permute-start | bytes 786440 | tf_op jit(solution)/shard_map/ppermute | solution.py:519
  59.1 3.0 %copy-start = (bf16[2,64,4096]{2,1,0:T(8,128)(2,1)S(1)}, bf16[2,64,4096]{2,1,0:T(8,128)(2,1)}, u32[]{:S(2)}) copy-start(bf16[2,64,4096]{2,1,0:T(8,128)(2,1)} %refs_1_.1) | copy-start | bytes 3145732
  59.2 11.5 %collective-permute-start.7 = (bf16[64,4096]{1,0:T(8,128)(2,1)S(1)}, bf16[64,4096]{1,0:T(8,128)(2,1)S(1)}, u32[]{:S(2)}, u32[]{:S(2)}) collective-permute-start(bf16[64,4096]{1,0:T(8,128)(2,1)S(1)} %after.5), channel_id=1, source_target_pairs={{0,16},{2,18},{4,20},{6,22},{8,24},{10,26},{12,28},{14,30},{16,0},... | collective-permute-start | bytes 1572872 | tf_op jit(solution)/shard_map/ppermute | solution.py:519
  60.8 1.3 %collective-permute-start.5 = (f32[256,128]{1,0:T(8,128)S(1)}, f32[256,128]{1,0:T(8,128)S(1)}, u32[]{:S(2)}, u32[]{:S(2)}) collective-permute-start(f32[256,128]{1,0:T(8,128)S(1)} %low_products.1.mine_ref.refs_1_), channel_id=1, source_target_pairs={{0,1},{1,0},{2,3},{3,2},{4,5},{5,4},{6,7},{7,6},{8,9},{9,8},{10,11... | collective-permute-start | bytes 393224 | tf_op jit(solution)/shard_map/ppermute | solution.py:590
  63.2 9.8 %collective-permute-start.8 = (bf16[32,4096]{1,0:T(8,128)(2,1)S(1)}, bf16[32,4096]{1,0:T(8,128)(2,1)S(1)}, u32[]{:S(2)}, u32[]{:S(2)}) collective-permute-start(bf16[32,4096]{1,0:T(8,128)(2,1)S(1)} %get-tuple-element.39), channel_id=1, source_target_pairs={{0,2},{2,0},{4,6},{6,4},{8,10},{10,8},{12,14},{14,12},{16,18},{18,... | collective-permute-start | bytes 786440 | tf_op jit(solution)/shard_map/ppermute | solution.py:519
  65.0 10.4 %collective-permute-start.10 = (bf16[32,4096]{1,0:T(8,128)(2,1)S(1)}, bf16[32,4096]{1,0:T(8,128)(2,1)S(1)}, u32[]{:S(2)}, u32[]{:S(2)}) collective-permute-start(bf16[32,4096]{1,0:T(8,128)(2,1)S(1)} %get-tuple-element.41), channel_id=1, source_target_pairs={{0,4},{2,6},{4,0},{6,2},{8,12},{10,14},{12,8},{14,10},{16,20},{18,... | collective-permute-start | bytes 786440 | tf_op jit(solution)/shard_map/ppermute | solution.py:519
  65.0 14.6 %collective-permute-start.12 = (bf16[32,4096]{1,0:T(8,128)(2,1)S(1)}, bf16[32,4096]{1,0:T(8,128)(2,1)S(1)}, u32[]{:S(2)}, u32[]{:S(2)}) collective-permute-start(bf16[32,4096]{1,0:T(8,128)(2,1)S(1)} %get-tuple-element.43), channel_id=1, source_target_pairs={{0,6},{2,4},{4,2},{6,0},{8,14},{10,12},{12,10},{14,8},{16,22},{18,... | collective-permute-start | bytes 786440 | tf_op jit(solution)/shard_map/ppermute | solution.py:519
  71.8 11.1 %collective-permute-start.9 = (bf16[32,4096]{1,0:T(8,128)(2,1)S(1)}, bf16[32,4096]{1,0:T(8,128)(2,1)S(1)}, u32[]{:S(2)}, u32[]{:S(2)}) collective-permute-start(bf16[32,4096]{1,0:T(8,128)(2,1)S(1)} %get-tuple-element.40), channel_id=1, source_target_pairs={{0,2},{2,0},{4,6},{6,4},{8,10},{10,8},{12,14},{14,12},{16,18},{18,... | collective-permute-start | bytes 786440 | tf_op jit(solution)/shard_map/ppermute | solution.py:519
  72.5 13.0 %collective-permute-start.11 = (bf16[32,4096]{1,0:T(8,128)(2,1)S(1)}, bf16[32,4096]{1,0:T(8,128)(2,1)S(1)}, u32[]{:S(2)}, u32[]{:S(2)}) collective-permute-start(bf16[32,4096]{1,0:T(8,128)(2,1)S(1)} %get-tuple-element.42), channel_id=1, source_target_pairs={{0,4},{2,6},{4,0},{6,2},{8,12},{10,14},{12,8},{14,10},{16,20},{18,... | collective-permute-start | bytes 786440 | tf_op jit(solution)/shard_map/ppermute | solution.py:519
  73.0 16.7 %collective-permute-start.13 = (bf16[32,4096]{1,0:T(8,128)(2,1)S(1)}, bf16[32,4096]{1,0:T(8,128)(2,1)S(1)}, u32[]{:S(2)}, u32[]{:S(2)}) collective-permute-start(bf16[32,4096]{1,0:T(8,128)(2,1)S(1)} %get-tuple-element.44), channel_id=1, source_target_pairs={{0,6},{2,4},{4,2},{6,0},{8,14},{10,12},{12,10},{14,8},{16,22},{18,... | collective-permute-start | bytes 786440 | tf_op jit(solution)/shard_map/ppermute | solution.py:519

commit v3 on v2

--- a/solution.py
+++ b/solution.py
@@ -452,35 +452,40 @@
     )(mine, other, weights)
 
 
-def lift_far_kernel(half_ref, mine_ref, other_ref, first_ref, second_ref, *out_refs):
+def lift_far_kernel(half_ref, mine_ref, other_ref, *refs):
+    number = (len(refs) - 4) // 2
+    first_refs, second_refs, out_refs = refs[:number], refs[number : 2 * number], refs[2 * number :]
     low = (mine_ref[...] + other_ref[...]).astype(jnp.bfloat16)
     swapped = half_ref[0] == 1
     cap = out_refs[0].shape[0]
-    zero = jnp.where(swapped, second_ref[...], first_ref[...])
-    one = jnp.where(swapped, first_ref[...], second_ref[...])
-    lifted = jnp.dot(
-        low, jnp.concatenate([zero, one], axis=0), preferred_element_type=jnp.float32
-    ).astype(jnp.bfloat16)
-    for b, out_ref in enumerate(out_refs):
-        out_ref[...] = lifted[b * cap : (b + 1) * cap]
+    place = 0
+    for first_ref, second_ref in zip(first_refs, second_refs):
+        columns = slice(place, place + first_ref.shape[1])
+        zero = jnp.where(swapped, second_ref[...], first_ref[...])
+        one = jnp.where(swapped, first_ref[...], second_ref[...])
+        lifted = jnp.dot(
+            low, jnp.concatenate([zero, one], axis=0), preferred_element_type=jnp.float32
+        ).astype(jnp.bfloat16)
+        for b, out_ref in enumerate(out_refs):
+            out_ref[:, columns] = lifted[b * cap : (b + 1) * cap]
+        place = columns.stop
 
 
 def lift_far(half, mine, other, first, second):
     rows, rank = mine.shape
-    width = first.shape[1]
-    step = 1024
+    width = sum(piece.shape[1] for piece in first)
     low = pl.BlockSpec((rows // 2, rank), lambda j: (1, 0))
     out = jax.ShapeDtypeStruct((rows // 8, width), jnp.bfloat16)
     return pl.pallas_call(
         lift_far_kernel,
-        grid=(width // step,),
+        grid=(1,),
         out_shape=(out,) * 4,
-        in_specs=[smem_spec(), low, low] + [pl.BlockSpec((rank // 2, step), lambda j: (0, j))] * 2,
-        out_specs=[pl.BlockSpec((rows // 8, step), lambda j: (0, j))] * 4,
+        in_specs=[smem_spec(), low, low] + [whole(piece) for piece in (*first, *second)],
+        out_specs=[whole(out)] * 4,
         compiler_params=params(),
         cost_estimate=cost(),
         name="lift_far",
-    )(half, mine, other, first, second)
+    )(half, mine, other, *first, *second)
 
 
 def gather_rows_kernel(slot_ref, *refs):
@@ -495,7 +500,7 @@
 def gather_rows(slots, blocks):
     rows = slots.shape[1]
     width = blocks[0].shape[1]
-    step = 1024
+    step = 2048
     return pl.pallas_call(
         gather_rows_kernel,
         grid=(width // step,),
@@ -549,6 +554,7 @@
     pool = key_value_pool.reshape(pages * page_len, features)
 
     columns = up.shape[1]
+    early = columns // 8 * 4
     rank = up.shape[0] // 2
     outgoing, *packs = outgoing_pages(
         half,
@@ -557,16 +563,17 @@
         key_value_pool,
         replicas,
         (down_rows, adapter_up_weight),
-        (((0, width, 0, 0),), ((0, columns, 1, 0),)),
-        ((rank, width), (rank, columns)),
+        (((0, width, 0, 0),), ((0, early, 1, 0), (early, columns, 2, 0))),
+        ((rank, width), (rank, early), (rank, columns - early)),
     )
     arrived = lax.all_to_all(outgoing, "rep", split_axis=0, concat_axis=0, tiled=True)
     found = attend_pool(queries, pool, entries, lengths, page_len)
-    first = [along(pack, 0, 4) for pack in after(packs, arrived, found[1])]
+    first = [along(pack, 0, 6) for pack in after(packs[:2], arrived, found[1])]
 
     def place(targets, replica):
         apart = jnp.bitwise_xor(targets, replica)
-        return (2 * jnp.bitwise_and(apart, 3) + jnp.right_shift(apart, 2)) * cap
+        far = jnp.right_shift(apart, 2)
+        return (2 * jnp.bitwise_xor(jnp.bitwise_and(apart, 3), 2 * far) + far) * cap
 
     slots, here, *outbound = finish(
         where,
@@ -583,14 +590,16 @@
         (2 * cap,) * 4,
         place,
     )
-    blocks = [here] + [along(block, 0, b + 1) for b, block in enumerate(outbound)]
-    second = [along(*after([first[0]], slots), 1, 0)]
+    blocks = [along(block, 0, 3 - b) for b, block in enumerate(outbound[::-1])]
+    blocks = [here] + blocks[::-1]
+    first.append(along(*after([packs[2]], blocks[3]), 0, 6))
+    second = [along(*after([first[0]], slots), 1, 0), along(*after([first[1]], blocks[1]), 1, 0)]
     mine = low_products(half, blocks, down, first[0], second[0])
-    second.append(along(*after([first[1]], mine), 1, 0))
     other = lax.ppermute(mine, "tp", [(0, 1), (1, 0)])
+    second.append(along(*after([first[2]], other), 1, 0))
     own = lift_own(mine, other, up)
     own = [block if b == 0 else along(block, 0, b) for b, block in enumerate(own)]
-    far = lift_far(half, mine, other, first[1], second[1])
+    far = lift_far(half, mine, other, first[1:], second[1:])
     far = [block if b == 0 else along(block, 0, b) for b, block in enumerate(far)]
     return gather_rows(slots, [block for pair in zip(own, far) for block in pair])
 

time: 92.5 us -> 84.8 us (0.917)
  waiting for transfers between devices: 46.6 us -> 33.7 us
  starting transfers between devices: 24 us -> 32.2 us
  local copies, waits for them, and re-layouts: 2.65 us -> 1.01 us
  Pallas kernels: 18.7 us -> 17.3 us
    ppermute x13 -> x15, waiting for transfers between devices: 42.5 us -> 31.1 us  [along(): return lax.ppermute(array, ('group', 'rep'), pairs)]
    ppermute x13 -> x15, starting transfers between devices: 16.7 us -> 24.9 us  [along(): return lax.ppermute(array, ('group', 'rep'), pairs)]
    unnamed x26 -> x27, local copies, waits for them, and re-layouts: 2.65 us -> 1.01 us
    ppermute x1, waiting for transfers between devices: 1.35 us -> 0.01 us  [shared_local(): other = lax.ppermute(mine, 'tp', [(0, 1), (1, 0)])]
  transfers between devices with their start and end apart: 15 -> 17, of which waited for: 9 -> 8; matrix products, arithmetic and copies ran while one was open for 0% -> 0% of each run, Pallas kernels for 14% -> 14%
where the time goes in v3:
time: 84.8 us; the launch traced here: 84.5 us
  waiting for transfers between devices  33.7 us (40%)
  starting transfers between devices  32.2 us (38%)
  Pallas kernels  17.3 us (20%)
  local copies, waits for them, and re-layouts  1.01 us (1%)
    ppermute x15, waiting for transfers between devices, along(): return lax.ppermute(array, ('group', 'rep'), pairs)  31.1 us
    ppermute x15, starting transfers between devices, along(): return lax.ppermute(array, ('group', 'rep'), pairs)  24.9 us
    all_to_all x1, starting transfers between devices, shared_local(): lax.all_to_all(outgoing, 'rep', split_axis=0, concat_axis=0, tiled=True)  7.29 us
    pallas_call x1, Pallas kernels, attend_pool(): pl.pallas_call(functools.partial(pool_kernel, page_len), grid=(kv_local,)...  6.15 us
    pallas_call x1, Pallas kernels, finish(): pl.pallas_call(functools.partial(finish_kernel, page_len, first_token, pl...  3.96 us
    pallas_call x1, Pallas kernels, outgoing_pages(): pl.pallas_call(functools.partial(outgoing_kernel, pieces), out_shape=out_...  3.48 us
    all_to_all x1, waiting for transfers between devices, shared_local(): lax.all_to_all(outgoing, 'rep', split_axis=0, concat_axis=0, tiled=True)  2.68 us
    pallas_call x1, Pallas kernels, gather_rows(): pl.pallas_call(gather_rows_kernel, grid=(width // step,), out_shape=jax.S...  1.72 us
  transfers between devices with their start and end apart: 17, of which 8 were waited for; matrix products, arithmetic and copies ran while one was open for 0% of the time, Pallas kernels for 14%

profile of v3, /device:TPU:0, one launch (start us, length us, event | category | flops | bytes accessed | tf_op | source)
XLA Modules:
  0.0 84.5 jit_solution(4577622730543789767)
XLA Ops:
  0.0 0.0 copy-start.2
  0.0 0.0 copy-start.3
  0.0 0.0 copy-start.8
  0.0 0.0 copy-start.9
  0.0 3.5 %outgoing_pages.1 = (bf16[16,16,512]{2,1,0:T(8,128)(2,1)}, bf16[64,2048]{1,0:T(8,128)(2,1)}, bf16[64,2048]{1,0:T(8,128)(2,1)}, bf16[64,2048]{1,0:T(8,128)(2,1)}) custom-call(s32[1]{0:T(128)} %bitcast.1.half_ref, s32[6]{0:T(128)} %page_ref.1, s32[6]{0:T(128)} %target_ref.1, bf16[96,16,512]{2,1,0:T(8,128)(2,1)} %pool_ref.1, bf16[2,64,2048]{2,1,0:T(8,128)(2,1)} %bitcast.14, ...), custom_call_target="tpu_custom_call" | custom-call | flops 1024 | bytes 1024 | tf_op jit(solution)/shard_map/outgoing_pages/pallas_call | solution.py:103
  3.5 7.3 %all-to-all-start = ((bf16[16,16,512]{2,1,0:T(8,128)(2,1)}), bf16[16,16,512]{2,1,0:T(8,128)(2,1)S(1)}, u32[]{:S(2)}, u32[]{:S(2)}) async-start(bf16[16,16,512]{2,1,0:T(8,128)(2,1)} %get-tuple-element.28), calls=%async_computation | async-start | bytes 524288 | tf_op jit(solution)/shard_map/all_to_all | solution.py:569
  10.8 0.0 copy-done.2
  10.8 0.0 copy-done.3
  10.8 0.0 copy-done.8
  10.8 0.0 copy-done.9
  10.8 0.0 copy-start.5
  10.8 0.0 copy-start.6
  10.8 0.0 copy-start.10
  10.9 0.0 copy-start.11
  10.9 6.2 %attend_pool.1 = (bf16[2048,128]{1,0:T(8,128)(2,1)S(1)}, f32[128,256]{1,0:T(8,128)S(1)}) custom-call(bf16[128,2048]{1,0:T(8,128)(2,1)S(1)} %copy-done.3, bf16[1536,512]{1,0:T(8,128)(2,1)S(1)} %bitcast.16, s32[4,128]{1,0:T(4,128)S(1)} %bitcast.17, s32[1,128]{1,0:T(1,128)S(1)} %bitcast.19), custom_call_target="tpu_custom_call" | custom-call | flops 1000000000 | bytes 1000000 | tf_op jit(solution)/shard_map/attend_pool/pallas_call | solution.py:219
  17.0 2.7 %all-to-all-done.refs_2_ = bf16[16,16,512]{2,1,0:T(8,128)(2,1)S(1)} async-done(((bf16[16,16,512]{2,1,0:T(8,128)(2,1)}), bf16[16,16,512]{2,1,0:T(8,128)(2,1)S(1)}, u32[]{:S(2)}, u32[]{:S(2)}) %all-to-all-start) | async-done | bytes 262176 | tf_op jit(solution)/shard_map/all_to_all | solution.py:569
  19.7 0.0 copy-done.5
  19.7 0.0 copy-done.6
  19.7 0.0 copy-start.4
  19.7 1.2 %collective-permute-start.3 = (bf16[64,2048]{1,0:T(8,128)(2,1)S(1)}, bf16[64,2048]{1,0:T(8,128)(2,1)S(1)}, u32[]{:S(2)}, u32[]{:S(2)}) collective-permute-start(bf16[64,2048]{1,0:T(8,128)(2,1)S(1)} %get-tuple-element.36), channel_id=1, source_target_pairs={{0,12},{2,14},{4,8},{6,10},{8,4},{10,6},{12,0},{14,2},{16,28},{18,... | collective-permute-start | bytes 786440 | tf_op jit(solution)/shard_map/ppermute | solution.py:524
  21.0 0.1 pad_add_fusion.where_ref
  21.0 0.0 copy-done.10
  21.0 0.0 copy-done.11
  21.0 0.9 %copy-done.7 = bf16[128,512]{1,0:T(8,128)(2,1)S(1)} copy-done((bf16[128,512]{1,0:T(8,128)(2,1)S(1)}, bf16[128,512]{1,0:T(8,128)(2,1)}, u32[]{:S(2)}) %copy-start.7) | copy-done | bytes 131096
  21.9 4.0 %finish.1 = (s32[1,128]{1,0:T(1,128)S(1)}, bf16[64,2176]{1,0:T(8,128)(2,1)S(1)}, bf16[64,2176]{1,0:T(8,128)(2,1)S(1)}, bf16[64,2176]{1,0:T(8,128)(2,1)S(1)}, bf16[64,2176]{1,0:T(8,128)(2,1)S(1)}) custom-call(s32[2]{0:T(128)S(1)} %pad_add_fusion.where_ref, bf16[128,2048]{1,0:T(8,128)(2,1)S(1)} %copy-done.3, bf16[2048,128]{1,0:T(8,128)(2,1)S(1)} %get-tuple-element.26.part_ref, ...), custom_call_target="tpu_custom_call" | custom-call | flops 1024 | bytes 1024 | tf_op jit(solution)/shard_map/finish/pallas_call | solution.py:337
  25.9 0.6 collective-permute-start.2
  26.6 1.4 %collective-permute-start = (bf16[64,2176]{1,0:T(8,128)(2,1)S(1)}, bf16[64,2176]{1,0:T(8,128)(2,1)S(1)}, u32[]{:S(2)}, u32[]{:S(2)}) collective-permute-start(bf16[64,2176]{1,0:T(8,128)(2,1)S(1)} %get-tuple-element.31), channel_id=1, source_target_pairs={{0,2},{2,0},{4,6},{6,4},{8,10},{10,8},{12,14},{14,12},{16,18},{18,... | collective-permute-start | bytes 835592 | tf_op jit(solution)/shard_map/ppermute | solution.py:524
  27.9 1.6 %collective-permute-start.1 = (bf16[64,2176]{1,0:T(8,128)(2,1)S(1)}, bf16[64,2176]{1,0:T(8,128)(2,1)S(1)}, u32[]{:S(2)}, u32[]{:S(2)}) collective-permute-start(bf16[64,2176]{1,0:T(8,128)(2,1)S(1)} %get-tuple-element.32), channel_id=1, source_target_pairs={{0,4},{2,6},{4,0},{6,2},{8,12},{10,14},{12,8},{14,10},{16,20},{18,... | collective-permute-start | bytes 835592 | tf_op jit(solution)/shard_map/ppermute | solution.py:524
  29.5 0.0 collective-permute-done.3.refs_5_
  29.5 1.6 %collective-permute-start.4 = (bf16[64,2048]{1,0:T(8,128)(2,1)S(1)}, bf16[64,2048]{1,0:T(8,128)(2,1)S(1)}, u32[]{:S(2)}, u32[]{:S(2)}) collective-permute-start(bf16[64,2048]{1,0:T(8,128)(2,1)S(1)} %after.6), channel_id=1, source_target_pairs={{0,16},{2,18},{4,20},{6,22},{8,24},{10,26},{12,28},{14,30},{16,0},... | collective-permute-start | bytes 786440 | tf_op jit(solution)/shard_map/ppermute | solution.py:524
  31.1 2.6 %collective-permute-start.6 = (bf16[64,2048]{1,0:T(8,128)(2,1)S(1)}, bf16[64,2048]{1,0:T(8,128)(2,1)S(1)}, u32[]{:S(2)}, u32[]{:S(2)}) collective-permute-start(bf16[64,2048]{1,0:T(8,128)(2,1)S(1)} %get-tuple-element.38), channel_id=1, source_target_pairs={{0,12},{2,14},{4,8},{6,10},{8,4},{10,6},{12,0},{14,2},{16,28},{18,... | collective-permute-start | bytes 786440 | tf_op jit(solution)/shard_map/ppermute | solution.py:524
  33.7 2.8 %collective-permute-done.2.refs_3_.refs_1_ = bf16[64,2176]{1,0:T(8,128)(2,1)S(1)} collective-permute-done((bf16[64,2176]{1,0:T(8,128)(2,1)S(1)}, bf16[64,2176]{1,0:T(8,128)(2,1)S(1)}, u32[]{:S(2)}, u32[]{:S(2)}) %collective-permute-start.2) | collective-permute-done | bytes 278560 | tf_op jit(solution)/shard_map/ppermute | solution.py:524
  36.5 0.0 copy-done.4
  36.5 2.7 %collective-permute-start.7 = (bf16[64,2048]{1,0:T(8,128)(2,1)S(1)}, bf16[64,2048]{1,0:T(8,128)(2,1)S(1)}, u32[]{:S(2)}, u32[]{:S(2)}) collective-permute-start(bf16[64,2048]{1,0:T(8,128)(2,1)S(1)} %after.7), channel_id=1, source_target_pairs={{0,12},{2,14},{4,8},{6,10},{8,4},{10,6},{12,0},{14,2},{16,28},{18,... | collective-permute-start | bytes 786440 | tf_op jit(solution)/shard_map/ppermute | solution.py:524
  39.2 0.6 collective-permute-done.refs_1_
  39.8 12.4 %collective-permute-done.1.refs_2_ = bf16[64,2176]{1,0:T(8,128)(2,1)S(1)} collective-permute-done((bf16[64,2176]{1,0:T(8,128)(2,1)S(1)}, bf16[64,2176]{1,0:T(8,128)(2,1)S(1)}, u32[]{:S(2)}, u32[]{:S(2)}) %collective-permute-start.1) | collective-permute-done | bytes 278560 | tf_op jit(solution)/shard_map/ppermute | solution.py:524
  52.1 0.0 collective-permute-done.4.refs_6_
  52.2 0.0 copy-done.1
  52.2 0.5 low_products.1.mine_ref
  52.6 0.0 copy-start
  52.6 0.1 collective-permute-start.5
  52.7 0.0 collective-permute-done.6.refs_0_
  52.8 1.6 %collective-permute-start.8 = (bf16[64,2048]{1,0:T(8,128)(2,1)S(1)}, bf16[64,2048]{1,0:T(8,128)(2,1)S(1)}, u32[]{:S(2)}, u32[]{:S(2)}) collective-permute-start(bf16[64,2048]{1,0:T(8,128)(2,1)S(1)} %after.8), channel_id=1, source_target_pairs={{0,16},{2,18},{4,20},{6,22},{8,24},{10,26},{12,28},{14,30},{16,0},... | collective-permute-start | bytes 786440 | tf_op jit(solution)/shard_map/ppermute | solution.py:524
  54.3 0.0 collective-permute-done.7.refs_1_
  54.4 0.0 collective-permute-done.5.other_ref.refs_1_
  54.4 1.2 %collective-permute-start.9 = (bf16[64,2048]{1,0:T(8,128)(2,1)S(1)}, bf16[64,2048]{1,0:T(8,128)(2,1)S(1)}, u32[]{:S(2)}, u32[]{:S(2)}) collective-permute-start(bf16[64,2048]{1,0:T(8,128)(2,1)S(1)} %after.9), channel_id=1, source_target_pairs={{0,16},{2,18},{4,20},{6,22},{8,24},{10,26},{12,28},{14,30},{16,0},... | collective-permute-start | bytes 786440 | tf_op jit(solution)/shard_map/ppermute | solution.py:524
  55.5 0.0 copy-done
  55.6 1.1 %lift_own.1 = (bf16[32,4096]{1,0:T(8,128)(2,1)S(1)}, bf16[32,4096]{1,0:T(8,128)(2,1)S(1)}, bf16[32,4096]{1,0:T(8,128)(2,1)S(1)}, bf16[32,4096]{1,0:T(8,128)(2,1)S(1)}) custom-call(f32[256,128]{1,0:T(8,128)S(1)} %low_products.1.mine_ref, f32[256,128]{1,0:T(8,128)S(1)} %collective-permute-done.5.other_ref.refs_1_, bf16[128,4096]{1,0:T(8,128)(2,1)S(1)} %bitcast.12), custom_call_target="tpu_custom_call" | custom-call | flops 1024 | bytes 1024 | tf_op jit(solution)/shard_map/lift_own/pallas_call | solution.py:443
  56.6 0.7 collective-permute-start.10
  57.3 3.2 %collective-permute-start.12 = (bf16[32,4096]{1,0:T(8,128)(2,1)S(1)}, bf16[32,4096]{1,0:T(8,128)(2,1)S(1)}, u32[]{:S(2)}, u32[]{:S(2)}) collective-permute-start(bf16[32,4096]{1,0:T(8,128)(2,1)S(1)} %get-tuple-element.43), channel_id=1, source_target_pairs={{0,4},{2,6},{4,0},{6,2},{8,12},{10,14},{12,8},{14,10},{16,20},{18,... | collective-permute-start | bytes 786440 | tf_op jit(solution)/shard_map/ppermute | solution.py:524
  60.4 0.9 %collective-permute-start.14 = (bf16[32,4096]{1,0:T(8,128)(2,1)S(1)}, bf16[32,4096]{1,0:T(8,128)(2,1)S(1)}, u32[]{:S(2)}, u32[]{:S(2)}) collective-permute-start(bf16[32,4096]{1,0:T(8,128)(2,1)S(1)} %get-tuple-element.45), channel_id=1, source_target_pairs={{0,6},{2,4},{4,2},{6,0},{8,14},{10,12},{12,10},{14,8},{16,22},{18,... | collective-permute-start | bytes 786440 | tf_op jit(solution)/shard_map/ppermute | solution.py:524
  61.3 0.6 collective-permute-done.8.refs_2_
  61.9 5.2 %collective-permute-done.9.refs_3_ = bf16[64,2048]{1,0:T(8,128)(2,1)S(1)} collective-permute-done((bf16[64,2048]{1,0:T(8,128)(2,1)S(1)}, bf16[64,2048]{1,0:T(8,128)(2,1)S(1)}, u32[]{:S(2)}, u32[]{:S(2)}) %collective-permute-start.9) | collective-permute-done | bytes 262176 | tf_op jit(solution)/shard_map/ppermute | solution.py:524
  67.1 0.4 lift_far.1
  67.6 0.7 collective-permute-start.11
  68.2 0.0 collective-permute-start.13
  68.2 0.0 collective-permute-done.10.refs_2_
  68.2 5.1 %collective-permute-start.15 = (bf16[32,4096]{1,0:T(8,128)(2,1)S(1)}, bf16[32,4096]{1,0:T(8,128)(2,1)S(1)}, u32[]{:S(2)}, u32[]{:S(2)}) collective-permute-start(bf16[32,4096]{1,0:T(8,128)(2,1)S(1)} %get-tuple-element.46), channel_id=1, source_target_pairs={{0,6},{2,4},{4,2},{6,0},{8,14},{10,12},{12,10},{14,8},{16,22},{18,... | collective-permute-start | bytes 786440 | tf_op jit(solution)/shard_map/ppermute | solution.py:524
  73.3 0.0 collective-permute-done.12.refs_4_
  73.3 0.0 collective-permute-done.14.refs_6_
  73.3 5.0 %collective-permute-done.11.refs_3_ = bf16[32,4096]{1,0:T(8,128)(2,1)S(1)} collective-permute-done((bf16[32,4096]{1,0:T(8,128)(2,1)S(1)}, bf16[32,4096]{1,0:T(8,128)(2,1)S(1)}, u32[]{:S(2)}, u32[]{:S(2)}) %collective-permute-start.11) | collective-permute-done | bytes 262176 | tf_op jit(solution)/shard_map/ppermute | solution.py:524
  78.3 0.0 collective-permute-done.13.refs_5_
  78.3 4.5 %collective-permute-done.15.refs_7_ = bf16[32,4096]{1,0:T(8,128)(2,1)S(1)} collective-permute-done((bf16[32,4096]{1,0:T(8,128)(2,1)S(1)}, bf16[32,4096]{1,0:T(8,128)(2,1)S(1)}, u32[]{:S(2)}, u32[]{:S(2)}) %collective-permute-start.15) | collective-permute-done | bytes 262176 | tf_op jit(solution)/shard_map/ppermute | solution.py:524
  82.8 1.7 %gather_rows.1 = bf16[128,4096]{1,0:T(8,128)(2,1)} custom-call(s32[1,128]{1,0:T(1,128)S(1)} %get-tuple-element.29.refs_1_.slot_ref, bf16[32,4096]{1,0:T(8,128)(2,1)S(1)} %get-tuple-element.37.refs_0_, bf16[32,4096]{1,0:T(8,128)(2,1)S(1)} %get-tuple-element.40.refs_1_, bf16[32,4096]{1,0:T(8,128)(2,1)S(1)} %collective-permute-done.10.refs_2_, ...), custom_call_target="tpu_custom_call" | custom-call | flops 1024 | bytes 1024 | tf_op jit(solution)/shard_map/gather_rows/pallas_call | solution.py:504
  (10 shorter events, 0.1 us)
Async XLA Ops:
  0.0 10.8 %copy-start.2 = (bf16[96,16,512]{2,1,0:T(8,128)(2,1)S(1)}, bf16[96,16,512]{2,1,0:T(8,128)(2,1)}, u32[]{:S(2)}) copy-start(bf16[96,16,512]{2,1,0:T(8,128)(2,1)} %pool_ref.1) | copy-start | bytes 4718596
  0.0 10.8 %copy-start.3 = (bf16[128,2048]{1,0:T(8,128)(2,1)S(1)}, bf16[128,2048]{1,0:T(8,128)(2,1)}, u32[]{:S(2)}) copy-start(bf16[128,2048]{1,0:T(8,128)(2,1)} %query_ref.3) | copy-start | bytes 1572868
  0.0 10.8 %copy-start.8 = (s32[128,4]{0,1:T(4,128)S(1)}, s32[128,4]{0,1:T(4,128)}, u32[]{:S(2)}) copy-start(s32[128,4]{0,1:T(4,128)} %param.14) | copy-start | bytes 6148
  0.0 10.8 %copy-start.9 = (s32[128]{0:T(128)S(1)}, s32[128]{0:T(128)}, u32[]{:S(2)}) copy-start(s32[128]{0:T(128)} %param.15) | copy-start | bytes 1540
  3.5 16.2 %all-to-all-start = ((bf16[16,16,512]{2,1,0:T(8,128)(2,1)}), bf16[16,16,512]{2,1,0:T(8,128)(2,1)S(1)}, u32[]{:S(2)}, u32[]{:S(2)}) async-start(bf16[16,16,512]{2,1,0:T(8,128)(2,1)} %get-tuple-element.28), calls=%async_computation | async-start | bytes 524288 | tf_op jit(solution)/shard_map/all_to_all | solution.py:569
  10.8 8.9 %copy-start.5 = (bf16[64,2048]{1,0:T(8,128)(2,1)S(1)}, bf16[64,2048]{1,0:T(8,128)(2,1)}, u32[]{:S(2)}) copy-start(bf16[64,2048]{1,0:T(8,128)(2,1)} %get-tuple-element.34.refs_0_) | copy-start | bytes 786436
  10.8 8.9 %copy-start.6 = (bf16[64,2048]{1,0:T(8,128)(2,1)S(1)}, bf16[64,2048]{1,0:T(8,128)(2,1)}, u32[]{:S(2)}) copy-start(bf16[64,2048]{1,0:T(8,128)(2,1)} %get-tuple-element.35.refs_1_) | copy-start | bytes 786436
  10.8 10.2 %copy-start.10 = (s32[128,1]{0,1:T(1,128)S(1)}, s32[128,1]{0,1:T(1,128)}, u32[]{:S(2)}) copy-start(s32[128,1]{0,1:T(1,128)} %param.18) | copy-start | bytes 1540
  10.9 10.2 %copy-start.11 = (s32[128]{0:T(128)S(1)}, s32[128]{0:T(128)}, u32[]{:S(2)}) copy-start(s32[128]{0:T(128)} %param.19) | copy-start | bytes 1540
  19.7 16.8 %copy-start.4 = (bf16[64,2048]{1,0:T(8,128)(2,1)S(1)}, bf16[64,2048]{1,0:T(8,128)(2,1)}, u32[]{:S(2)}) copy-start(bf16[64,2048]{1,0:T(8,128)(2,1)} %get-tuple-element.39.refs_0_) | copy-start | bytes 786436
  19.7 9.8 %collective-permute-start.3 = (bf16[64,2048]{1,0:T(8,128)(2,1)S(1)}, bf16[64,2048]{1,0:T(8,128)(2,1)S(1)}, u32[]{:S(2)}, u32[]{:S(2)}) collective-permute-start(bf16[64,2048]{1,0:T(8,128)(2,1)S(1)} %get-tuple-element.36), channel_id=1, source_target_pairs={{0,12},{2,14},{4,8},{6,10},{8,4},{10,6},{12,0},{14,2},{16,28},{18,... | collective-permute-start | bytes 786440 | tf_op jit(solution)/shard_map/ppermute | solution.py:524
  21.0 0.9 %copy-start.7 = (bf16[128,512]{1,0:T(8,128)(2,1)S(1)}, bf16[128,512]{1,0:T(8,128)(2,1)}, u32[]{:S(2)}) copy-start(bf16[128,512]{1,0:T(8,128)(2,1)} %fresh_ref.1) | copy-start | bytes 393220
  21.9 30.2 %copy-start.1 = (bf16[2,2048,64]{1,2,0:T(8,128)(2,1)S(1)}, bf16[2,2048,64]{1,2,0:T(8,128)(2,1)}, u32[]{:S(2)}) copy-start(bf16[2,2048,64]{1,2,0:T(8,128)(2,1)} %param.20) | copy-start | bytes 1572868
  25.9 10.6 %collective-permute-start.2 = (bf16[64,2176]{1,0:T(8,128)(2,1)S(1)}, bf16[64,2176]{1,0:T(8,128)(2,1)S(1)}, u32[]{:S(2)}, u32[]{:S(2)}) collective-permute-start(bf16[64,2176]{1,0:T(8,128)(2,1)S(1)} %get-tuple-element.33), channel_id=1, source_target_pairs={{0,6},{2,4},{4,2},{6,0},{8,14},{10,12},{12,10},{14,8},{16,22},{18,... | collective-permute-start | bytes 835592 | tf_op jit(solution)/shard_map/ppermute | solution.py:524
  26.6 13.2 %collective-permute-start = (bf16[64,2176]{1,0:T(8,128)(2,1)S(1)}, bf16[64,2176]{1,0:T(8,128)(2,1)S(1)}, u32[]{:S(2)}, u32[]{:S(2)}) collective-permute-start(bf16[64,2176]{1,0:T(8,128)(2,1)S(1)} %get-tuple-element.31), channel_id=1, source_target_pairs={{0,2},{2,0},{4,6},{6,4},{8,10},{10,8},{12,14},{14,12},{16,18},{18,... | collective-permute-start | bytes 835592 | tf_op jit(solution)/shard_map/ppermute | solution.py:524
  27.9 24.2 %collective-permute-start.1 = (bf16[64,2176]{1,0:T(8,128)(2,1)S(1)}, bf16[64,2176]{1,0:T(8,128)(2,1)S(1)}, u32[]{:S(2)}, u32[]{:S(2)}) collective-permute-start(bf16[64,2176]{1,0:T(8,128)(2,1)S(1)} %get-tuple-element.32), channel_id=1, source_target_pairs={{0,4},{2,6},{4,0},{6,2},{8,12},{10,14},{12,8},{14,10},{16,20},{18,... | collective-permute-start | bytes 835592 | tf_op jit(solution)/shard_map/ppermute | solution.py:524
  29.5 22.6 %collective-permute-start.4 = (bf16[64,2048]{1,0:T(8,128)(2,1)S(1)}, bf16[64,2048]{1,0:T(8,128)(2,1)S(1)}, u32[]{:S(2)}, u32[]{:S(2)}) collective-permute-start(bf16[64,2048]{1,0:T(8,128)(2,1)S(1)} %after.6), channel_id=1, source_target_pairs={{0,16},{2,18},{4,20},{6,22},{8,24},{10,26},{12,28},{14,30},{16,0},... | collective-permute-start | bytes 786440 | tf_op jit(solution)/shard_map/ppermute | solution.py:524
  31.1 21.6 %collective-permute-start.6 = (bf16[64,2048]{1,0:T(8,128)(2,1)S(1)}, bf16[64,2048]{1,0:T(8,128)(2,1)S(1)}, u32[]{:S(2)}, u32[]{:S(2)}) collective-permute-start(bf16[64,2048]{1,0:T(8,128)(2,1)S(1)} %get-tuple-element.38), channel_id=1, source_target_pairs={{0,12},{2,14},{4,8},{6,10},{8,4},{10,6},{12,0},{14,2},{16,28},{18,... | collective-permute-start | bytes 786440 | tf_op jit(solution)/shard_map/ppermute | solution.py:524
  36.5 17.8 %collective-permute-start.7 = (bf16[64,2048]{1,0:T(8,128)(2,1)S(1)}, bf16[64,2048]{1,0:T(8,128)(2,1)S(1)}, u32[]{:S(2)}, u32[]{:S(2)}) collective-permute-start(bf16[64,2048]{1,0:T(8,128)(2,1)S(1)} %after.7), channel_id=1, source_target_pairs={{0,12},{2,14},{4,8},{6,10},{8,4},{10,6},{12,0},{14,2},{16,28},{18,... | collective-permute-start | bytes 786440 | tf_op jit(solution)/shard_map/ppermute | solution.py:524
  52.6 2.9 %copy-start = (bf16[2,64,4096]{2,1,0:T(8,128)(2,1)S(1)}, bf16[2,64,4096]{2,1,0:T(8,128)(2,1)}, u32[]{:S(2)}) copy-start(bf16[2,64,4096]{2,1,0:T(8,128)(2,1)} %refs_1_.1) | copy-start | bytes 3145732
  52.6 1.7 %collective-permute-start.5 = (f32[256,128]{1,0:T(8,128)S(1)}, f32[256,128]{1,0:T(8,128)S(1)}, u32[]{:S(2)}, u32[]{:S(2)}) collective-permute-start(f32[256,128]{1,0:T(8,128)S(1)} %low_products.1.mine_ref), channel_id=1, source_target_pairs={{0,1},{1,0},{2,3},{3,2},{4,5},{5,4},{6,7},{7,6},{8,9},{9,8},{10,11... | collective-permute-start | bytes 393224 | tf_op jit(solution)/shard_map/ppermute | solution.py:598
  52.8 9.2 %collective-permute-start.8 = (bf16[64,2048]{1,0:T(8,128)(2,1)S(1)}, bf16[64,2048]{1,0:T(8,128)(2,1)S(1)}, u32[]{:S(2)}, u32[]{:S(2)}) collective-permute-start(bf16[64,2048]{1,0:T(8,128)(2,1)S(1)} %after.8), channel_id=1, source_target_pairs={{0,16},{2,18},{4,20},{6,22},{8,24},{10,26},{12,28},{14,30},{16,0},... | collective-permute-start | bytes 786440 | tf_op jit(solution)/shard_map/ppermute | solution.py:524
  54.4 12.8 %collective-permute-start.9 = (bf16[64,2048]{1,0:T(8,128)(2,1)S(1)}, bf16[64,2048]{1,0:T(8,128)(2,1)S(1)}, u32[]{:S(2)}, u32[]{:S(2)}) collective-permute-start(bf16[64,2048]{1,0:T(8,128)(2,1)S(1)} %after.9), channel_id=1, source_target_pairs={{0,16},{2,18},{4,20},{6,22},{8,24},{10,26},{12,28},{14,30},{16,0},... | collective-permute-start | bytes 786440 | tf_op jit(solution)/shard_map/ppermute | solution.py:524
  56.6 11.6 %collective-permute-start.10 = (bf16[32,4096]{1,0:T(8,128)(2,1)S(1)}, bf16[32,4096]{1,0:T(8,128)(2,1)S(1)}, u32[]{:S(2)}, u32[]{:S(2)}) collective-permute-start(bf16[32,4096]{1,0:T(8,128)(2,1)S(1)} %get-tuple-element.41), channel_id=1, source_target_pairs={{0,2},{2,0},{4,6},{6,4},{8,10},{10,8},{12,14},{14,12},{16,18},{18,... | collective-permute-start | bytes 786440 | tf_op jit(solution)/shard_map/ppermute | solution.py:524
  57.3 16.0 %collective-permute-start.12 = (bf16[32,4096]{1,0:T(8,128)(2,1)S(1)}, bf16[32,4096]{1,0:T(8,128)(2,1)S(1)}, u32[]{:S(2)}, u32[]{:S(2)}) collective-permute-start(bf16[32,4096]{1,0:T(8,128)(2,1)S(1)} %get-tuple-element.43), channel_id=1, source_target_pairs={{0,4},{2,6},{4,0},{6,2},{8,12},{10,14},{12,8},{14,10},{16,20},{18,... | collective-permute-start | bytes 786440 | tf_op jit(solution)/shard_map/ppermute | solution.py:524
  60.4 12.9 %collective-permute-start.14 = (bf16[32,4096]{1,0:T(8,128)(2,1)S(1)}, bf16[32,4096]{1,0:T(8,128)(2,1)S(1)}, u32[]{:S(2)}, u32[]{:S(2)}) collective-permute-start(bf16[32,4096]{1,0:T(8,128)(2,1)S(1)} %get-tuple-element.45), channel_id=1, source_target_pairs={{0,6},{2,4},{4,2},{6,0},{8,14},{10,12},{12,10},{14,8},{16,22},{18,... | collective-permute-start | bytes 786440 | tf_op jit(solution)/shard_map/ppermute | solution.py:524
  67.6 10.8 %collective-permute-start.11 = (bf16[32,4096]{1,0:T(8,128)(2,1)S(1)}, bf16[32,4096]{1,0:T(8,128)(2,1)S(1)}, u32[]{:S(2)}, u32[]{:S(2)}) collective-permute-start(bf16[32,4096]{1,0:T(8,128)(2,1)S(1)} %get-tuple-element.42), channel_id=1, source_target_pairs={{0,2},{2,0},{4,6},{6,4},{8,10},{10,8},{12,14},{14,12},{16,18},{18,... | collective-permute-start | bytes 786440 | tf_op jit(solution)/shard_map/ppermute | solution.py:524
  68.2 10.1 %collective-permute-start.13 = (bf16[32,4096]{1,0:T(8,128)(2,1)S(1)}, bf16[32,4096]{1,0:T(8,128)(2,1)S(1)}, u32[]{:S(2)}, u32[]{:S(2)}) collective-permute-start(bf16[32,4096]{1,0:T(8,128)(2,1)S(1)} %get-tuple-element.44), channel_id=1, source_target_pairs={{0,4},{2,6},{4,0},{6,2},{8,12},{10,14},{12,8},{14,10},{16,20},{18,... | collective-permute-start | bytes 786440 | tf_op jit(solution)/shard_map/ppermute | solution.py:524
  68.2 14.6 %collective-permute-start.15 = (bf16[32,4096]{1,0:T(8,128)(2,1)S(1)}, bf16[32,4096]{1,0:T(8,128)(2,1)S(1)}, u32[]{:S(2)}, u32[]{:S(2)}) collective-permute-start(bf16[32,4096]{1,0:T(8,128)(2,1)S(1)} %get-tuple-element.46), channel_id=1, source_target_pairs={{0,6},{2,4},{4,2},{6,0},{8,14},{10,12},{12,10},{14,8},{16,22},{18,... | collective-permute-start | bytes 786440 | tf_op jit(solution)/shard_map/ppermute | solution.py:524

commit v4 on v3

--- a/solution.py
+++ b/solution.py
@@ -437,7 +437,7 @@
 def lift_own(mine, other, weights):
     rows, rank = mine.shape
     width = weights.shape[1]
-    step = 1024
+    step = width
     low = pl.BlockSpec((rows // 2, rank), lambda j: (0, 0))
     out = jax.ShapeDtypeStruct((rows // 8, width), jnp.bfloat16)
     return pl.pallas_call(
@@ -500,7 +500,7 @@
 def gather_rows(slots, blocks):
     rows = slots.shape[1]
     width = blocks[0].shape[1]
-    step = 2048
+    step = 4096
     return pl.pallas_call(
         gather_rows_kernel,
         grid=(width // step,),
@@ -554,7 +554,7 @@
     pool = key_value_pool.reshape(pages * page_len, features)
 
     columns = up.shape[1]
-    early = columns // 8 * 4
+    early = columns // 8 * 5
     rank = up.shape[0] // 2
     outgoing, *packs = outgoing_pages(
         half,
@@ -568,7 +568,7 @@
     )
     arrived = lax.all_to_all(outgoing, "rep", split_axis=0, concat_axis=0, tiled=True)
     found = attend_pool(queries, pool, entries, lengths, page_len)
-    first = [along(pack, 0, 6) for pack in after(packs[:2], arrived, found[1])]
+    first = [along(*after(packs[:1], arrived, found[1]), 0, 6), along(packs[1], 0, 6)]
 
     def place(targets, replica):
         apart = jnp.bitwise_xor(targets, replica)

time: 84.8 us -> 83.7 us (0.987)
  waiting for transfers between devices: 33.7 us -> 37.7 us
  starting transfers between devices: 32.2 us -> 28.9 us
  Pallas kernels: 17.3 us -> 16.4 us
  local copies, waits for them, and re-layouts: 1.01 us -> 0.11 us
    ppermute x15, waiting for transfers between devices: 31.1 us -> 35 us  [along(): return lax.ppermute(array, ('group', 'rep'), pairs)]
    ppermute x15, starting transfers between devices: 24.9 us -> 21.5 us  [along(): return lax.ppermute(array, ('group', 'rep'), pairs)]
    unnamed x27, local copies, waits for them, and re-layouts: 1.01 us -> 0.11 us
where the time goes in v4:
time: 83.7 us; the launch traced here: 83.4 us
  waiting for transfers between devices  37.7 us (45%)
  starting transfers between devices  28.9 us (35%)
  Pallas kernels  16.4 us (20%)
    ppermute x15, waiting for transfers between devices, along(): return lax.ppermute(array, ('group', 'rep'), pairs)  35 us
    ppermute x15, starting transfers between devices, along(): return lax.ppermute(array, ('group', 'rep'), pairs)  21.5 us
    all_to_all x1, starting transfers between devices, shared_local(): lax.all_to_all(outgoing, 'rep', split_axis=0, concat_axis=0, tiled=True)  7.28 us
    pallas_call x1, Pallas kernels, attend_pool(): pl.pallas_call(functools.partial(pool_kernel, page_len), grid=(kv_local,)...  6.15 us
    pallas_call x1, Pallas kernels, finish(): pl.pallas_call(functools.partial(finish_kernel, page_len, first_token, pl...  3.99 us
    pallas_call x1, Pallas kernels, outgoing_pages(): pl.pallas_call(functools.partial(outgoing_kernel, pieces), out_shape=out_...  3.5 us
    all_to_all x1, waiting for transfers between devices, shared_local(): lax.all_to_all(outgoing, 'rep', split_axis=0, concat_axis=0, tiled=True)  2.66 us
  transfers between devices with their start and end apart: 17, of which 8 were waited for; matrix products, arithmetic and copies ran while one was open for 0% of the time, Pallas kernels for 14%

profile of v4, /device:TPU:0, one launch (start us, length us, event | category | flops | bytes accessed | tf_op | source)
XLA Modules:
  0.0 83.4 jit_solution(17303313883588205843)
XLA Ops:
  0.0 0.0 copy-start.2
  0.0 0.0 copy-start.3
  0.0 0.0 copy-start.7
  0.0 0.0 copy-start.8
  0.0 3.5 %outgoing_pages.1 = (bf16[16,16,512]{2,1,0:T(8,128)(2,1)}, bf16[64,2048]{1,0:T(8,128)(2,1)}, bf16[64,2560]{1,0:T(8,128)(2,1)}, bf16[64,1536]{1,0:T(8,128)(2,1)}) custom-call(s32[1]{0:T(128)} %bitcast.1.half_ref, s32[6]{0:T(128)} %page_ref.1, s32[6]{0:T(128)} %target_ref.1, bf16[96,16,512]{2,1,0:T(8,128)(2,1)} %pool_ref.1, bf16[2,64,2048]{2,1,0:T(8,128)(2,1)} %bitcast.14, ...), custom_call_target="tpu_custom_call" | custom-call | flops 1024 | bytes 1024 | tf_op jit(solution)/shard_map/outgoing_pages/pallas_call | solution.py:103
  3.5 7.3 %all-to-all-start = ((bf16[16,16,512]{2,1,0:T(8,128)(2,1)}), bf16[16,16,512]{2,1,0:T(8,128)(2,1)S(1)}, u32[]{:S(2)}, u32[]{:S(2)}) async-start(bf16[16,16,512]{2,1,0:T(8,128)(2,1)} %get-tuple-element.26), calls=%async_computation | async-start | bytes 524288 | tf_op jit(solution)/shard_map/all_to_all | solution.py:569
  10.8 0.0 copy-done.2
  10.8 0.0 copy-done.3
  10.8 0.0 copy-done.7
  10.8 0.0 copy-done.8
  10.8 0.0 copy-start.4
  10.8 0.0 copy-start.6
  10.9 0.0 copy-start.9
  10.9 0.0 copy-start.10
  10.9 6.2 %attend_pool.1 = (bf16[2048,128]{1,0:T(8,128)(2,1)S(1)}, f32[128,256]{1,0:T(8,128)S(1)}) custom-call(bf16[128,2048]{1,0:T(8,128)(2,1)S(1)} %copy-done.3, bf16[1536,512]{1,0:T(8,128)(2,1)S(1)} %bitcast.16, s32[4,128]{1,0:T(4,128)S(1)} %bitcast.17, s32[1,128]{1,0:T(1,128)S(1)} %bitcast.19), custom_call_target="tpu_custom_call" | custom-call | flops 1000000000 | bytes 1000000 | tf_op jit(solution)/shard_map/attend_pool/pallas_call | solution.py:219
  17.0 0.0 copy-start.11
  17.1 2.7 %all-to-all-done.refs_1_ = bf16[16,16,512]{2,1,0:T(8,128)(2,1)S(1)} async-done(((bf16[16,16,512]{2,1,0:T(8,128)(2,1)}), bf16[16,16,512]{2,1,0:T(8,128)(2,1)S(1)}, u32[]{:S(2)}, u32[]{:S(2)}) %all-to-all-start) | async-done | bytes 262176 | tf_op jit(solution)/shard_map/all_to_all | solution.py:569
  19.7 0.0 copy-done.4
  19.7 0.0 copy-start.5
  19.7 1.3 %collective-permute-start.3 = (bf16[64,2048]{1,0:T(8,128)(2,1)S(1)}, bf16[64,2048]{1,0:T(8,128)(2,1)S(1)}, u32[]{:S(2)}, u32[]{:S(2)}) collective-permute-start(bf16[64,2048]{1,0:T(8,128)(2,1)S(1)} %after.5), channel_id=1, source_target_pairs={{0,12},{2,14},{4,8},{6,10},{8,4},{10,6},{12,0},{14,2},{16,28},{18,... | collective-permute-start | bytes 786440 | tf_op jit(solution)/shard_map/ppermute | solution.py:524
  21.0 0.1 pad_add_fusion.where_ref
  21.0 0.0 copy-done.6
  21.1 0.0 copy-done.9
  21.1 0.0 copy-done.10
  21.1 4.0 %finish.1 = (s32[1,128]{1,0:T(1,128)S(1)}, bf16[64,2176]{1,0:T(8,128)(2,1)S(1)}, bf16[64,2176]{1,0:T(8,128)(2,1)S(1)}, bf16[64,2176]{1,0:T(8,128)(2,1)S(1)}, bf16[64,2176]{1,0:T(8,128)(2,1)S(1)}) custom-call(s32[2]{0:T(128)S(1)} %pad_add_fusion.where_ref, bf16[128,2048]{1,0:T(8,128)(2,1)S(1)} %copy-done.3, bf16[2048,128]{1,0:T(8,128)(2,1)S(1)} %get-tuple-element.24.part_ref, ...), custom_call_target="tpu_custom_call" | custom-call | flops 1024 | bytes 1024 | tf_op jit(solution)/shard_map/finish/pallas_call | solution.py:337
  25.1 0.6 collective-permute-start.2
  25.7 1.3 %collective-permute-start = (bf16[64,2176]{1,0:T(8,128)(2,1)S(1)}, bf16[64,2176]{1,0:T(8,128)(2,1)S(1)}, u32[]{:S(2)}, u32[]{:S(2)}) collective-permute-start(bf16[64,2176]{1,0:T(8,128)(2,1)S(1)} %get-tuple-element.29), channel_id=1, source_target_pairs={{0,2},{2,0},{4,6},{6,4},{8,10},{10,8},{12,14},{14,12},{16,18},{18,... | collective-permute-start | bytes 835592 | tf_op jit(solution)/shard_map/ppermute | solution.py:524
  27.0 1.6 %collective-permute-start.1 = (bf16[64,2176]{1,0:T(8,128)(2,1)S(1)}, bf16[64,2176]{1,0:T(8,128)(2,1)S(1)}, u32[]{:S(2)}, u32[]{:S(2)}) collective-permute-start(bf16[64,2176]{1,0:T(8,128)(2,1)S(1)} %get-tuple-element.30), channel_id=1, source_target_pairs={{0,4},{2,6},{4,0},{6,2},{8,12},{10,14},{12,8},{14,10},{16,20},{18,... | collective-permute-start | bytes 835592 | tf_op jit(solution)/shard_map/ppermute | solution.py:524
  28.6 0.0 copy-done.11
  28.6 2.6 %collective-permute-start.6 = (bf16[64,2560]{1,0:T(8,128)(2,1)S(1)}, bf16[64,2560]{1,0:T(8,128)(2,1)S(1)}, u32[]{:S(2)}, u32[]{:S(2)}) collective-permute-start(bf16[64,2560]{1,0:T(8,128)(2,1)S(1)} %copy-done.11), channel_id=1, source_target_pairs={{0,12},{2,14},{4,8},{6,10},{8,4},{10,6},{12,0},{14,2},{16,28},{18,... | collective-permute-start | bytes 983048 | tf_op jit(solution)/shard_map/ppermute | solution.py:524
  31.2 0.0 collective-permute-done.3.refs_5_
  31.2 1.6 %collective-permute-start.4 = (bf16[64,2048]{1,0:T(8,128)(2,1)S(1)}, bf16[64,2048]{1,0:T(8,128)(2,1)S(1)}, u32[]{:S(2)}, u32[]{:S(2)}) collective-permute-start(bf16[64,2048]{1,0:T(8,128)(2,1)S(1)} %after.6), channel_id=1, source_target_pairs={{0,16},{2,18},{4,20},{6,22},{8,24},{10,26},{12,28},{14,30},{16,0},... | collective-permute-start | bytes 786440 | tf_op jit(solution)/shard_map/ppermute | solution.py:524
  32.8 3.2 %collective-permute-done.2.refs_3_.refs_1_ = bf16[64,2176]{1,0:T(8,128)(2,1)S(1)} collective-permute-done((bf16[64,2176]{1,0:T(8,128)(2,1)S(1)}, bf16[64,2176]{1,0:T(8,128)(2,1)S(1)}, u32[]{:S(2)}, u32[]{:S(2)}) %collective-permute-start.2) | collective-permute-done | bytes 278560 | tf_op jit(solution)/shard_map/ppermute | solution.py:524
  36.0 0.0 copy-done.5
  36.0 2.6 %collective-permute-start.7 = (bf16[64,1536]{1,0:T(8,128)(2,1)S(1)}, bf16[64,1536]{1,0:T(8,128)(2,1)S(1)}, u32[]{:S(2)}, u32[]{:S(2)}) collective-permute-start(bf16[64,1536]{1,0:T(8,128)(2,1)S(1)} %after.7), channel_id=1, source_target_pairs={{0,12},{2,14},{4,8},{6,10},{8,4},{10,6},{12,0},{14,2},{16,28},{18,... | collective-permute-start | bytes 589832 | tf_op jit(solution)/shard_map/ppermute | solution.py:524
  38.7 0.3 collective-permute-done.refs_1_
  38.9 12.8 %collective-permute-done.1.refs_2_ = bf16[64,2176]{1,0:T(8,128)(2,1)S(1)} collective-permute-done((bf16[64,2176]{1,0:T(8,128)(2,1)S(1)}, bf16[64,2176]{1,0:T(8,128)(2,1)S(1)}, u32[]{:S(2)}, u32[]{:S(2)}) %collective-permute-start.1) | collective-permute-done | bytes 278560 | tf_op jit(solution)/shard_map/ppermute | solution.py:524
  51.7 0.0 collective-permute-done.4.refs_6_
  51.7 0.0 copy-done.1
  51.7 0.5 low_products.1.mine_ref
  52.2 0.1 collective-permute-start.5
  52.3 0.0 collective-permute-done.6.refs_0_
  52.3 1.6 %collective-permute-start.8 = (bf16[64,2560]{1,0:T(8,128)(2,1)S(1)}, bf16[64,2560]{1,0:T(8,128)(2,1)S(1)}, u32[]{:S(2)}, u32[]{:S(2)}) collective-permute-start(bf16[64,2560]{1,0:T(8,128)(2,1)S(1)} %after.8), channel_id=1, source_target_pairs={{0,16},{2,18},{4,20},{6,22},{8,24},{10,26},{12,28},{14,30},{16,0},... | collective-permute-start | bytes 983048 | tf_op jit(solution)/shard_map/ppermute | solution.py:524
  53.9 0.0 collective-permute-done.5.other_ref.refs_1_
  53.9 0.0 copy-done
  53.9 0.4 lift_own.1
  54.3 1.1 %collective-permute-start.10 = (bf16[32,4096]{1,0:T(8,128)(2,1)S(1)}, bf16[32,4096]{1,0:T(8,128)(2,1)S(1)}, u32[]{:S(2)}, u32[]{:S(2)}) collective-permute-start(bf16[32,4096]{1,0:T(8,128)(2,1)S(1)} %get-tuple-element.37), channel_id=1, source_target_pairs={{0,2},{2,0},{4,6},{6,4},{8,10},{10,8},{12,14},{14,12},{16,18},{18,... | collective-permute-start | bytes 786440 | tf_op jit(solution)/shard_map/ppermute | solution.py:524
  55.4 0.0 collective-permute-done.7.refs_1_
  55.5 1.3 %collective-permute-start.9 = (bf16[64,1536]{1,0:T(8,128)(2,1)S(1)}, bf16[64,1536]{1,0:T(8,128)(2,1)S(1)}, u32[]{:S(2)}, u32[]{:S(2)}) collective-permute-start(bf16[64,1536]{1,0:T(8,128)(2,1)S(1)} %after.9), channel_id=1, source_target_pairs={{0,16},{2,18},{4,20},{6,22},{8,24},{10,26},{12,28},{14,30},{16,0},... | collective-permute-start | bytes 589832 | tf_op jit(solution)/shard_map/ppermute | solution.py:524
  56.7 0.0 collective-permute-start.12
  56.8 2.4 %collective-permute-start.14 = (bf16[32,4096]{1,0:T(8,128)(2,1)S(1)}, bf16[32,4096]{1,0:T(8,128)(2,1)S(1)}, u32[]{:S(2)}, u32[]{:S(2)}) collective-permute-start(bf16[32,4096]{1,0:T(8,128)(2,1)S(1)} %get-tuple-element.41), channel_id=1, source_target_pairs={{0,6},{2,4},{4,2},{6,0},{8,14},{10,12},{12,10},{14,8},{16,22},{18,... | collective-permute-start | bytes 786440 | tf_op jit(solution)/shard_map/ppermute | solution.py:524
  59.2 3.7 %collective-permute-done.8.refs_2_ = bf16[64,2560]{1,0:T(8,128)(2,1)S(1)} collective-permute-done((bf16[64,2560]{1,0:T(8,128)(2,1)S(1)}, bf16[64,2560]{1,0:T(8,128)(2,1)S(1)}, u32[]{:S(2)}, u32[]{:S(2)}) %collective-permute-start.8) | collective-permute-done | bytes 327712 | tf_op jit(solution)/shard_map/ppermute | solution.py:524
  62.9 3.8 %collective-permute-done.9.refs_3_ = bf16[64,1536]{1,0:T(8,128)(2,1)S(1)} collective-permute-done((bf16[64,1536]{1,0:T(8,128)(2,1)S(1)}, bf16[64,1536]{1,0:T(8,128)(2,1)S(1)}, u32[]{:S(2)}, u32[]{:S(2)}) %collective-permute-start.9) | collective-permute-done | bytes 196640 | tf_op jit(solution)/shard_map/ppermute | solution.py:524
  66.7 0.4 lift_far.1
  67.1 1.1 %collective-permute-start.11 = (bf16[32,4096]{1,0:T(8,128)(2,1)S(1)}, bf16[32,4096]{1,0:T(8,128)(2,1)S(1)}, u32[]{:S(2)}, u32[]{:S(2)}) collective-permute-start(bf16[32,4096]{1,0:T(8,128)(2,1)S(1)} %get-tuple-element.38), channel_id=1, source_target_pairs={{0,2},{2,0},{4,6},{6,4},{8,10},{10,8},{12,14},{14,12},{16,18},{18,... | collective-permute-start | bytes 786440 | tf_op jit(solution)/shard_map/ppermute | solution.py:524
  68.2 0.0 collective-permute-start.13
  68.2 0.0 collective-permute-done.10.refs_2_
  68.2 2.5 %collective-permute-start.15 = (bf16[32,4096]{1,0:T(8,128)(2,1)S(1)}, bf16[32,4096]{1,0:T(8,128)(2,1)S(1)}, u32[]{:S(2)}, u32[]{:S(2)}) collective-permute-start(bf16[32,4096]{1,0:T(8,128)(2,1)S(1)} %get-tuple-element.42), channel_id=1, source_target_pairs={{0,6},{2,4},{4,2},{6,0},{8,14},{10,12},{12,10},{14,8},{16,22},{18,... | collective-permute-start | bytes 786440 | tf_op jit(solution)/shard_map/ppermute | solution.py:524
  70.7 0.0 collective-permute-done.12.refs_4_
  70.7 0.0 collective-permute-done.14.refs_6_
  70.7 7.0 %collective-permute-done.11.refs_3_ = bf16[32,4096]{1,0:T(8,128)(2,1)S(1)} collective-permute-done((bf16[32,4096]{1,0:T(8,128)(2,1)S(1)}, bf16[32,4096]{1,0:T(8,128)(2,1)S(1)}, u32[]{:S(2)}, u32[]{:S(2)}) %collective-permute-start.11) | collective-permute-done | bytes 262176 | tf_op jit(solution)/shard_map/ppermute | solution.py:524
  77.7 0.0 collective-permute-done.13.refs_5_
  77.7 4.2 %collective-permute-done.15.refs_7_ = bf16[32,4096]{1,0:T(8,128)(2,1)S(1)} collective-permute-done((bf16[32,4096]{1,0:T(8,128)(2,1)S(1)}, bf16[32,4096]{1,0:T(8,128)(2,1)S(1)}, u32[]{:S(2)}, u32[]{:S(2)}) %collective-permute-start.15) | collective-permute-done | bytes 262176 | tf_op jit(solution)/shard_map/ppermute | solution.py:524
  81.9 1.5 %gather_rows.1 = bf16[128,4096]{1,0:T(8,128)(2,1)} custom-call(s32[1,128]{1,0:T(1,128)S(1)} %get-tuple-element.27.refs_1_.slot_ref, bf16[32,4096]{1,0:T(8,128)(2,1)S(1)} %get-tuple-element.33.refs_0_, bf16[32,4096]{1,0:T(8,128)(2,1)S(1)} %get-tuple-element.36.refs_1_, bf16[32,4096]{1,0:T(8,128)(2,1)S(1)} %collective-permute-done.10.refs_2_, ...), custom_call_target="tpu_custom_call" | custom-call | flops 1024 | bytes 1024 | tf_op jit(solution)/shard_map/gather_rows/pallas_call | solution.py:504
  (10 shorter events, 0.1 us)
Async XLA Ops:
  0.0 10.8 %copy-start.2 = (bf16[96,16,512]{2,1,0:T(8,128)(2,1)S(1)}, bf16[96,16,512]{2,1,0:T(8,128)(2,1)}, u32[]{:S(2)}) copy-start(bf16[96,16,512]{2,1,0:T(8,128)(2,1)} %pool_ref.1) | copy-start | bytes 4718596
  0.0 10.8 %copy-start.3 = (bf16[128,2048]{1,0:T(8,128)(2,1)S(1)}, bf16[128,2048]{1,0:T(8,128)(2,1)}, u32[]{:S(2)}) copy-start(bf16[128,2048]{1,0:T(8,128)(2,1)} %query_ref.3) | copy-start | bytes 1572868
  0.0 10.8 %copy-start.7 = (s32[128,4]{0,1:T(4,128)S(1)}, s32[128,4]{0,1:T(4,128)}, u32[]{:S(2)}) copy-start(s32[128,4]{0,1:T(4,128)} %param.14) | copy-start | bytes 6148
  0.0 10.8 %copy-start.8 = (s32[128]{0:T(128)S(1)}, s32[128]{0:T(128)}, u32[]{:S(2)}) copy-start(s32[128]{0:T(128)} %param.15) | copy-start | bytes 1540
  3.5 16.2 %all-to-all-start = ((bf16[16,16,512]{2,1,0:T(8,128)(2,1)}), bf16[16,16,512]{2,1,0:T(8,128)(2,1)S(1)}, u32[]{:S(2)}, u32[]{:S(2)}) async-start(bf16[16,16,512]{2,1,0:T(8,128)(2,1)} %get-tuple-element.26), calls=%async_computation | async-start | bytes 524288 | tf_op jit(solution)/shard_map/all_to_all | solution.py:569
  10.8 8.9 %copy-start.4 = (bf16[64,2048]{1,0:T(8,128)(2,1)S(1)}, bf16[64,2048]{1,0:T(8,128)(2,1)}, u32[]{:S(2)}) copy-start(bf16[64,2048]{1,0:T(8,128)(2,1)} %get-tuple-element.32.refs_0_) | copy-start | bytes 786436
  10.8 10.2 %copy-start.6 = (bf16[128,512]{1,0:T(8,128)(2,1)S(1)}, bf16[128,512]{1,0:T(8,128)(2,1)}, u32[]{:S(2)}) copy-start(bf16[128,512]{1,0:T(8,128)(2,1)} %fresh_ref.1) | copy-start | bytes 393220
  10.9 10.2 %copy-start.9 = (s32[128,1]{0,1:T(1,128)S(1)}, s32[128,1]{0,1:T(1,128)}, u32[]{:S(2)}) copy-start(s32[128,1]{0,1:T(1,128)} %param.18) | copy-start | bytes 1540
  10.9 10.2 %copy-start.10 = (s32[128]{0:T(128)S(1)}, s32[128]{0:T(128)}, u32[]{:S(2)}) copy-start(s32[128]{0:T(128)} %param.19) | copy-start | bytes 1540
  17.0 11.6 %copy-start.11 = (bf16[64,2560]{1,0:T(8,128)(2,1)S(1)}, bf16[64,2560]{1,0:T(8,128)(2,1)}, u32[]{:S(2)}) copy-start(bf16[64,2560]{1,0:T(8,128)(2,1)} %get-tuple-element.34) | copy-start | bytes 983044
  19.7 16.3 %copy-start.5 = (bf16[64,1536]{1,0:T(8,128)(2,1)S(1)}, bf16[64,1536]{1,0:T(8,128)(2,1)}, u32[]{:S(2)}) copy-start(bf16[64,1536]{1,0:T(8,128)(2,1)} %get-tuple-element.35.refs_0_) | copy-start | bytes 589828
  19.7 11.5 %collective-permute-start.3 = (bf16[64,2048]{1,0:T(8,128)(2,1)S(1)}, bf16[64,2048]{1,0:T(8,128)(2,1)S(1)}, u32[]{:S(2)}, u32[]{:S(2)}) collective-permute-start(bf16[64,2048]{1,0:T(8,128)(2,1)S(1)} %after.5), channel_id=1, source_target_pairs={{0,12},{2,14},{4,8},{6,10},{8,4},{10,6},{12,0},{14,2},{16,28},{18,... | collective-permute-start | bytes 786440 | tf_op jit(solution)/shard_map/ppermute | solution.py:524
  21.1 30.7 %copy-start.1 = (bf16[2,2048,64]{1,2,0:T(8,128)(2,1)S(1)}, bf16[2,2048,64]{1,2,0:T(8,128)(2,1)}, u32[]{:S(2)}) copy-start(bf16[2,2048,64]{1,2,0:T(8,128)(2,1)} %param.20) | copy-start | bytes 1572868
  25.1 11.0 %collective-permute-start.2 = (bf16[64,2176]{1,0:T(8,128)(2,1)S(1)}, bf16[64,2176]{1,0:T(8,128)(2,1)S(1)}, u32[]{:S(2)}, u32[]{:S(2)}) collective-permute-start(bf16[64,2176]{1,0:T(8,128)(2,1)S(1)} %get-tuple-element.31), channel_id=1, source_target_pairs={{0,6},{2,4},{4,2},{6,0},{8,14},{10,12},{12,10},{14,8},{16,22},{18,... | collective-permute-start | bytes 835592 | tf_op jit(solution)/shard_map/ppermute | solution.py:524
  25.7 13.2 %collective-permute-start = (bf16[64,2176]{1,0:T(8,128)(2,1)S(1)}, bf16[64,2176]{1,0:T(8,128)(2,1)S(1)}, u32[]{:S(2)}, u32[]{:S(2)}) collective-permute-start(bf16[64,2176]{1,0:T(8,128)(2,1)S(1)} %get-tuple-element.29), channel_id=1, source_target_pairs={{0,2},{2,0},{4,6},{6,4},{8,10},{10,8},{12,14},{14,12},{16,18},{18,... | collective-permute-start | bytes 835592 | tf_op jit(solution)/shard_map/ppermute | solution.py:524
  27.0 24.8 %collective-permute-start.1 = (bf16[64,2176]{1,0:T(8,128)(2,1)S(1)}, bf16[64,2176]{1,0:T(8,128)(2,1)S(1)}, u32[]{:S(2)}, u32[]{:S(2)}) collective-permute-start(bf16[64,2176]{1,0:T(8,128)(2,1)S(1)} %get-tuple-element.30), channel_id=1, source_target_pairs={{0,4},{2,6},{4,0},{6,2},{8,12},{10,14},{12,8},{14,10},{16,20},{18,... | collective-permute-start | bytes 835592 | tf_op jit(solution)/shard_map/ppermute | solution.py:524
  28.6 23.7 %collective-permute-start.6 = (bf16[64,2560]{1,0:T(8,128)(2,1)S(1)}, bf16[64,2560]{1,0:T(8,128)(2,1)S(1)}, u32[]{:S(2)}, u32[]{:S(2)}) collective-permute-start(bf16[64,2560]{1,0:T(8,128)(2,1)S(1)} %copy-done.11), channel_id=1, source_target_pairs={{0,12},{2,14},{4,8},{6,10},{8,4},{10,6},{12,0},{14,2},{16,28},{18,... | collective-permute-start | bytes 983048 | tf_op jit(solution)/shard_map/ppermute | solution.py:524
  31.2 20.5 %collective-permute-start.4 = (bf16[64,2048]{1,0:T(8,128)(2,1)S(1)}, bf16[64,2048]{1,0:T(8,128)(2,1)S(1)}, u32[]{:S(2)}, u32[]{:S(2)}) collective-permute-start(bf16[64,2048]{1,0:T(8,128)(2,1)S(1)} %after.6), channel_id=1, source_target_pairs={{0,16},{2,18},{4,20},{6,22},{8,24},{10,26},{12,28},{14,30},{16,0},... | collective-permute-start | bytes 786440 | tf_op jit(solution)/shard_map/ppermute | solution.py:524
  36.0 19.4 %collective-permute-start.7 = (bf16[64,1536]{1,0:T(8,128)(2,1)S(1)}, bf16[64,1536]{1,0:T(8,128)(2,1)S(1)}, u32[]{:S(2)}, u32[]{:S(2)}) collective-permute-start(bf16[64,1536]{1,0:T(8,128)(2,1)S(1)} %after.7), channel_id=1, source_target_pairs={{0,12},{2,14},{4,8},{6,10},{8,4},{10,6},{12,0},{14,2},{16,28},{18,... | collective-permute-start | bytes 589832 | tf_op jit(solution)/shard_map/ppermute | solution.py:524
  51.7 2.2 %copy-start = (bf16[2,64,4096]{2,1,0:T(8,128)(2,1)S(1)}, bf16[2,64,4096]{2,1,0:T(8,128)(2,1)}, u32[]{:S(2)}) copy-start(bf16[2,64,4096]{2,1,0:T(8,128)(2,1)} %refs_1_.1) | copy-start | bytes 3145732
  52.2 1.7 %collective-permute-start.5 = (f32[256,128]{1,0:T(8,128)S(1)}, f32[256,128]{1,0:T(8,128)S(1)}, u32[]{:S(2)}, u32[]{:S(2)}) collective-permute-start(f32[256,128]{1,0:T(8,128)S(1)} %low_products.1.mine_ref), channel_id=1, source_target_pairs={{0,1},{1,0},{2,3},{3,2},{4,5},{5,4},{6,7},{7,6},{8,9},{9,8},{10,11... | collective-permute-start | bytes 393224 | tf_op jit(solution)/shard_map/ppermute | solution.py:598
  52.3 10.6 %collective-permute-start.8 = (bf16[64,2560]{1,0:T(8,128)(2,1)S(1)}, bf16[64,2560]{1,0:T(8,128)(2,1)S(1)}, u32[]{:S(2)}, u32[]{:S(2)}) collective-permute-start(bf16[64,2560]{1,0:T(8,128)(2,1)S(1)} %after.8), channel_id=1, source_target_pairs={{0,16},{2,18},{4,20},{6,22},{8,24},{10,26},{12,28},{14,30},{16,0},... | collective-permute-start | bytes 983048 | tf_op jit(solution)/shard_map/ppermute | solution.py:524
  54.3 13.9 %collective-permute-start.10 = (bf16[32,4096]{1,0:T(8,128)(2,1)S(1)}, bf16[32,4096]{1,0:T(8,128)(2,1)S(1)}, u32[]{:S(2)}, u32[]{:S(2)}) collective-permute-start(bf16[32,4096]{1,0:T(8,128)(2,1)S(1)} %get-tuple-element.37), channel_id=1, source_target_pairs={{0,2},{2,0},{4,6},{6,4},{8,10},{10,8},{12,14},{14,12},{16,18},{18,... | collective-permute-start | bytes 786440 | tf_op jit(solution)/shard_map/ppermute | solution.py:524
  55.5 11.3 %collective-permute-start.9 = (bf16[64,1536]{1,0:T(8,128)(2,1)S(1)}, bf16[64,1536]{1,0:T(8,128)(2,1)S(1)}, u32[]{:S(2)}, u32[]{:S(2)}) collective-permute-start(bf16[64,1536]{1,0:T(8,128)(2,1)S(1)} %after.9), channel_id=1, source_target_pairs={{0,16},{2,18},{4,20},{6,22},{8,24},{10,26},{12,28},{14,30},{16,0},... | collective-permute-start | bytes 589832 | tf_op jit(solution)/shard_map/ppermute | solution.py:524
  56.7 14.0 %collective-permute-start.12 = (bf16[32,4096]{1,0:T(8,128)(2,1)S(1)}, bf16[32,4096]{1,0:T(8,128)(2,1)S(1)}, u32[]{:S(2)}, u32[]{:S(2)}) collective-permute-start(bf16[32,4096]{1,0:T(8,128)(2,1)S(1)} %get-tuple-element.39), channel_id=1, source_target_pairs={{0,4},{2,6},{4,0},{6,2},{8,12},{10,14},{12,8},{14,10},{16,20},{18,... | collective-permute-start | bytes 786440 | tf_op jit(solution)/shard_map/ppermute | solution.py:524
  56.8 13.9 %collective-permute-start.14 = (bf16[32,4096]{1,0:T(8,128)(2,1)S(1)}, bf16[32,4096]{1,0:T(8,128)(2,1)S(1)}, u32[]{:S(2)}, u32[]{:S(2)}) collective-permute-start(bf16[32,4096]{1,0:T(8,128)(2,1)S(1)} %get-tuple-element.41), channel_id=1, source_target_pairs={{0,6},{2,4},{4,2},{6,0},{8,14},{10,12},{12,10},{14,8},{16,22},{18,... | collective-permute-start | bytes 786440 | tf_op jit(solution)/shard_map/ppermute | solution.py:524
  67.1 10.6 %collective-permute-start.11 = (bf16[32,4096]{1,0:T(8,128)(2,1)S(1)}, bf16[32,4096]{1,0:T(8,128)(2,1)S(1)}, u32[]{:S(2)}, u32[]{:S(2)}) collective-permute-start(bf16[32,4096]{1,0:T(8,128)(2,1)S(1)} %get-tuple-element.38), channel_id=1, source_target_pairs={{0,2},{2,0},{4,6},{6,4},{8,10},{10,8},{12,14},{14,12},{16,18},{18,... | collective-permute-start | bytes 786440 | tf_op jit(solution)/shard_map/ppermute | solution.py:524
  68.2 9.5 %collective-permute-start.13 = (bf16[32,4096]{1,0:T(8,128)(2,1)S(1)}, bf16[32,4096]{1,0:T(8,128)(2,1)S(1)}, u32[]{:S(2)}, u32[]{:S(2)}) collective-permute-start(bf16[32,4096]{1,0:T(8,128)(2,1)S(1)} %get-tuple-element.40), channel_id=1, source_target_pairs={{0,4},{2,6},{4,0},{6,2},{8,12},{10,14},{12,8},{14,10},{16,20},{18,... | collective-permute-start | bytes 786440 | tf_op jit(solution)/shard_map/ppermute | solution.py:524
  68.2 13.7 %collective-permute-start.15 = (bf16[32,4096]{1,0:T(8,128)(2,1)S(1)}, bf16[32,4096]{1,0:T(8,128)(2,1)S(1)}, u32[]{:S(2)}, u32[]{:S(2)}) collective-permute-start(bf16[32,4096]{1,0:T(8,128)(2,1)S(1)} %get-tuple-element.42), channel_id=1, source_target_pairs={{0,6},{2,4},{4,2},{6,0},{8,14},{10,12},{12,10},{14,8},{16,22},{18,... | collective-permute-start | bytes 786440 | tf_op jit(solution)/shard_map/ppermute | solution.py:524

commit v5 on v4

--- a/solution.py
+++ b/solution.py
@@ -85,12 +85,13 @@
                     share_sem.at[len(shares)],
                 )
             )
-    lax.fori_loop(0, slot_number, clear, 0)
-    lax.fori_loop(0, entry_number, place, 0)
-    lax.fori_loop(0, slot_number, send, 0)
     for share in shares:
         share.start()
-    lax.fori_loop(0, slot_number, finish, 0)
+    unroll = slot_number <= 16
+    lax.fori_loop(0, slot_number, clear, 0, unroll=unroll)
+    lax.fori_loop(0, entry_number, place, 0, unroll=unroll)
+    lax.fori_loop(0, slot_number, send, 0, unroll=unroll)
+    lax.fori_loop(0, slot_number, finish, 0, unroll=unroll)
     for share in shares:
         share.wait()
 

time: 83.7 us -> 83.5 us (level)
  no operation moved by 1% of the time
where the time goes in v5:
time: 83.5 us; the launch traced here: 83.2 us
  waiting for transfers between devices  37.7 us (45%)
  starting transfers between devices  28.9 us (35%)
  Pallas kernels  16.2 us (19%)
    ppermute x15, waiting for transfers between devices, along(): return lax.ppermute(array, ('group', 'rep'), pairs)  35 us
    ppermute x15, starting transfers between devices, along(): return lax.ppermute(array, ('group', 'rep'), pairs)  21.6 us
    all_to_all x1, starting transfers between devices, shared_local(): lax.all_to_all(outgoing, 'rep', split_axis=0, concat_axis=0, tiled=True)  7.26 us
    pallas_call x1, Pallas kernels, attend_pool(): pl.pallas_call(functools.partial(pool_kernel, page_len), grid=(kv_local,)...  6.15 us
    pallas_call x1, Pallas kernels, finish(): pl.pallas_call(functools.partial(finish_kernel, page_len, first_token, pl...  3.99 us
    pallas_call x1, Pallas kernels, outgoing_pages(): pl.pallas_call(functools.partial(outgoing_kernel, pieces), out_shape=out_...  3.31 us
    all_to_all x1, waiting for transfers between devices, shared_local(): lax.all_to_all(outgoing, 'rep', split_axis=0, concat_axis=0, tiled=True)  2.67 us
  transfers between devices with their start and end apart: 17, of which 8 were waited for; matrix products, arithmetic and copies ran while one was open for 0% of the time, Pallas kernels for 14%

profile of v5, /device:TPU:0, one launch (start us, length us, event | category | flops | bytes accessed | tf_op | source)
XLA Modules:
  0.0 83.2 jit_solution(17641168712916514420)
XLA Ops:
  0.0 0.0 copy-start.2
  0.0 0.0 copy-start.3
  0.0 0.0 copy-start.8
  0.0 3.3 %outgoing_pages.1 = (bf16[16,16,512]{2,1,0:T(8,128)(2,1)}, bf16[64,2048]{1,0:T(8,128)(2,1)}, bf16[64,2560]{1,0:T(8,128)(2,1)}, bf16[64,1536]{1,0:T(8,128)(2,1)}) custom-call(s32[1]{0:T(128)} %bitcast.1.half_ref, s32[6]{0:T(128)} %page_ref.1, s32[6]{0:T(128)} %target_ref.1, bf16[96,16,512]{2,1,0:T(8,128)(2,1)} %pool_ref.1, bf16[2,64,2048]{2,1,0:T(8,128)(2,1)} %bitcast.14, ...), custom_call_target="tpu_custom_call" | custom-call | flops 1024 | bytes 1024 | tf_op jit(solution)/shard_map/outgoing_pages/pallas_call | solution.py:104
  3.3 7.3 %all-to-all-start = ((bf16[16,16,512]{2,1,0:T(8,128)(2,1)}), bf16[16,16,512]{2,1,0:T(8,128)(2,1)S(1)}, u32[]{:S(2)}, u32[]{:S(2)}) async-start(bf16[16,16,512]{2,1,0:T(8,128)(2,1)} %get-tuple-element.26), calls=%async_computation | async-start | bytes 524288 | tf_op jit(solution)/shard_map/all_to_all | solution.py:570
  10.6 0.0 copy-done.2
  10.6 0.0 copy-done.3
  10.6 0.0 copy-done.7
  10.6 0.0 copy-done.8
  10.6 0.0 copy-start.4
  10.6 0.0 copy-start.6
  10.6 0.0 copy-start.9
  10.7 0.0 copy-start.10
  10.7 6.2 %attend_pool.1 = (bf16[2048,128]{1,0:T(8,128)(2,1)S(1)}, f32[128,256]{1,0:T(8,128)S(1)}) custom-call(bf16[128,2048]{1,0:T(8,128)(2,1)S(1)} %copy-done.3, bf16[1536,512]{1,0:T(8,128)(2,1)S(1)} %bitcast.16, s32[4,128]{1,0:T(4,128)S(1)} %bitcast.17, s32[1,128]{1,0:T(1,128)S(1)} %bitcast.19), custom_call_target="tpu_custom_call" | custom-call | flops 1000000000 | bytes 1000000 | tf_op jit(solution)/shard_map/attend_pool/pallas_call | solution.py:220
  16.8 0.0 copy-start.11
  16.8 2.7 %all-to-all-done.refs_1_ = bf16[16,16,512]{2,1,0:T(8,128)(2,1)S(1)} async-done(((bf16[16,16,512]{2,1,0:T(8,128)(2,1)}), bf16[16,16,512]{2,1,0:T(8,128)(2,1)S(1)}, u32[]{:S(2)}, u32[]{:S(2)}) %all-to-all-start) | async-done | bytes 262176 | tf_op jit(solution)/shard_map/all_to_all | solution.py:570
  19.5 0.0 copy-done.4
  19.5 0.0 copy-start.5
  19.5 1.2 %collective-permute-start.3 = (bf16[64,2048]{1,0:T(8,128)(2,1)S(1)}, bf16[64,2048]{1,0:T(8,128)(2,1)S(1)}, u32[]{:S(2)}, u32[]{:S(2)}) collective-permute-start(bf16[64,2048]{1,0:T(8,128)(2,1)S(1)} %after.5), channel_id=1, source_target_pairs={{0,12},{2,14},{4,8},{6,10},{8,4},{10,6},{12,0},{14,2},{16,28},{18,... | collective-permute-start | bytes 786440 | tf_op jit(solution)/shard_map/ppermute | solution.py:525
  20.8 0.1 pad_add_fusion.where_ref
  20.8 0.0 copy-done.6
  20.8 0.0 copy-done.9
  20.8 0.0 copy-done.10
  20.8 0.0 copy-start.1
  20.9 4.0 %finish.1 = (s32[1,128]{1,0:T(1,128)S(1)}, bf16[64,2176]{1,0:T(8,128)(2,1)S(1)}, bf16[64,2176]{1,0:T(8,128)(2,1)S(1)}, bf16[64,2176]{1,0:T(8,128)(2,1)S(1)}, bf16[64,2176]{1,0:T(8,128)(2,1)S(1)}) custom-call(s32[2]{0:T(128)S(1)} %pad_add_fusion.where_ref, bf16[128,2048]{1,0:T(8,128)(2,1)S(1)} %copy-done.3, bf16[2048,128]{1,0:T(8,128)(2,1)S(1)} %get-tuple-element.24.part_ref, ...), custom_call_target="tpu_custom_call" | custom-call | flops 1024 | bytes 1024 | tf_op jit(solution)/shard_map/finish/pallas_call | solution.py:338
  24.8 0.6 collective-permute-start.2
  25.5 1.3 %collective-permute-start = (bf16[64,2176]{1,0:T(8,128)(2,1)S(1)}, bf16[64,2176]{1,0:T(8,128)(2,1)S(1)}, u32[]{:S(2)}, u32[]{:S(2)}) collective-permute-start(bf16[64,2176]{1,0:T(8,128)(2,1)S(1)} %get-tuple-element.29), channel_id=1, source_target_pairs={{0,2},{2,0},{4,6},{6,4},{8,10},{10,8},{12,14},{14,12},{16,18},{18,... | collective-permute-start | bytes 835592 | tf_op jit(solution)/shard_map/ppermute | solution.py:525
  26.8 1.6 %collective-permute-start.1 = (bf16[64,2176]{1,0:T(8,128)(2,1)S(1)}, bf16[64,2176]{1,0:T(8,128)(2,1)S(1)}, u32[]{:S(2)}, u32[]{:S(2)}) collective-permute-start(bf16[64,2176]{1,0:T(8,128)(2,1)S(1)} %get-tuple-element.30), channel_id=1, source_target_pairs={{0,4},{2,6},{4,0},{6,2},{8,12},{10,14},{12,8},{14,10},{16,20},{18,... | collective-permute-start | bytes 835592 | tf_op jit(solution)/shard_map/ppermute | solution.py:525
  28.4 0.0 copy-done.11
  28.4 2.6 %collective-permute-start.6 = (bf16[64,2560]{1,0:T(8,128)(2,1)S(1)}, bf16[64,2560]{1,0:T(8,128)(2,1)S(1)}, u32[]{:S(2)}, u32[]{:S(2)}) collective-permute-start(bf16[64,2560]{1,0:T(8,128)(2,1)S(1)} %copy-done.11), channel_id=1, source_target_pairs={{0,12},{2,14},{4,8},{6,10},{8,4},{10,6},{12,0},{14,2},{16,28},{18,... | collective-permute-start | bytes 983048 | tf_op jit(solution)/shard_map/ppermute | solution.py:525
  31.0 0.0 collective-permute-done.3.refs_5_
  31.0 1.6 %collective-permute-start.4 = (bf16[64,2048]{1,0:T(8,128)(2,1)S(1)}, bf16[64,2048]{1,0:T(8,128)(2,1)S(1)}, u32[]{:S(2)}, u32[]{:S(2)}) collective-permute-start(bf16[64,2048]{1,0:T(8,128)(2,1)S(1)} %after.6), channel_id=1, source_target_pairs={{0,16},{2,18},{4,20},{6,22},{8,24},{10,26},{12,28},{14,30},{16,0},... | collective-permute-start | bytes 786440 | tf_op jit(solution)/shard_map/ppermute | solution.py:525
  32.6 3.2 %collective-permute-done.2.refs_3_.refs_1_ = bf16[64,2176]{1,0:T(8,128)(2,1)S(1)} collective-permute-done((bf16[64,2176]{1,0:T(8,128)(2,1)S(1)}, bf16[64,2176]{1,0:T(8,128)(2,1)S(1)}, u32[]{:S(2)}, u32[]{:S(2)}) %collective-permute-start.2) | collective-permute-done | bytes 278560 | tf_op jit(solution)/shard_map/ppermute | solution.py:525
  35.8 0.0 copy-done.5
  35.8 2.6 %collective-permute-start.7 = (bf16[64,1536]{1,0:T(8,128)(2,1)S(1)}, bf16[64,1536]{1,0:T(8,128)(2,1)S(1)}, u32[]{:S(2)}, u32[]{:S(2)}) collective-permute-start(bf16[64,1536]{1,0:T(8,128)(2,1)S(1)} %after.7), channel_id=1, source_target_pairs={{0,12},{2,14},{4,8},{6,10},{8,4},{10,6},{12,0},{14,2},{16,28},{18,... | collective-permute-start | bytes 589832 | tf_op jit(solution)/shard_map/ppermute | solution.py:525
  38.5 0.3 collective-permute-done.refs_1_
  38.7 12.8 %collective-permute-done.1.refs_2_ = bf16[64,2176]{1,0:T(8,128)(2,1)S(1)} collective-permute-done((bf16[64,2176]{1,0:T(8,128)(2,1)S(1)}, bf16[64,2176]{1,0:T(8,128)(2,1)S(1)}, u32[]{:S(2)}, u32[]{:S(2)}) %collective-permute-start.1) | collective-permute-done | bytes 278560 | tf_op jit(solution)/shard_map/ppermute | solution.py:525
  51.5 0.0 collective-permute-done.4.refs_6_
  51.5 0.0 copy-done.1
  51.5 0.5 low_products.1.mine_ref
  52.0 0.1 collective-permute-start.5
  52.1 0.0 collective-permute-done.6.refs_0_
  52.1 1.6 %collective-permute-start.8 = (bf16[64,2560]{1,0:T(8,128)(2,1)S(1)}, bf16[64,2560]{1,0:T(8,128)(2,1)S(1)}, u32[]{:S(2)}, u32[]{:S(2)}) collective-permute-start(bf16[64,2560]{1,0:T(8,128)(2,1)S(1)} %after.8), channel_id=1, source_target_pairs={{0,16},{2,18},{4,20},{6,22},{8,24},{10,26},{12,28},{14,30},{16,0},... | collective-permute-start | bytes 983048 | tf_op jit(solution)/shard_map/ppermute | solution.py:525
  53.7 0.0 collective-permute-done.5.other_ref.refs_1_
  53.7 0.0 copy-done
  53.7 0.4 lift_own.1
  54.1 1.1 %collective-permute-start.10 = (bf16[32,4096]{1,0:T(8,128)(2,1)S(1)}, bf16[32,4096]{1,0:T(8,128)(2,1)S(1)}, u32[]{:S(2)}, u32[]{:S(2)}) collective-permute-start(bf16[32,4096]{1,0:T(8,128)(2,1)S(1)} %get-tuple-element.37), channel_id=1, source_target_pairs={{0,2},{2,0},{4,6},{6,4},{8,10},{10,8},{12,14},{14,12},{16,18},{18,... | collective-permute-start | bytes 786440 | tf_op jit(solution)/shard_map/ppermute | solution.py:525
  55.2 0.0 collective-permute-done.7.refs_1_
  55.3 1.3 %collective-permute-start.9 = (bf16[64,1536]{1,0:T(8,128)(2,1)S(1)}, bf16[64,1536]{1,0:T(8,128)(2,1)S(1)}, u32[]{:S(2)}, u32[]{:S(2)}) collective-permute-start(bf16[64,1536]{1,0:T(8,128)(2,1)S(1)} %after.9), channel_id=1, source_target_pairs={{0,16},{2,18},{4,20},{6,22},{8,24},{10,26},{12,28},{14,30},{16,0},... | collective-permute-start | bytes 589832 | tf_op jit(solution)/shard_map/ppermute | solution.py:525
  56.6 0.0 collective-permute-start.12
  56.6 2.4 %collective-permute-start.14 = (bf16[32,4096]{1,0:T(8,128)(2,1)S(1)}, bf16[32,4096]{1,0:T(8,128)(2,1)S(1)}, u32[]{:S(2)}, u32[]{:S(2)}) collective-permute-start(bf16[32,4096]{1,0:T(8,128)(2,1)S(1)} %get-tuple-element.41), channel_id=1, source_target_pairs={{0,6},{2,4},{4,2},{6,0},{8,14},{10,12},{12,10},{14,8},{16,22},{18,... | collective-permute-start | bytes 786440 | tf_op jit(solution)/shard_map/ppermute | solution.py:525
  59.0 3.7 %collective-permute-done.8.refs_2_ = bf16[64,2560]{1,0:T(8,128)(2,1)S(1)} collective-permute-done((bf16[64,2560]{1,0:T(8,128)(2,1)S(1)}, bf16[64,2560]{1,0:T(8,128)(2,1)S(1)}, u32[]{:S(2)}, u32[]{:S(2)}) %collective-permute-start.8) | collective-permute-done | bytes 327712 | tf_op jit(solution)/shard_map/ppermute | solution.py:525
  62.7 3.8 %collective-permute-done.9.refs_3_ = bf16[64,1536]{1,0:T(8,128)(2,1)S(1)} collective-permute-done((bf16[64,1536]{1,0:T(8,128)(2,1)S(1)}, bf16[64,1536]{1,0:T(8,128)(2,1)S(1)}, u32[]{:S(2)}, u32[]{:S(2)}) %collective-permute-start.9) | collective-permute-done | bytes 196640 | tf_op jit(solution)/shard_map/ppermute | solution.py:525
  66.5 0.4 lift_far.1
  66.9 1.1 %collective-permute-start.11 = (bf16[32,4096]{1,0:T(8,128)(2,1)S(1)}, bf16[32,4096]{1,0:T(8,128)(2,1)S(1)}, u32[]{:S(2)}, u32[]{:S(2)}) collective-permute-start(bf16[32,4096]{1,0:T(8,128)(2,1)S(1)} %get-tuple-element.38), channel_id=1, source_target_pairs={{0,2},{2,0},{4,6},{6,4},{8,10},{10,8},{12,14},{14,12},{16,18},{18,... | collective-permute-start | bytes 786440 | tf_op jit(solution)/shard_map/ppermute | solution.py:525
  68.0 0.0 collective-permute-start.13
  68.0 0.0 collective-permute-done.10.refs_2_
  68.0 2.4 %collective-permute-start.15 = (bf16[32,4096]{1,0:T(8,128)(2,1)S(1)}, bf16[32,4096]{1,0:T(8,128)(2,1)S(1)}, u32[]{:S(2)}, u32[]{:S(2)}) collective-permute-start(bf16[32,4096]{1,0:T(8,128)(2,1)S(1)} %get-tuple-element.42), channel_id=1, source_target_pairs={{0,6},{2,4},{4,2},{6,0},{8,14},{10,12},{12,10},{14,8},{16,22},{18,... | collective-permute-start | bytes 786440 | tf_op jit(solution)/shard_map/ppermute | solution.py:525
  70.5 0.0 collective-permute-done.12.refs_4_
  70.5 0.0 collective-permute-done.14.refs_6_
  70.5 7.0 %collective-permute-done.11.refs_3_ = bf16[32,4096]{1,0:T(8,128)(2,1)S(1)} collective-permute-done((bf16[32,4096]{1,0:T(8,128)(2,1)S(1)}, bf16[32,4096]{1,0:T(8,128)(2,1)S(1)}, u32[]{:S(2)}, u32[]{:S(2)}) %collective-permute-start.11) | collective-permute-done | bytes 262176 | tf_op jit(solution)/shard_map/ppermute | solution.py:525
  77.5 0.0 collective-permute-done.13.refs_5_
  77.5 4.2 %collective-permute-done.15.refs_7_ = bf16[32,4096]{1,0:T(8,128)(2,1)S(1)} collective-permute-done((bf16[32,4096]{1,0:T(8,128)(2,1)S(1)}, bf16[32,4096]{1,0:T(8,128)(2,1)S(1)}, u32[]{:S(2)}, u32[]{:S(2)}) %collective-permute-start.15) | collective-permute-done | bytes 262176 | tf_op jit(solution)/shard_map/ppermute | solution.py:525
  81.7 1.5 %gather_rows.1 = bf16[128,4096]{1,0:T(8,128)(2,1)} custom-call(s32[1,128]{1,0:T(1,128)S(1)} %get-tuple-element.27.refs_1_.slot_ref, bf16[32,4096]{1,0:T(8,128)(2,1)S(1)} %get-tuple-element.33.refs_0_, bf16[32,4096]{1,0:T(8,128)(2,1)S(1)} %get-tuple-element.36.refs_1_, bf16[32,4096]{1,0:T(8,128)(2,1)S(1)} %collective-permute-done.10.refs_2_, ...), custom_call_target="tpu_custom_call" | custom-call | flops 1024 | bytes 1024 | tf_op jit(solution)/shard_map/gather_rows/pallas_call | solution.py:505
  (10 shorter events, 0.1 us)
Async XLA Ops:
  0.0 10.6 %copy-start.2 = (bf16[96,16,512]{2,1,0:T(8,128)(2,1)S(1)}, bf16[96,16,512]{2,1,0:T(8,128)(2,1)}, u32[]{:S(2)}) copy-start(bf16[96,16,512]{2,1,0:T(8,128)(2,1)} %pool_ref.1) | copy-start | bytes 4718596
  0.0 10.6 %copy-start.3 = (bf16[128,2048]{1,0:T(8,128)(2,1)S(1)}, bf16[128,2048]{1,0:T(8,128)(2,1)}, u32[]{:S(2)}) copy-start(bf16[128,2048]{1,0:T(8,128)(2,1)} %query_ref.3) | copy-start | bytes 1572868
  0.0 10.6 %copy-start.7 = (s32[128,4]{0,1:T(4,128)S(1)}, s32[128,4]{0,1:T(4,128)}, u32[]{:S(2)}) copy-start(s32[128,4]{0,1:T(4,128)} %param.14) | copy-start | bytes 6148
  0.0 10.6 %copy-start.8 = (s32[128]{0:T(128)S(1)}, s32[128]{0:T(128)}, u32[]{:S(2)}) copy-start(s32[128]{0:T(128)} %param.15) | copy-start | bytes 1540
  3.3 16.2 %all-to-all-start = ((bf16[16,16,512]{2,1,0:T(8,128)(2,1)}), bf16[16,16,512]{2,1,0:T(8,128)(2,1)S(1)}, u32[]{:S(2)}, u32[]{:S(2)}) async-start(bf16[16,16,512]{2,1,0:T(8,128)(2,1)} %get-tuple-element.26), calls=%async_computation | async-start | bytes 524288 | tf_op jit(solution)/shard_map/all_to_all | solution.py:570
  10.6 8.9 %copy-start.4 = (bf16[64,2048]{1,0:T(8,128)(2,1)S(1)}, bf16[64,2048]{1,0:T(8,128)(2,1)}, u32[]{:S(2)}) copy-start(bf16[64,2048]{1,0:T(8,128)(2,1)} %get-tuple-element.32.refs_0_) | copy-start | bytes 786436
  10.6 10.2 %copy-start.6 = (bf16[128,512]{1,0:T(8,128)(2,1)S(1)}, bf16[128,512]{1,0:T(8,128)(2,1)}, u32[]{:S(2)}) copy-start(bf16[128,512]{1,0:T(8,128)(2,1)} %fresh_ref.1) | copy-start | bytes 393220
  10.6 10.2 %copy-start.9 = (s32[128,1]{0,1:T(1,128)S(1)}, s32[128,1]{0,1:T(1,128)}, u32[]{:S(2)}) copy-start(s32[128,1]{0,1:T(1,128)} %param.18) | copy-start | bytes 1540
  10.7 10.2 %copy-start.10 = (s32[128]{0:T(128)S(1)}, s32[128]{0:T(128)}, u32[]{:S(2)}) copy-start(s32[128]{0:T(128)} %param.19) | copy-start | bytes 1540
  16.8 11.6 %copy-start.11 = (bf16[64,2560]{1,0:T(8,128)(2,1)S(1)}, bf16[64,2560]{1,0:T(8,128)(2,1)}, u32[]{:S(2)}) copy-start(bf16[64,2560]{1,0:T(8,128)(2,1)} %get-tuple-element.34) | copy-start | bytes 983044
  19.5 16.3 %copy-start.5 = (bf16[64,1536]{1,0:T(8,128)(2,1)S(1)}, bf16[64,1536]{1,0:T(8,128)(2,1)}, u32[]{:S(2)}) copy-start(bf16[64,1536]{1,0:T(8,128)(2,1)} %get-tuple-element.35.refs_0_) | copy-start | bytes 589828
  19.5 11.5 %collective-permute-start.3 = (bf16[64,2048]{1,0:T(8,128)(2,1)S(1)}, bf16[64,2048]{1,0:T(8,128)(2,1)S(1)}, u32[]{:S(2)}, u32[]{:S(2)}) collective-permute-start(bf16[64,2048]{1,0:T(8,128)(2,1)S(1)} %after.5), channel_id=1, source_target_pairs={{0,12},{2,14},{4,8},{6,10},{8,4},{10,6},{12,0},{14,2},{16,28},{18,... | collective-permute-start | bytes 786440 | tf_op jit(solution)/shard_map/ppermute | solution.py:525
  20.8 30.7 %copy-start.1 = (bf16[2,2048,64]{1,2,0:T(8,128)(2,1)S(1)}, bf16[2,2048,64]{1,2,0:T(8,128)(2,1)}, u32[]{:S(2)}) copy-start(bf16[2,2048,64]{1,2,0:T(8,128)(2,1)} %param.20) | copy-start | bytes 1572868
  24.8 11.0 %collective-permute-start.2 = (bf16[64,2176]{1,0:T(8,128)(2,1)S(1)}, bf16[64,2176]{1,0:T(8,128)(2,1)S(1)}, u32[]{:S(2)}, u32[]{:S(2)}) collective-permute-start(bf16[64,2176]{1,0:T(8,128)(2,1)S(1)} %get-tuple-element.31), channel_id=1, source_target_pairs={{0,6},{2,4},{4,2},{6,0},{8,14},{10,12},{12,10},{14,8},{16,22},{18,... | collective-permute-start | bytes 835592 | tf_op jit(solution)/shard_map/ppermute | solution.py:525
  25.5 13.2 %collective-permute-start = (bf16[64,2176]{1,0:T(8,128)(2,1)S(1)}, bf16[64,2176]{1,0:T(8,128)(2,1)S(1)}, u32[]{:S(2)}, u32[]{:S(2)}) collective-permute-start(bf16[64,2176]{1,0:T(8,128)(2,1)S(1)} %get-tuple-element.29), channel_id=1, source_target_pairs={{0,2},{2,0},{4,6},{6,4},{8,10},{10,8},{12,14},{14,12},{16,18},{18,... | collective-permute-start | bytes 835592 | tf_op jit(solution)/shard_map/ppermute | solution.py:525
  26.8 24.8 %collective-permute-start.1 = (bf16[64,2176]{1,0:T(8,128)(2,1)S(1)}, bf16[64,2176]{1,0:T(8,128)(2,1)S(1)}, u32[]{:S(2)}, u32[]{:S(2)}) collective-permute-start(bf16[64,2176]{1,0:T(8,128)(2,1)S(1)} %get-tuple-element.30), channel_id=1, source_target_pairs={{0,4},{2,6},{4,0},{6,2},{8,12},{10,14},{12,8},{14,10},{16,20},{18,... | collective-permute-start | bytes 835592 | tf_op jit(solution)/shard_map/ppermute | solution.py:525
  28.4 23.7 %collective-permute-start.6 = (bf16[64,2560]{1,0:T(8,128)(2,1)S(1)}, bf16[64,2560]{1,0:T(8,128)(2,1)S(1)}, u32[]{:S(2)}, u32[]{:S(2)}) collective-permute-start(bf16[64,2560]{1,0:T(8,128)(2,1)S(1)} %copy-done.11), channel_id=1, source_target_pairs={{0,12},{2,14},{4,8},{6,10},{8,4},{10,6},{12,0},{14,2},{16,28},{18,... | collective-permute-start | bytes 983048 | tf_op jit(solution)/shard_map/ppermute | solution.py:525
  31.0 20.5 %collective-permute-start.4 = (bf16[64,2048]{1,0:T(8,128)(2,1)S(1)}, bf16[64,2048]{1,0:T(8,128)(2,1)S(1)}, u32[]{:S(2)}, u32[]{:S(2)}) collective-permute-start(bf16[64,2048]{1,0:T(8,128)(2,1)S(1)} %after.6), channel_id=1, source_target_pairs={{0,16},{2,18},{4,20},{6,22},{8,24},{10,26},{12,28},{14,30},{16,0},... | collective-permute-start | bytes 786440 | tf_op jit(solution)/shard_map/ppermute | solution.py:525
  35.8 19.4 %collective-permute-start.7 = (bf16[64,1536]{1,0:T(8,128)(2,1)S(1)}, bf16[64,1536]{1,0:T(8,128)(2,1)S(1)}, u32[]{:S(2)}, u32[]{:S(2)}) collective-permute-start(bf16[64,1536]{1,0:T(8,128)(2,1)S(1)} %after.7), channel_id=1, source_target_pairs={{0,12},{2,14},{4,8},{6,10},{8,4},{10,6},{12,0},{14,2},{16,28},{18,... | collective-permute-start | bytes 589832 | tf_op jit(solution)/shard_map/ppermute | solution.py:525
  51.5 2.2 %copy-start = (bf16[2,64,4096]{2,1,0:T(8,128)(2,1)S(1)}, bf16[2,64,4096]{2,1,0:T(8,128)(2,1)}, u32[]{:S(2)}) copy-start(bf16[2,64,4096]{2,1,0:T(8,128)(2,1)} %refs_1_.1) | copy-start | bytes 3145732
  52.0 1.7 %collective-permute-start.5 = (f32[256,128]{1,0:T(8,128)S(1)}, f32[256,128]{1,0:T(8,128)S(1)}, u32[]{:S(2)}, u32[]{:S(2)}) collective-permute-start(f32[256,128]{1,0:T(8,128)S(1)} %low_products.1.mine_ref), channel_id=1, source_target_pairs={{0,1},{1,0},{2,3},{3,2},{4,5},{5,4},{6,7},{7,6},{8,9},{9,8},{10,11... | collective-permute-start | bytes 393224 | tf_op jit(solution)/shard_map/ppermute | solution.py:599
  52.1 10.6 %collective-permute-start.8 = (bf16[64,2560]{1,0:T(8,128)(2,1)S(1)}, bf16[64,2560]{1,0:T(8,128)(2,1)S(1)}, u32[]{:S(2)}, u32[]{:S(2)}) collective-permute-start(bf16[64,2560]{1,0:T(8,128)(2,1)S(1)} %after.8), channel_id=1, source_target_pairs={{0,16},{2,18},{4,20},{6,22},{8,24},{10,26},{12,28},{14,30},{16,0},... | collective-permute-start | bytes 983048 | tf_op jit(solution)/shard_map/ppermute | solution.py:525
  54.1 13.9 %collective-permute-start.10 = (bf16[32,4096]{1,0:T(8,128)(2,1)S(1)}, bf16[32,4096]{1,0:T(8,128)(2,1)S(1)}, u32[]{:S(2)}, u32[]{:S(2)}) collective-permute-start(bf16[32,4096]{1,0:T(8,128)(2,1)S(1)} %get-tuple-element.37), channel_id=1, source_target_pairs={{0,2},{2,0},{4,6},{6,4},{8,10},{10,8},{12,14},{14,12},{16,18},{18,... | collective-permute-start | bytes 786440 | tf_op jit(solution)/shard_map/ppermute | solution.py:525
  55.3 11.2 %collective-permute-start.9 = (bf16[64,1536]{1,0:T(8,128)(2,1)S(1)}, bf16[64,1536]{1,0:T(8,128)(2,1)S(1)}, u32[]{:S(2)}, u32[]{:S(2)}) collective-permute-start(bf16[64,1536]{1,0:T(8,128)(2,1)S(1)} %after.9), channel_id=1, source_target_pairs={{0,16},{2,18},{4,20},{6,22},{8,24},{10,26},{12,28},{14,30},{16,0},... | collective-permute-start | bytes 589832 | tf_op jit(solution)/shard_map/ppermute | solution.py:525
  56.6 13.9 %collective-permute-start.12 = (bf16[32,4096]{1,0:T(8,128)(2,1)S(1)}, bf16[32,4096]{1,0:T(8,128)(2,1)S(1)}, u32[]{:S(2)}, u32[]{:S(2)}) collective-permute-start(bf16[32,4096]{1,0:T(8,128)(2,1)S(1)} %get-tuple-element.39), channel_id=1, source_target_pairs={{0,4},{2,6},{4,0},{6,2},{8,12},{10,14},{12,8},{14,10},{16,20},{18,... | collective-permute-start | bytes 786440 | tf_op jit(solution)/shard_map/ppermute | solution.py:525
  56.6 13.9 %collective-permute-start.14 = (bf16[32,4096]{1,0:T(8,128)(2,1)S(1)}, bf16[32,4096]{1,0:T(8,128)(2,1)S(1)}, u32[]{:S(2)}, u32[]{:S(2)}) collective-permute-start(bf16[32,4096]{1,0:T(8,128)(2,1)S(1)} %get-tuple-element.41), channel_id=1, source_target_pairs={{0,6},{2,4},{4,2},{6,0},{8,14},{10,12},{12,10},{14,8},{16,22},{18,... | collective-permute-start | bytes 786440 | tf_op jit(solution)/shard_map/ppermute | solution.py:525
  66.9 10.6 %collective-permute-start.11 = (bf16[32,4096]{1,0:T(8,128)(2,1)S(1)}, bf16[32,4096]{1,0:T(8,128)(2,1)S(1)}, u32[]{:S(2)}, u32[]{:S(2)}) collective-permute-start(bf16[32,4096]{1,0:T(8,128)(2,1)S(1)} %get-tuple-element.38), channel_id=1, source_target_pairs={{0,2},{2,0},{4,6},{6,4},{8,10},{10,8},{12,14},{14,12},{16,18},{18,... | collective-permute-start | bytes 786440 | tf_op jit(solution)/shard_map/ppermute | solution.py:525
  68.0 9.5 %collective-permute-start.13 = (bf16[32,4096]{1,0:T(8,128)(2,1)S(1)}, bf16[32,4096]{1,0:T(8,128)(2,1)S(1)}, u32[]{:S(2)}, u32[]{:S(2)}) collective-permute-start(bf16[32,4096]{1,0:T(8,128)(2,1)S(1)} %get-tuple-element.40), channel_id=1, source_target_pairs={{0,4},{2,6},{4,0},{6,2},{8,12},{10,14},{12,8},{14,10},{16,20},{18,... | collective-permute-start | bytes 786440 | tf_op jit(solution)/shard_map/ppermute | solution.py:525
  68.0 13.7 %collective-permute-start.15 = (bf16[32,4096]{1,0:T(8,128)(2,1)S(1)}, bf16[32,4096]{1,0:T(8,128)(2,1)S(1)}, u32[]{:S(2)}, u32[]{:S(2)}) collective-permute-start(bf16[32,4096]{1,0:T(8,128)(2,1)S(1)} %get-tuple-element.42), channel_id=1, source_target_pairs={{0,6},{2,4},{4,2},{6,0},{8,14},{10,12},{12,10},{14,8},{16,22},{18,... | collective-permute-start | bytes 786440 | tf_op jit(solution)/shard_map/ppermute | solution.py:525

commit v6 on v5

--- a/solution.py
+++ b/solution.py
@@ -599,9 +599,9 @@
     other = lax.ppermute(mine, "tp", [(0, 1), (1, 0)])
     second.append(along(*after([first[2]], other), 1, 0))
     own = lift_own(mine, other, up)
-    own = [block if b == 0 else along(block, 0, b) for b, block in enumerate(own)]
+    own = [own[0], *[along(own[b], 0, b) for b in (3, 2, 1)][::-1]]
     far = lift_far(half, mine, other, first[1:], second[1:])
-    far = [block if b == 0 else along(block, 0, b) for b, block in enumerate(far)]
+    far = [far[0], *[along(far[b], 0, b) for b in (3, 2, 1)][::-1]]
     return gather_rows(slots, [block for pair in zip(own, far) for block in pair])
 
 

time: 83.5 us -> 83.5 us (level)
  no operation moved by 1% of the time
where the time goes in v6:
time: 83.5 us; the launch traced here: 83.2 us
  waiting for transfers between devices  37.7 us (45%)
  starting transfers between devices  28.8 us (34%)
  Pallas kernels  16.3 us (20%)
    ppermute x15, waiting for transfers between devices, along(): return lax.ppermute(array, ('group', 'rep'), pairs)  35.1 us
    ppermute x15, starting transfers between devices, along(): return lax.ppermute(array, ('group', 'rep'), pairs)  21.5 us
    all_to_all x1, starting transfers between devices, shared_local(): lax.all_to_all(outgoing, 'rep', split_axis=0, concat_axis=0, tiled=True)  7.26 us
    pallas_call x1, Pallas kernels, attend_pool(): pl.pallas_call(functools.partial(pool_kernel, page_len), grid=(kv_local,)...  6.16 us
    pallas_call x1, Pallas kernels, finish(): pl.pallas_call(functools.partial(finish_kernel, page_len, first_token, pl...  3.99 us
    pallas_call x1, Pallas kernels, outgoing_pages(): pl.pallas_call(functools.partial(outgoing_kernel, pieces), out_shape=out_...  3.33 us
    all_to_all x1, waiting for transfers between devices, shared_local(): lax.all_to_all(outgoing, 'rep', split_axis=0, concat_axis=0, tiled=True)  2.66 us
  transfers between devices with their start and end apart: 17, of which 8 were waited for; matrix products, arithmetic and copies ran while one was open for 0% of the time, Pallas kernels for 14%

profile of v6, /device:TPU:0, one launch (start us, length us, event | category | flops | bytes accessed | tf_op | source)
XLA Modules:
  0.0 83.2 jit_solution(17641168712916514420)
XLA Ops:
  0.0 0.0 copy-start.2
  0.0 0.0 copy-start.3
  0.0 0.0 copy-start.7
  0.0 0.0 copy-start.8
  0.0 3.3 %outgoing_pages.1 = (bf16[16,16,512]{2,1,0:T(8,128)(2,1)}, bf16[64,2048]{1,0:T(8,128)(2,1)}, bf16[64,2560]{1,0:T(8,128)(2,1)}, bf16[64,1536]{1,0:T(8,128)(2,1)}) custom-call(s32[1]{0:T(128)} %bitcast.1.half_ref, s32[6]{0:T(128)} %page_ref.1, s32[6]{0:T(128)} %target_ref.1, bf16[96,16,512]{2,1,0:T(8,128)(2,1)} %pool_ref.1, bf16[2,64,2048]{2,1,0:T(8,128)(2,1)} %bitcast.14, ...), custom_call_target="tpu_custom_call" | custom-call | flops 1024 | bytes 1024 | tf_op jit(solution)/shard_map/outgoing_pages/pallas_call | solution.py:104
  3.3 7.3 %all-to-all-start = ((bf16[16,16,512]{2,1,0:T(8,128)(2,1)}), bf16[16,16,512]{2,1,0:T(8,128)(2,1)S(1)}, u32[]{:S(2)}, u32[]{:S(2)}) async-start(bf16[16,16,512]{2,1,0:T(8,128)(2,1)} %get-tuple-element.26), calls=%async_computation | async-start | bytes 524288 | tf_op jit(solution)/shard_map/all_to_all | solution.py:570
  10.6 0.0 copy-done.2
  10.6 0.0 copy-done.3
  10.6 0.0 copy-done.7
  10.6 0.0 copy-done.8
  10.6 0.0 copy-start.4
  10.7 0.0 copy-start.6
  10.7 0.0 copy-start.9
  10.7 0.0 copy-start.10
  10.7 6.2 %attend_pool.1 = (bf16[2048,128]{1,0:T(8,128)(2,1)S(1)}, f32[128,256]{1,0:T(8,128)S(1)}) custom-call(bf16[128,2048]{1,0:T(8,128)(2,1)S(1)} %copy-done.3, bf16[1536,512]{1,0:T(8,128)(2,1)S(1)} %bitcast.16, s32[4,128]{1,0:T(4,128)S(1)} %bitcast.17, s32[1,128]{1,0:T(1,128)S(1)} %bitcast.19), custom_call_target="tpu_custom_call" | custom-call | flops 1000000000 | bytes 1000000 | tf_op jit(solution)/shard_map/attend_pool/pallas_call | solution.py:220
  16.9 0.0 copy-start.11
  16.9 2.7 %all-to-all-done.refs_1_ = bf16[16,16,512]{2,1,0:T(8,128)(2,1)S(1)} async-done(((bf16[16,16,512]{2,1,0:T(8,128)(2,1)}), bf16[16,16,512]{2,1,0:T(8,128)(2,1)S(1)}, u32[]{:S(2)}, u32[]{:S(2)}) %all-to-all-start) | async-done | bytes 262176 | tf_op jit(solution)/shard_map/all_to_all | solution.py:570
  19.5 0.0 copy-done.4
  19.5 0.0 copy-start.5
  19.5 1.2 %collective-permute-start.3 = (bf16[64,2048]{1,0:T(8,128)(2,1)S(1)}, bf16[64,2048]{1,0:T(8,128)(2,1)S(1)}, u32[]{:S(2)}, u32[]{:S(2)}) collective-permute-start(bf16[64,2048]{1,0:T(8,128)(2,1)S(1)} %after.5), channel_id=1, source_target_pairs={{0,12},{2,14},{4,8},{6,10},{8,4},{10,6},{12,0},{14,2},{16,28},{18,... | collective-permute-start | bytes 786440 | tf_op jit(solution)/shard_map/ppermute | solution.py:525
  20.8 0.1 pad_add_fusion.where_ref
  20.9 0.0 copy-done.6
  20.9 0.0 copy-done.9
  20.9 0.0 copy-done.10
  20.9 4.0 %finish.1 = (s32[1,128]{1,0:T(1,128)S(1)}, bf16[64,2176]{1,0:T(8,128)(2,1)S(1)}, bf16[64,2176]{1,0:T(8,128)(2,1)S(1)}, bf16[64,2176]{1,0:T(8,128)(2,1)S(1)}, bf16[64,2176]{1,0:T(8,128)(2,1)S(1)}) custom-call(s32[2]{0:T(128)S(1)} %pad_add_fusion.where_ref, bf16[128,2048]{1,0:T(8,128)(2,1)S(1)} %copy-done.3, bf16[2048,128]{1,0:T(8,128)(2,1)S(1)} %get-tuple-element.24.part_ref, ...), custom_call_target="tpu_custom_call" | custom-call | flops 1024 | bytes 1024 | tf_op jit(solution)/shard_map/finish/pallas_call | solution.py:338
  24.9 0.6 collective-permute-start.2
  25.5 1.3 %collective-permute-start = (bf16[64,2176]{1,0:T(8,128)(2,1)S(1)}, bf16[64,2176]{1,0:T(8,128)(2,1)S(1)}, u32[]{:S(2)}, u32[]{:S(2)}) collective-permute-start(bf16[64,2176]{1,0:T(8,128)(2,1)S(1)} %get-tuple-element.29), channel_id=1, source_target_pairs={{0,2},{2,0},{4,6},{6,4},{8,10},{10,8},{12,14},{14,12},{16,18},{18,... | collective-permute-start | bytes 835592 | tf_op jit(solution)/shard_map/ppermute | solution.py:525
  26.8 1.7 %collective-permute-start.1 = (bf16[64,2176]{1,0:T(8,128)(2,1)S(1)}, bf16[64,2176]{1,0:T(8,128)(2,1)S(1)}, u32[]{:S(2)}, u32[]{:S(2)}) collective-permute-start(bf16[64,2176]{1,0:T(8,128)(2,1)S(1)} %get-tuple-element.30), channel_id=1, source_target_pairs={{0,4},{2,6},{4,0},{6,2},{8,12},{10,14},{12,8},{14,10},{16,20},{18,... | collective-permute-start | bytes 835592 | tf_op jit(solution)/shard_map/ppermute | solution.py:525
  28.4 0.0 copy-done.11
  28.4 2.6 %collective-permute-start.6 = (bf16[64,2560]{1,0:T(8,128)(2,1)S(1)}, bf16[64,2560]{1,0:T(8,128)(2,1)S(1)}, u32[]{:S(2)}, u32[]{:S(2)}) collective-permute-start(bf16[64,2560]{1,0:T(8,128)(2,1)S(1)} %copy-done.11), channel_id=1, source_target_pairs={{0,12},{2,14},{4,8},{6,10},{8,4},{10,6},{12,0},{14,2},{16,28},{18,... | collective-permute-start | bytes 983048 | tf_op jit(solution)/shard_map/ppermute | solution.py:525
  31.0 0.0 collective-permute-done.3.refs_5_
  31.0 1.6 %collective-permute-start.4 = (bf16[64,2048]{1,0:T(8,128)(2,1)S(1)}, bf16[64,2048]{1,0:T(8,128)(2,1)S(1)}, u32[]{:S(2)}, u32[]{:S(2)}) collective-permute-start(bf16[64,2048]{1,0:T(8,128)(2,1)S(1)} %after.6), channel_id=1, source_target_pairs={{0,16},{2,18},{4,20},{6,22},{8,24},{10,26},{12,28},{14,30},{16,0},... | collective-permute-start | bytes 786440 | tf_op jit(solution)/shard_map/ppermute | solution.py:525
  32.6 3.3 %collective-permute-done.2.refs_3_.refs_1_ = bf16[64,2176]{1,0:T(8,128)(2,1)S(1)} collective-permute-done((bf16[64,2176]{1,0:T(8,128)(2,1)S(1)}, bf16[64,2176]{1,0:T(8,128)(2,1)S(1)}, u32[]{:S(2)}, u32[]{:S(2)}) %collective-permute-start.2) | collective-permute-done | bytes 278560 | tf_op jit(solution)/shard_map/ppermute | solution.py:525
  35.8 0.0 copy-done.5
  35.9 2.6 %collective-permute-start.7 = (bf16[64,1536]{1,0:T(8,128)(2,1)S(1)}, bf16[64,1536]{1,0:T(8,128)(2,1)S(1)}, u32[]{:S(2)}, u32[]{:S(2)}) collective-permute-start(bf16[64,1536]{1,0:T(8,128)(2,1)S(1)} %after.7), channel_id=1, source_target_pairs={{0,12},{2,14},{4,8},{6,10},{8,4},{10,6},{12,0},{14,2},{16,28},{18,... | collective-permute-start | bytes 589832 | tf_op jit(solution)/shard_map/ppermute | solution.py:525
  38.5 0.3 collective-permute-done.refs_1_
  38.7 12.8 %collective-permute-done.1.refs_2_ = bf16[64,2176]{1,0:T(8,128)(2,1)S(1)} collective-permute-done((bf16[64,2176]{1,0:T(8,128)(2,1)S(1)}, bf16[64,2176]{1,0:T(8,128)(2,1)S(1)}, u32[]{:S(2)}, u32[]{:S(2)}) %collective-permute-start.1) | collective-permute-done | bytes 278560 | tf_op jit(solution)/shard_map/ppermute | solution.py:525
  51.5 0.0 collective-permute-done.4.refs_6_
  51.5 0.0 copy-done.1
  51.5 0.5 low_products.1.mine_ref
  52.0 0.1 collective-permute-start.5
  52.1 0.0 collective-permute-done.6.refs_0_
  52.1 1.5 %collective-permute-start.8 = (bf16[64,2560]{1,0:T(8,128)(2,1)S(1)}, bf16[64,2560]{1,0:T(8,128)(2,1)S(1)}, u32[]{:S(2)}, u32[]{:S(2)}) collective-permute-start(bf16[64,2560]{1,0:T(8,128)(2,1)S(1)} %after.8), channel_id=1, source_target_pairs={{0,16},{2,18},{4,20},{6,22},{8,24},{10,26},{12,28},{14,30},{16,0},... | collective-permute-start | bytes 983048 | tf_op jit(solution)/shard_map/ppermute | solution.py:525
  53.7 0.0 collective-permute-done.5.other_ref.refs_1_
  53.7 0.0 copy-done
  53.7 0.4 lift_own.1
  54.1 1.1 %collective-permute-start.10 = (bf16[32,4096]{1,0:T(8,128)(2,1)S(1)}, bf16[32,4096]{1,0:T(8,128)(2,1)S(1)}, u32[]{:S(2)}, u32[]{:S(2)}) collective-permute-start(bf16[32,4096]{1,0:T(8,128)(2,1)S(1)} %get-tuple-element.37), channel_id=1, source_target_pairs={{0,2},{2,0},{4,6},{6,4},{8,10},{10,8},{12,14},{14,12},{16,18},{18,... | collective-permute-start | bytes 786440 | tf_op jit(solution)/shard_map/ppermute | solution.py:525
  55.2 0.0 collective-permute-done.7.refs_1_
  55.3 1.3 %collective-permute-start.9 = (bf16[64,1536]{1,0:T(8,128)(2,1)S(1)}, bf16[64,1536]{1,0:T(8,128)(2,1)S(1)}, u32[]{:S(2)}, u32[]{:S(2)}) collective-permute-start(bf16[64,1536]{1,0:T(8,128)(2,1)S(1)} %after.9), channel_id=1, source_target_pairs={{0,16},{2,18},{4,20},{6,22},{8,24},{10,26},{12,28},{14,30},{16,0},... | collective-permute-start | bytes 589832 | tf_op jit(solution)/shard_map/ppermute | solution.py:525
  56.5 0.0 collective-permute-start.12
  56.6 2.4 %collective-permute-start.14 = (bf16[32,4096]{1,0:T(8,128)(2,1)S(1)}, bf16[32,4096]{1,0:T(8,128)(2,1)S(1)}, u32[]{:S(2)}, u32[]{:S(2)}) collective-permute-start(bf16[32,4096]{1,0:T(8,128)(2,1)S(1)} %get-tuple-element.41), channel_id=1, source_target_pairs={{0,6},{2,4},{4,2},{6,0},{8,14},{10,12},{12,10},{14,8},{16,22},{18,... | collective-permute-start | bytes 786440 | tf_op jit(solution)/shard_map/ppermute | solution.py:525
  59.0 3.7 %collective-permute-done.8.refs_2_ = bf16[64,2560]{1,0:T(8,128)(2,1)S(1)} collective-permute-done((bf16[64,2560]{1,0:T(8,128)(2,1)S(1)}, bf16[64,2560]{1,0:T(8,128)(2,1)S(1)}, u32[]{:S(2)}, u32[]{:S(2)}) %collective-permute-start.8) | collective-permute-done | bytes 327712 | tf_op jit(solution)/shard_map/ppermute | solution.py:525
  62.7 3.8 %collective-permute-done.9.refs_3_ = bf16[64,1536]{1,0:T(8,128)(2,1)S(1)} collective-permute-done((bf16[64,1536]{1,0:T(8,128)(2,1)S(1)}, bf16[64,1536]{1,0:T(8,128)(2,1)S(1)}, u32[]{:S(2)}, u32[]{:S(2)}) %collective-permute-start.9) | collective-permute-done | bytes 196640 | tf_op jit(solution)/shard_map/ppermute | solution.py:525
  66.5 0.4 lift_far.1
  67.0 1.1 %collective-permute-start.11 = (bf16[32,4096]{1,0:T(8,128)(2,1)S(1)}, bf16[32,4096]{1,0:T(8,128)(2,1)S(1)}, u32[]{:S(2)}, u32[]{:S(2)}) collective-permute-start(bf16[32,4096]{1,0:T(8,128)(2,1)S(1)} %get-tuple-element.38), channel_id=1, source_target_pairs={{0,2},{2,0},{4,6},{6,4},{8,10},{10,8},{12,14},{14,12},{16,18},{18,... | collective-permute-start | bytes 786440 | tf_op jit(solution)/shard_map/ppermute | solution.py:525
  68.1 0.0 collective-permute-start.13
  68.1 0.0 collective-permute-done.10.refs_2_
  68.1 2.4 %collective-permute-start.15 = (bf16[32,4096]{1,0:T(8,128)(2,1)S(1)}, bf16[32,4096]{1,0:T(8,128)(2,1)S(1)}, u32[]{:S(2)}, u32[]{:S(2)}) collective-permute-start(bf16[32,4096]{1,0:T(8,128)(2,1)S(1)} %get-tuple-element.42), channel_id=1, source_target_pairs={{0,6},{2,4},{4,2},{6,0},{8,14},{10,12},{12,10},{14,8},{16,22},{18,... | collective-permute-start | bytes 786440 | tf_op jit(solution)/shard_map/ppermute | solution.py:525
  70.5 0.0 collective-permute-done.12.refs_4_
  70.5 0.0 collective-permute-done.14.refs_6_
  70.5 7.0 %collective-permute-done.11.refs_3_ = bf16[32,4096]{1,0:T(8,128)(2,1)S(1)} collective-permute-done((bf16[32,4096]{1,0:T(8,128)(2,1)S(1)}, bf16[32,4096]{1,0:T(8,128)(2,1)S(1)}, u32[]{:S(2)}, u32[]{:S(2)}) %collective-permute-start.11) | collective-permute-done | bytes 262176 | tf_op jit(solution)/shard_map/ppermute | solution.py:525
  77.5 0.0 collective-permute-done.13.refs_5_
  77.5 4.3 %collective-permute-done.15.refs_7_ = bf16[32,4096]{1,0:T(8,128)(2,1)S(1)} collective-permute-done((bf16[32,4096]{1,0:T(8,128)(2,1)S(1)}, bf16[32,4096]{1,0:T(8,128)(2,1)S(1)}, u32[]{:S(2)}, u32[]{:S(2)}) %collective-permute-start.15) | collective-permute-done | bytes 262176 | tf_op jit(solution)/shard_map/ppermute | solution.py:525
  81.7 1.5 %gather_rows.1 = bf16[128,4096]{1,0:T(8,128)(2,1)} custom-call(s32[1,128]{1,0:T(1,128)S(1)} %get-tuple-element.27.refs_1_.slot_ref, bf16[32,4096]{1,0:T(8,128)(2,1)S(1)} %get-tuple-element.33.refs_0_, bf16[32,4096]{1,0:T(8,128)(2,1)S(1)} %get-tuple-element.36.refs_1_, bf16[32,4096]{1,0:T(8,128)(2,1)S(1)} %collective-permute-done.10.refs_2_, ...), custom_call_target="tpu_custom_call" | custom-call | flops 1024 | bytes 1024 | tf_op jit(solution)/shard_map/gather_rows/pallas_call | solution.py:505
  (10 shorter events, 0.1 us)
Async XLA Ops:
  0.0 10.6 %copy-start.2 = (bf16[96,16,512]{2,1,0:T(8,128)(2,1)S(1)}, bf16[96,16,512]{2,1,0:T(8,128)(2,1)}, u32[]{:S(2)}) copy-start(bf16[96,16,512]{2,1,0:T(8,128)(2,1)} %pool_ref.1) | copy-start | bytes 4718596
  0.0 10.6 %copy-start.3 = (bf16[128,2048]{1,0:T(8,128)(2,1)S(1)}, bf16[128,2048]{1,0:T(8,128)(2,1)}, u32[]{:S(2)}) copy-start(bf16[128,2048]{1,0:T(8,128)(2,1)} %query_ref.3) | copy-start | bytes 1572868
  0.0 10.6 %copy-start.7 = (s32[128,4]{0,1:T(4,128)S(1)}, s32[128,4]{0,1:T(4,128)}, u32[]{:S(2)}) copy-start(s32[128,4]{0,1:T(4,128)} %param.14) | copy-start | bytes 6148
  0.0 10.6 %copy-start.8 = (s32[128]{0:T(128)S(1)}, s32[128]{0:T(128)}, u32[]{:S(2)}) copy-start(s32[128]{0:T(128)} %param.15) | copy-start | bytes 1540
  3.3 16.2 %all-to-all-start = ((bf16[16,16,512]{2,1,0:T(8,128)(2,1)}), bf16[16,16,512]{2,1,0:T(8,128)(2,1)S(1)}, u32[]{:S(2)}, u32[]{:S(2)}) async-start(bf16[16,16,512]{2,1,0:T(8,128)(2,1)} %get-tuple-element.26), calls=%async_computation | async-start | bytes 524288 | tf_op jit(solution)/shard_map/all_to_all | solution.py:570
  10.6 8.9 %copy-start.4 = (bf16[64,2048]{1,0:T(8,128)(2,1)S(1)}, bf16[64,2048]{1,0:T(8,128)(2,1)}, u32[]{:S(2)}) copy-start(bf16[64,2048]{1,0:T(8,128)(2,1)} %get-tuple-element.32.refs_0_) | copy-start | bytes 786436
  10.7 10.2 %copy-start.6 = (bf16[128,512]{1,0:T(8,128)(2,1)S(1)}, bf16[128,512]{1,0:T(8,128)(2,1)}, u32[]{:S(2)}) copy-start(bf16[128,512]{1,0:T(8,128)(2,1)} %fresh_ref.1) | copy-start | bytes 393220
  10.7 10.2 %copy-start.9 = (s32[128,1]{0,1:T(1,128)S(1)}, s32[128,1]{0,1:T(1,128)}, u32[]{:S(2)}) copy-start(s32[128,1]{0,1:T(1,128)} %param.18) | copy-start | bytes 1540
  10.7 10.2 %copy-start.10 = (s32[128]{0:T(128)S(1)}, s32[128]{0:T(128)}, u32[]{:S(2)}) copy-start(s32[128]{0:T(128)} %param.19) | copy-start | bytes 1540
  16.9 11.6 %copy-start.11 = (bf16[64,2560]{1,0:T(8,128)(2,1)S(1)}, bf16[64,2560]{1,0:T(8,128)(2,1)}, u32[]{:S(2)}) copy-start(bf16[64,2560]{1,0:T(8,128)(2,1)} %get-tuple-element.34) | copy-start | bytes 983044
  19.5 16.3 %copy-start.5 = (bf16[64,1536]{1,0:T(8,128)(2,1)S(1)}, bf16[64,1536]{1,0:T(8,128)(2,1)}, u32[]{:S(2)}) copy-start(bf16[64,1536]{1,0:T(8,128)(2,1)} %get-tuple-element.35.refs_0_) | copy-start | bytes 589828
  19.5 11.5 %collective-permute-start.3 = (bf16[64,2048]{1,0:T(8,128)(2,1)S(1)}, bf16[64,2048]{1,0:T(8,128)(2,1)S(1)}, u32[]{:S(2)}, u32[]{:S(2)}) collective-permute-start(bf16[64,2048]{1,0:T(8,128)(2,1)S(1)} %after.5), channel_id=1, source_target_pairs={{0,12},{2,14},{4,8},{6,10},{8,4},{10,6},{12,0},{14,2},{16,28},{18,... | collective-permute-start | bytes 786440 | tf_op jit(solution)/shard_map/ppermute | solution.py:525
  20.9 30.7 %copy-start.1 = (bf16[2,2048,64]{1,2,0:T(8,128)(2,1)S(1)}, bf16[2,2048,64]{1,2,0:T(8,128)(2,1)}, u32[]{:S(2)}) copy-start(bf16[2,2048,64]{1,2,0:T(8,128)(2,1)} %param.20) | copy-start | bytes 1572868
  24.9 11.0 %collective-permute-start.2 = (bf16[64,2176]{1,0:T(8,128)(2,1)S(1)}, bf16[64,2176]{1,0:T(8,128)(2,1)S(1)}, u32[]{:S(2)}, u32[]{:S(2)}) collective-permute-start(bf16[64,2176]{1,0:T(8,128)(2,1)S(1)} %get-tuple-element.31), channel_id=1, source_target_pairs={{0,6},{2,4},{4,2},{6,0},{8,14},{10,12},{12,10},{14,8},{16,22},{18,... | collective-permute-start | bytes 835592 | tf_op jit(solution)/shard_map/ppermute | solution.py:525
  25.5 13.2 %collective-permute-start = (bf16[64,2176]{1,0:T(8,128)(2,1)S(1)}, bf16[64,2176]{1,0:T(8,128)(2,1)S(1)}, u32[]{:S(2)}, u32[]{:S(2)}) collective-permute-start(bf16[64,2176]{1,0:T(8,128)(2,1)S(1)} %get-tuple-element.29), channel_id=1, source_target_pairs={{0,2},{2,0},{4,6},{6,4},{8,10},{10,8},{12,14},{14,12},{16,18},{18,... | collective-permute-start | bytes 835592 | tf_op jit(solution)/shard_map/ppermute | solution.py:525
  26.8 24.8 %collective-permute-start.1 = (bf16[64,2176]{1,0:T(8,128)(2,1)S(1)}, bf16[64,2176]{1,0:T(8,128)(2,1)S(1)}, u32[]{:S(2)}, u32[]{:S(2)}) collective-permute-start(bf16[64,2176]{1,0:T(8,128)(2,1)S(1)} %get-tuple-element.30), channel_id=1, source_target_pairs={{0,4},{2,6},{4,0},{6,2},{8,12},{10,14},{12,8},{14,10},{16,20},{18,... | collective-permute-start | bytes 835592 | tf_op jit(solution)/shard_map/ppermute | solution.py:525
  28.4 23.7 %collective-permute-start.6 = (bf16[64,2560]{1,0:T(8,128)(2,1)S(1)}, bf16[64,2560]{1,0:T(8,128)(2,1)S(1)}, u32[]{:S(2)}, u32[]{:S(2)}) collective-permute-start(bf16[64,2560]{1,0:T(8,128)(2,1)S(1)} %copy-done.11), channel_id=1, source_target_pairs={{0,12},{2,14},{4,8},{6,10},{8,4},{10,6},{12,0},{14,2},{16,28},{18,... | collective-permute-start | bytes 983048 | tf_op jit(solution)/shard_map/ppermute | solution.py:525
  31.0 20.5 %collective-permute-start.4 = (bf16[64,2048]{1,0:T(8,128)(2,1)S(1)}, bf16[64,2048]{1,0:T(8,128)(2,1)S(1)}, u32[]{:S(2)}, u32[]{:S(2)}) collective-permute-start(bf16[64,2048]{1,0:T(8,128)(2,1)S(1)} %after.6), channel_id=1, source_target_pairs={{0,16},{2,18},{4,20},{6,22},{8,24},{10,26},{12,28},{14,30},{16,0},... | collective-permute-start | bytes 786440 | tf_op jit(solution)/shard_map/ppermute | solution.py:525
  35.9 19.4 %collective-permute-start.7 = (bf16[64,1536]{1,0:T(8,128)(2,1)S(1)}, bf16[64,1536]{1,0:T(8,128)(2,1)S(1)}, u32[]{:S(2)}, u32[]{:S(2)}) collective-permute-start(bf16[64,1536]{1,0:T(8,128)(2,1)S(1)} %after.7), channel_id=1, source_target_pairs={{0,12},{2,14},{4,8},{6,10},{8,4},{10,6},{12,0},{14,2},{16,28},{18,... | collective-permute-start | bytes 589832 | tf_op jit(solution)/shard_map/ppermute | solution.py:525
  51.5 2.2 %copy-start = (bf16[2,64,4096]{2,1,0:T(8,128)(2,1)S(1)}, bf16[2,64,4096]{2,1,0:T(8,128)(2,1)}, u32[]{:S(2)}) copy-start(bf16[2,64,4096]{2,1,0:T(8,128)(2,1)} %refs_1_.1) | copy-start | bytes 3145732
  52.0 1.7 %collective-permute-start.5 = (f32[256,128]{1,0:T(8,128)S(1)}, f32[256,128]{1,0:T(8,128)S(1)}, u32[]{:S(2)}, u32[]{:S(2)}) collective-permute-start(f32[256,128]{1,0:T(8,128)S(1)} %low_products.1.mine_ref), channel_id=1, source_target_pairs={{0,1},{1,0},{2,3},{3,2},{4,5},{5,4},{6,7},{7,6},{8,9},{9,8},{10,11... | collective-permute-start | bytes 393224 | tf_op jit(solution)/shard_map/ppermute | solution.py:599
  52.1 10.6 %collective-permute-start.8 = (bf16[64,2560]{1,0:T(8,128)(2,1)S(1)}, bf16[64,2560]{1,0:T(8,128)(2,1)S(1)}, u32[]{:S(2)}, u32[]{:S(2)}) collective-permute-start(bf16[64,2560]{1,0:T(8,128)(2,1)S(1)} %after.8), channel_id=1, source_target_pairs={{0,16},{2,18},{4,20},{6,22},{8,24},{10,26},{12,28},{14,30},{16,0},... | collective-permute-start | bytes 983048 | tf_op jit(solution)/shard_map/ppermute | solution.py:525
  54.1 13.9 %collective-permute-start.10 = (bf16[32,4096]{1,0:T(8,128)(2,1)S(1)}, bf16[32,4096]{1,0:T(8,128)(2,1)S(1)}, u32[]{:S(2)}, u32[]{:S(2)}) collective-permute-start(bf16[32,4096]{1,0:T(8,128)(2,1)S(1)} %get-tuple-element.37), channel_id=1, source_target_pairs={{0,2},{2,0},{4,6},{6,4},{8,10},{10,8},{12,14},{14,12},{16,18},{18,... | collective-permute-start | bytes 786440 | tf_op jit(solution)/shard_map/ppermute | solution.py:525
  55.3 11.3 %collective-permute-start.9 = (bf16[64,1536]{1,0:T(8,128)(2,1)S(1)}, bf16[64,1536]{1,0:T(8,128)(2,1)S(1)}, u32[]{:S(2)}, u32[]{:S(2)}) collective-permute-start(bf16[64,1536]{1,0:T(8,128)(2,1)S(1)} %after.9), channel_id=1, source_target_pairs={{0,16},{2,18},{4,20},{6,22},{8,24},{10,26},{12,28},{14,30},{16,0},... | collective-permute-start | bytes 589832 | tf_op jit(solution)/shard_map/ppermute | solution.py:525
  56.5 14.0 %collective-permute-start.12 = (bf16[32,4096]{1,0:T(8,128)(2,1)S(1)}, bf16[32,4096]{1,0:T(8,128)(2,1)S(1)}, u32[]{:S(2)}, u32[]{:S(2)}) collective-permute-start(bf16[32,4096]{1,0:T(8,128)(2,1)S(1)} %get-tuple-element.39), channel_id=1, source_target_pairs={{0,4},{2,6},{4,0},{6,2},{8,12},{10,14},{12,8},{14,10},{16,20},{18,... | collective-permute-start | bytes 786440 | tf_op jit(solution)/shard_map/ppermute | solution.py:525
  56.6 14.0 %collective-permute-start.14 = (bf16[32,4096]{1,0:T(8,128)(2,1)S(1)}, bf16[32,4096]{1,0:T(8,128)(2,1)S(1)}, u32[]{:S(2)}, u32[]{:S(2)}) collective-permute-start(bf16[32,4096]{1,0:T(8,128)(2,1)S(1)} %get-tuple-element.41), channel_id=1, source_target_pairs={{0,6},{2,4},{4,2},{6,0},{8,14},{10,12},{12,10},{14,8},{16,22},{18,... | collective-permute-start | bytes 786440 | tf_op jit(solution)/shard_map/ppermute | solution.py:525
  67.0 10.5 %collective-permute-start.11 = (bf16[32,4096]{1,0:T(8,128)(2,1)S(1)}, bf16[32,4096]{1,0:T(8,128)(2,1)S(1)}, u32[]{:S(2)}, u32[]{:S(2)}) collective-permute-start(bf16[32,4096]{1,0:T(8,128)(2,1)S(1)} %get-tuple-element.38), channel_id=1, source_target_pairs={{0,2},{2,0},{4,6},{6,4},{8,10},{10,8},{12,14},{14,12},{16,18},{18,... | collective-permute-start | bytes 786440 | tf_op jit(solution)/shard_map/ppermute | solution.py:525
  68.1 9.4 %collective-permute-start.13 = (bf16[32,4096]{1,0:T(8,128)(2,1)S(1)}, bf16[32,4096]{1,0:T(8,128)(2,1)S(1)}, u32[]{:S(2)}, u32[]{:S(2)}) collective-permute-start(bf16[32,4096]{1,0:T(8,128)(2,1)S(1)} %get-tuple-element.40), channel_id=1, source_target_pairs={{0,4},{2,6},{4,0},{6,2},{8,12},{10,14},{12,8},{14,10},{16,20},{18,... | collective-permute-start | bytes 786440 | tf_op jit(solution)/shard_map/ppermute | solution.py:525
  68.1 13.7 %collective-permute-start.15 = (bf16[32,4096]{1,0:T(8,128)(2,1)S(1)}, bf16[32,4096]{1,0:T(8,128)(2,1)S(1)}, u32[]{:S(2)}, u32[]{:S(2)}) collective-permute-start(bf16[32,4096]{1,0:T(8,128)(2,1)S(1)} %get-tuple-element.42), channel_id=1, source_target_pairs={{0,6},{2,4},{4,2},{6,0},{8,14},{10,12},{12,10},{14,8},{16,22},{18,... | collective-permute-start | bytes 786440 | tf_op jit(solution)/shard_map/ppermute | solution.py:525
